TPU v7x, 32 devices: a whole 2x2x4 slice. The times are simulated.
32 devices in a mesh: grp: 4 (over x, core), dev: 8 (over z, y).
Axes of the slice: x: 2, y: 2, z: 4, core: 2. Of those that a mesh axis runs over, the one named last changes fastest.
Arguments:
- density: float32 [2, 8192, 8192], P(None, 'dev', 'grp'), may hold values from -64 to 64, as said below
- costate: float32 [2, 8192, 8192], P(None, 'dev', 'grp'), may hold values from -64 to 64, as said below
- phases: float32 [24, 2, 64], replicated, may hold values from -3.140625 to 3.140625
- displacements: float32 [24, 2, 2, 64, 64], replicated, may hold values from -0.5 to 0.5
- table_slot: int32 [24], replicated, may hold values from 0 to 23, each once
- checkpoint: int32 [1], replicated, may hold values from 0 to 22
Outputs:
- costate_start: float32 [2, 8192, 8192], P(None, 'dev', 'grp')
- phase_grads: float32 [2, 2, 64], replicated
Inputs may be any that keep to these rules, and one draw needn't show every extreme that they name: `density`: Hermitian: real part symmetric, imaginary part antisymmetric. `costate`: Hermitian: real part symmetric, imaginary part antisymmetric. `table_slot`: every row of phases once.
All inputs are finite; a program needn't handle non-finite values.
Results may differ from a plain program's by a relative error of at most 0.00011.
Values sent between devices are 32-bit elements; how exact they have to be, the bound alone decides.
No kernel may reach another device: no remote copies, remote signals or barrier semaphores. Data moves between devices by JAX's collectives and lax.ppermute only.
A program may use at most 384 MiB of HBM per device.

v0:
```python
import functools

import jax
import jax.numpy as jnp
from jax import lax
from jax.experimental import pallas as pl
from jax.experimental.pallas import tpu as pltpu
from jax.sharding import PartitionSpec as P

LEVELS = 64
TRANSMON = 2
WIDE = LEVELS * TRANSMON
PAIR = 2 * WIDE
HIGH = lax.Precision.HIGHEST
F32 = jnp.float32
BF16 = jnp.bfloat16
SMALL = pl.CostEstimate(flops=1024, bytes_accessed=1024, transcendentals=0)
LARGE = pl.CostEstimate(flops=2 * 10**11, bytes_accessed=1024, transcendentals=0)
PARAMS = pltpu.CompilerParams(vmem_limit_bytes=60 * 1024 * 1024)


def split_value(value):
    high = value.astype(BF16)
    low = (value - high.astype(F32)).astype(BF16)
    return high, low


def mxu(left, right, dims=(((1,), (0,)), ((), ()))):
    return lax.dot_general(left, right, dims, preferred_element_type=F32)


def exact(left, right, dims=(((1,), (0,)), ((), ()))):
    return lax.dot_general(left, right, dims, precision=HIGH, preferred_element_type=F32)


def grid_of(shape, dim):
    return lax.broadcasted_iota(jnp.int32, shape, dim)


def pick_matrix(count, chosen):
    shape = (count, count)
    return (chosen(grid_of(shape, 0)) == grid_of(shape, 1)).astype(F32)


def spread(matrix):
    tall = (grid_of((WIDE, LEVELS), 0) // TRANSMON == grid_of((WIDE, LEVELS), 1)).astype(F32)
    long = (grid_of((LEVELS, WIDE), 1) // TRANSMON == grid_of((LEVELS, WIDE), 0)).astype(F32)
    same = grid_of((WIDE, WIDE), 0) % TRANSMON == grid_of((WIDE, WIDE), 1) % TRANSMON
    return jnp.where(same, exact(exact(tall, matrix), long), 0.0)


def blocks(upper_left, upper_right, lower_left, lower_right):
    return jnp.concatenate(
        [
            jnp.concatenate([upper_left, upper_right], axis=1),
            jnp.concatenate([lower_left, lower_right], axis=1),
        ],
        axis=0,
    )


def complex_product(left, right):
    return (
        exact(left[0], right[0]) - exact(left[1], right[1]),
        exact(left[0], right[1]) + exact(left[1], right[0]),
    )


def weights_kernel(parts, chunks, slot_ref, start_ref, seat_ref, *refs):
    angle_refs, matrix_refs = refs[0:2], refs[2:4]
    first_ref, open_ref, turn_ref, level_ref, lane_ref = refs[-5:]
    seat = seat_ref[0]
    width = LEVELS // parts
    share = WIDE // parts
    size = share // chunks
    first, second = [], []
    for layer in range(2):
        cosine = jnp.cos(angle_refs[layer][...])
        sine = jnp.sin(angle_refs[layer][...])
        for mode, kept in enumerate((first, second)):
            turn_real, turn_imag = cosine[mode:mode + 1], sine[mode:mode + 1]
            real_part = matrix_refs[layer][mode, 0]
            imag_part = matrix_refs[layer][mode, 1]
            kept.append(
                (
                    real_part * turn_real - imag_part * turn_imag,
                    real_part * turn_imag + imag_part * turn_real,
                )
            )
    both_first = complex_product(first[1], first[0])
    both_second = complex_product(second[1], second[0])

    order = pick_matrix(
        LEVELS, lambda row: lax.bitwise_xor(row // width, seat) * width + row % width
    )

    def put_level(ref, index, real_part, imag_part):
        full = blocks(real_part, -imag_part, imag_part, real_part)
        high, low = split_value(full)
        made = blocks(high, high, low, jnp.zeros_like(low))
        if index is None:
            ref[...] = made
        else:
            ref[index] = made

    put_level(turn_ref, None, exact(both_first[0].T, order), exact(-both_first[1].T, order))
    put_level(level_ref, 0, first[1][0].T, first[1][1].T)
    put_level(level_ref, 1, exact(first[0][0], order), exact(-first[0][1], order))
    put_level(level_ref, 2, exact(order, first[0][0].T), exact(order, first[0][1].T))

    def put_lane(index, real_part, imag_part):
        real_part, imag_part = spread(real_part), spread(imag_part)
        high, low = split_value(blocks(real_part, imag_part, -imag_part, real_part))
        lane_ref[index, 0] = high
        lane_ref[index, 1] = low

    put_lane(0, *second[1])
    put_lane(1, second[0][0].T, -second[0][1].T)
    put_lane(2, *second[0])

    real_part, imag_part = spread(both_second[0].T), spread(both_second[1].T)
    full = blocks(real_part, -imag_part, -imag_part, -real_part)

    def source(row):
        chunk, rest = row // (2 * size * parts), row % (2 * size * parts)
        step, rest = rest // (2 * size), rest % (2 * size)
        half, place = rest // size, rest % size
        return half * WIDE + lax.bitwise_xor(step, seat) * share + chunk * size + place

    chosen = exact(pick_matrix(PAIR, source), full)
    high, low = split_value(chosen)
    open_ref[0] = high
    open_ref[1] = low
    high, low = split_value(chosen[:PAIR // chunks].T)
    first_ref[...] = blocks(high, low, high, jnp.zeros_like(low))


def make_weights(phases, displacements, table_slot, checkpoint, seat, parts, chunks):
    def angles(layer):
        return pl.BlockSpec(
            (None, 2, LEVELS), lambda i, slot, start, own: (slot[start[0] + layer], 0, 0)
        )

    def matrices(layer):
        return pl.BlockSpec(
            (None, 2, 2, LEVELS, LEVELS),
            lambda i, slot, start, own: (start[0] + layer, 0, 0, 0, 0),
        )

    def whole(shape):
        return pl.BlockSpec(shape, lambda i, slot, start, own: (0,) * len(shape))

    shapes = [(2 * PAIR, 2 * PAIR // chunks), (2, PAIR, PAIR), (PAIR, PAIR), (3, PAIR, PAIR), (3, 2, PAIR, PAIR)]
    return pl.pallas_call(
        functools.partial(weights_kernel, parts, chunks),
        grid_spec=pltpu.PrefetchScalarGridSpec(
            num_scalar_prefetch=3,
            grid=(1,),
            in_specs=[angles(0), angles(1), matrices(0), matrices(1)],
            out_specs=[whole(shape) for shape in shapes],
        ),
        out_shape=[jax.ShapeDtypeStruct(shape, BF16) for shape in shapes],
        compiler_params=PARAMS,
        cost_estimate=SMALL,
    )(table_slot, checkpoint, seat, phases, phases, displacements, displacements)


def open_kernel(count, waited, weight_ref, field_ref, *refs):
    both = jnp.concatenate([field_ref[0], field_ref[1]], axis=1)
    high, low = split_value(both)
    across = (((1,), (1,)), ((), ()))
    made = mxu(weight_ref[0], high, across) + (
        mxu(weight_ref[0], low, across) + mxu(weight_ref[1], high, across)
    )
    tall = made.shape[0] // count
    for place, out in enumerate(refs[waited:]):
        piece = made[place * tall:(place + 1) * tall]
        for first in range(out.shape[0]):
            out[first] = piece[:, first * WIDE:(first + 1) * WIDE]


def open_first_kernel(size, weight_ref, field_ref, *out_refs):
    levels = field_ref.shape[2] // WIDE
    rows = []
    for level in range(levels):
        place = slice(level * WIDE, (level + 1) * WIDE)
        real_high, real_low = split_value(field_ref[0, :, place])
        imag_high, imag_low = split_value(field_ref[1, :, place])
        rows.append(jnp.concatenate([real_high, imag_high, real_low, imag_low], axis=1))
    made = mxu(jnp.concatenate(rows, axis=0), weight_ref[...])
    middle = made.shape[1] // 2
    tall = 2 * size
    for level in range(levels):
        turned = made[level * WIDE:(level + 1) * WIDE].T
        turned = turned[:middle] + turned[middle:]
        for step, out in enumerate(out_refs):
            out[level * tall:(level + 1) * tall, :] = turned[step * tall:(step + 1) * tall]


def open_first(field, weights, parts, size):
    rows, cols = field.shape[1:]
    firsts = rows // WIDE
    tall = cols // WIDE * 2 * size
    outs = pl.pallas_call(
        functools.partial(open_first_kernel, size),
        grid=(firsts,),
        in_specs=[
            pl.BlockSpec(weights.shape, lambda i: (0, 0)),
            pl.BlockSpec((2, WIDE, cols), lambda i: (0, i, 0)),
        ],
        out_specs=[pl.BlockSpec((None, tall, WIDE), lambda i: (i, 0, 0))] * parts,
        out_shape=[jax.ShapeDtypeStruct((firsts, tall, WIDE), F32)] * parts,
        compiler_params=PARAMS,
        cost_estimate=SMALL,
    )(weights, field)
    return [outs]


def open_state(field, weights, parts, size, chunk_start, chunk_count, waited):
    rows, cols = field.shape[1:]
    firsts = rows // WIDE
    column_levels = cols // WIDE
    count = parts * chunk_count
    tall = count * 2 * size
    shape = jax.ShapeDtypeStruct((firsts, column_levels * 2 * size, WIDE), F32)
    weights = lax.slice_in_dim(
        weights, chunk_start * parts * 2 * size, chunk_start * parts * 2 * size + tall, axis=1
    )
    outs = pl.pallas_call(
        functools.partial(open_kernel, count, len(waited)),
        grid=(column_levels,),
        in_specs=[
            pl.BlockSpec((2, tall, PAIR), lambda i: (0, 0, 0)),
            pl.BlockSpec((2, rows, WIDE), lambda i: (0, 0, i)),
        ]
        + [pl.BlockSpec(memory_space=pl.ANY)] * len(waited),
        out_specs=[pl.BlockSpec((firsts, 2 * size, WIDE), lambda i: (0, i, 0))] * count,
        out_shape=[shape] * count,
        compiler_params=PARAMS,
        cost_estimate=SMALL,
    )(weights, field, *waited)
    return [outs[c * parts:(c + 1) * parts] for c in range(chunk_count)]


def cut_kernel(size, waited, seat_ref, field_ref, *refs):
    seat = seat_ref[0]
    levels = field_ref.shape[-1] // WIDE
    for step, out in enumerate(refs[waited:]):
        part = lax.bitwise_xor(seat, step)
        for half in range(2):
            for level in range(levels):
                start = (2 * level + half) * size
                out[start:start + size, :] = field_ref[
                    half, part, :, level * WIDE:(level + 1) * WIDE
                ]


def cut_pieces(field, seat, parts, chunk, size, waited):
    rows, cols = field.shape[1:]
    firsts = rows // WIDE
    chunks = WIDE // parts // size
    tall = cols // WIDE * 2 * size
    return pl.pallas_call(
        functools.partial(cut_kernel, size, len(waited)),
        grid=(firsts,),
        in_specs=[
            pl.BlockSpec(memory_space=pltpu.SMEM),
            pl.BlockSpec((2, None, parts, None, size, cols), lambda i: (0, i, 0, chunk, 0, 0)),
        ]
        + [pl.BlockSpec(memory_space=pl.ANY)] * len(waited),
        out_specs=[pl.BlockSpec((None, tall, WIDE), lambda i: (i, 0, 0))] * parts,
        out_shape=[jax.ShapeDtypeStruct((firsts, tall, WIDE), F32)] * parts,
        compiler_params=PARAMS,
        cost_estimate=SMALL,
    )(seat, field.reshape(2, firsts, parts, chunks, size, cols), *waited)


def level_apply(weights, real_part, imag_part):
    real_high, real_low = split_value(real_part)
    imag_high, imag_low = split_value(imag_part)
    stacked = jnp.concatenate([real_high, imag_high, real_low, imag_low], axis=0)
    made = mxu(weights, stacked)
    return made[:WIDE] + made[WIDE:]


def lane_apply(weight_ref, index, real_part, imag_part):
    high, low = split_value(jnp.concatenate([real_part, imag_part], axis=1))
    made = mxu(high, weight_ref[index, 0]) + (
        mxu(low, weight_ref[index, 0]) + mxu(high, weight_ref[index, 1])
    )
    return made[:, :WIDE], made[:, WIDE:]


def gather_levels(refs, size, half):
    columns = []
    for place in range(size):
        parts = [
            ref[pl.ds(half * size + place, ref.shape[0] // (2 * size), stride=2 * size), :]
            for ref in refs
        ]
        columns.append(jnp.concatenate(parts, axis=0) if len(parts) > 1 else parts[0])
    return jnp.concatenate(columns, axis=1)


def scatter_levels(ref, size, half, value):
    for place in range(size):
        ref[pl.ds(half * size + place, LEVELS, stride=2 * size), :] = value[
            :, place * WIDE:(place + 1) * WIDE
        ]


def turn_kernel(parts, size, weight_ref, *refs):
    pieces = refs[:parts]
    out_ref = refs[-1].reshape(LEVELS * 2 * size, WIDE)
    made = level_apply(
        weight_ref[...], gather_levels(pieces, size, 0), gather_levels(pieces, size, 1)
    )
    scatter_levels(out_ref, size, 0, made[:LEVELS])
    scatter_levels(out_ref, size, 1, made[LEVELS:])


def turn_columns(pieces, weights, size, waited):
    firsts = pieces[0].shape[0]
    parts = len(pieces)
    block = pieces[0].shape[1:]
    return pl.pallas_call(
        functools.partial(turn_kernel, parts, size),
        grid=(firsts,),
        in_specs=[pl.BlockSpec((PAIR, PAIR), lambda i: (0, 0))]
        + [pl.BlockSpec((None,) + block, lambda i: (i, 0, 0))] * parts
        + [pl.BlockSpec(memory_space=pl.ANY)] * len(waited),
        out_specs=pl.BlockSpec((LEVELS, None, 2 * size, WIDE), lambda i: (0, i, 0, 0)),
        out_shape=jax.ShapeDtypeStruct((LEVELS, firsts, 2 * size, WIDE), F32),
        compiler_params=PARAMS,
        cost_estimate=SMALL,
    )(weights, *pieces, *waited)


def halves(value, size):
    value = value.reshape(LEVELS, 2, size, WIDE)
    rows = LEVELS * size
    return value[:, 0].reshape(rows, WIDE), value[:, 1].reshape(rows, WIDE)


def join(real_part, imag_part, size):
    shape = (LEVELS, 1, size, WIDE)
    both = jnp.concatenate([real_part.reshape(shape), imag_part.reshape(shape)], axis=1)
    return both.reshape(LEVELS * 2 * size, WIDE)


def close_kernel(parts, size, lane_ref, level_ref, field_ref, *refs):
    rho_refs = refs[:parts]
    out_refs = refs[-parts - 3:-3]
    grad_ref, work_a, work_b = refs[-3:]
    step = pl.program_id(0)

    @pl.when(step == 0)
    def _():
        grad_ref[...] = jnp.zeros_like(grad_ref)

    flat = field_ref.reshape(LEVELS * 2 * size, WIDE)
    real_part, imag_part = lane_apply(lane_ref, 0, *halves(flat[...], size))
    work_a[...] = join(real_part, imag_part, size)

    rho = jnp.concatenate([ref[...] for ref in rho_refs], axis=0)
    rho_real, rho_imag = halves(rho, size)
    real_part, imag_part = lane_apply(lane_ref, 1, rho_real, rho_imag)
    work_b[...] = join(real_part, imag_part, size)

    mid = level_apply(level_ref[0], gather_levels([work_a], size, 0), gather_levels([work_a], size, 1))
    seen = level_apply(level_ref[1], gather_levels([work_b], size, 0), gather_levels([work_b], size, 1))
    terms = seen[:LEVELS] * mid[LEVELS:] - seen[LEVELS:] * mid[:LEVELS]
    total = terms[:, :WIDE]
    for place in range(1, size):
        total = total + terms[:, place * WIDE:(place + 1) * WIDE]
    grad_ref[1] += total

    last = level_apply(level_ref[2], mid[:LEVELS], mid[LEVELS:])
    scatter_levels(work_a, size, 0, last[:LEVELS])
    scatter_levels(work_a, size, 1, last[LEVELS:])
    real_part, imag_part = lane_apply(lane_ref, 2, *halves(work_a[...], size))
    terms = rho_real * imag_part - rho_imag * real_part
    grad_ref[0] += jnp.sum(terms.reshape(LEVELS, size, WIDE), axis=1)
    made = join(real_part, imag_part, size)
    rows = made.shape[0] // parts
    for part in range(parts):
        out_refs[part][...] = made[part * rows:(part + 1) * rows]


def close_columns(field, rho_pieces, lane, level, size, waited):
    total_first, firsts = field.shape[:2]
    devs = total_first // firsts
    parts = len(rho_pieces)
    rows = LEVELS * 2 * size
    field = field.reshape(devs, firsts, firsts * 2 * size, WIDE)
    piece = rho_pieces[0]
    piece_spec = pl.BlockSpec((None,) + piece.shape[1:], lambda i: (i, 0, 0))
    outs = pl.pallas_call(
        functools.partial(close_kernel, parts, size),
        grid=(firsts,),
        in_specs=[
            pl.BlockSpec(lane.shape, lambda i: (0, 0, 0, 0)),
            pl.BlockSpec(level.shape, lambda i: (0, 0, 0)),
            pl.BlockSpec((devs, None, firsts * 2 * size, WIDE), lambda i: (0, i, 0, 0)),
        ]
        + [piece_spec] * parts
        + [pl.BlockSpec(memory_space=pl.ANY)] * len(waited),
        out_specs=[piece_spec] * parts + [pl.BlockSpec((2, LEVELS, WIDE), lambda i: (0, 0, 0))],
        out_shape=[jax.ShapeDtypeStruct(piece.shape, F32)] * parts
        + [jax.ShapeDtypeStruct((2, LEVELS, WIDE), F32)],
        scratch_shapes=[pltpu.VMEM((rows, WIDE), F32), pltpu.VMEM((rows, WIDE), F32)],
        compiler_params=PARAMS,
        cost_estimate=LARGE,
    )(lane, level, field, *rho_pieces, *waited)
    return list(outs[:parts]), outs[parts]


def place_kernel(parts, size, aliased, seat_ref, *refs):
    pieces = refs[:parts]
    out_ref = refs[parts + aliased]
    seat = seat_ref[0]
    levels = pieces[0].shape[0] // (2 * size)
    for step in range(parts):
        part = lax.bitwise_xor(seat, step)
        for half in range(2):
            for level in range(levels):
                start = level * 2 * size + half * size
                out_ref[half, part, :, level * WIDE:(level + 1) * WIDE] = pieces[step][
                    start:start + size, :
                ]


def place_pieces(pieces, seat, held, chunk, shape, size):
    parts = len(pieces)
    firsts, chunks = shape[1], shape[3]
    aliased = 0 if held is None else 1
    piece = pieces[0]
    cols = shape[-1]
    return pl.pallas_call(
        functools.partial(place_kernel, parts, size, aliased),
        grid=(firsts,),
        in_specs=[pl.BlockSpec(memory_space=pltpu.SMEM)]
        + [pl.BlockSpec((None,) + piece.shape[1:], lambda i: (i, 0, 0))] * parts
        + [pl.BlockSpec(memory_space=pl.ANY)] * aliased,
        out_specs=pl.BlockSpec(
            (2, None, parts, None, size, cols), lambda i: (0, i, 0, chunk, 0, 0)
        ),
        out_shape=jax.ShapeDtypeStruct(shape, F32),
        input_output_aliases={parts + 1: 0} if aliased else {},
        compiler_params=PARAMS,
        cost_estimate=SMALL,
    )(seat, *pieces, *([held] if aliased else []))


def swap(pieces, parts):
    moved = [pieces[0]]
    for step in range(1, parts):
        pairs = [(member, member ^ step) for member in range(parts)]
        moved.append(lax.ppermute(pieces[step], "grp", pairs))
    return moved


def grad_kernel(parts, count, seat_ref, *refs):
    out_ref = refs[-1]
    grad = refs[0][...]
    for ref in refs[1:count]:
        grad = grad + ref[...]
    grad = -2.0 * grad
    width = LEVELS // parts
    order = pick_matrix(
        LEVELS, lambda row: lax.bitwise_xor(row // width, seat_ref[0]) * width + row % width
    )
    fold = (grid_of((WIDE, LEVELS), 0) // TRANSMON == grid_of((WIDE, LEVELS), 1)).astype(F32)
    for layer in range(2):
        firsts = exact(jnp.ones((8, WIDE), F32), grad[layer], (((1,), (1,)), ((), ())))
        if layer == 0:
            firsts = exact(firsts, order)
        seconds = exact(exact(jnp.ones((8, LEVELS), F32), grad[layer]), fold)
        out_ref[2 * layer:2 * layer + 1, :] = firsts[:1]
        out_ref[2 * layer + 1:2 * layer + 2, :] = seconds[:1]


def device_grad(grads, seat, parts, waited):
    return pl.pallas_call(
        functools.partial(grad_kernel, parts, len(grads)),
        in_specs=[pl.BlockSpec(memory_space=pltpu.SMEM)]
        + [pl.BlockSpec(memory_space=pltpu.VMEM)] * len(grads)
        + [pl.BlockSpec(memory_space=pl.ANY)] * len(waited),
        out_specs=pl.BlockSpec(memory_space=pltpu.VMEM),
        out_shape=jax.ShapeDtypeStruct((4, LEVELS), F32),
        compiler_params=PARAMS,
        cost_estimate=SMALL,
    )(seat, *grads, *waited)


def grand_total(value):
    rounds = []
    for axis in ("grp", "dev"):
        count = lax.axis_size(axis)
        rounds.append([(axis, 1 << bit, count) for bit in range(count.bit_length() - 1)])
    for axis, step, count in rounds[0][:1] + rounds[1] + rounds[0][1:]:
        pairs = [(member, member ^ step) for member in range(count)]
        value = value + lax.ppermute(value, axis, pairs)
    return value


def per_device(density, costate, phases, displacements, table_slot, checkpoint):
    parts = lax.axis_size("grp")
    share = WIDE // parts
    chunks = max(1, min(4, share // 8))
    size = share // chunks
    seat = lax.axis_index("grp").astype(jnp.int32)
    seats = seat.reshape(1)
    rows, cols = costate.shape[1:]

    opened_first, opened, turned_by, level, lane = make_weights(
        phases, displacements, table_slot, checkpoint, seats, parts, chunks
    )
    state_cut = open_first(costate, opened_first, parts, size)
    if chunks > 1:
        state_cut += open_state(
            costate, opened, parts, size, 1, chunks - 1, list(state_cut[0][:1])
        )
    rho = [
        cut_pieces(density, seats, parts, chunk, size, list(state_cut[-1][:1]))
        for chunk in range(chunks)
    ]
    state = [swap(pieces, parts) for pieces in state_cut[:3]]
    rho_there = [swap(pieces, parts) for pieces in rho]

    shape = (2, rows // WIDE, parts, chunks, size, cols)
    fields, closed, made, grads = [], [], [], []

    def close(chunk, waited):
        if chunk > 0:
            waited = waited + closed[chunk - 1][:1]
        out, grad = close_columns(
            fields[chunk], rho_there[chunk], lane, level, size, waited
        )
        closed.append(out)
        if chunk == chunks - 2 and chunk > 0:
            out, rho_there[-1] = lax.optimization_barrier((out, rho_there[-1]))
        if chunk == chunks - 1 and chunk > 1:
            out, made[-1] = lax.optimization_barrier((out, made[-1]))
        made.append(swap(out, parts))
        grads.append(grad)

    for chunk in range(chunks):
        waited = [rho[chunk][0]]
        if chunk > 0:
            waited.append(field)
        if chunk > 1:
            close(chunk - 2, [])
            waited += closed[chunk - 2][:1]
        field = turn_columns(state[chunk], turned_by, size, waited)
        if chunk + 1 == len(state) < chunks:
            pieces, field = lax.optimization_barrier((state_cut[chunk + 1], field))
            state.append(swap(pieces, parts))
        fields.append(lax.all_to_all(field, "dev", split_axis=0, concat_axis=0, tiled=True))
    whole = None
    for chunk in range(chunks):
        while len(made) < min(chunk + 2, chunks):
            waited = list(made[-2][1:]) if len(made) > 1 else []
            close(len(made), [whole] if 0 < chunk == chunks - 2 else waited)
        whole = place_pieces(made[chunk], seats, whole, chunk, shape, size)
    grad = grand_total(device_grad(grads, seats, parts, []))
    return whole.reshape(costate.shape), grad.reshape(2, 2, LEVELS)


def solution(mesh):
    return jax.shard_map(
        per_device,
        mesh=mesh,
        in_specs=(P(None, "dev", "grp"), P(None, "dev", "grp"), P(), P(), P(), P()),
        out_specs=(P(None, "dev", "grp"), P()),
        check_vma=False,
    )
```

profile of v0, /device:TPU:0, one launch (start us, length us, event | category | flops | bytes accessed | tf_op | source)
XLA Modules:
  0.0 595.4 jit_solution(15033746906358941537)
XLA Ops:
  1.3 4.6 shard_map.77
  5.9 12.2 %shard_map.78 = (f32[8,256,128]{2,1,0:T(8,128)}, f32[8,256,128]{2,1,0:T(8,128)}, f32[8,256,128]{2,1,0:T(8,128)}, f32[8,256,128]{2,1,0:T(8,128)}) custom-call(bf16[512,128]{1,0:T(8,128)(2,1)} %get-tuple-element.84.weight_ref, f32[2,1024,2048]{2,1,0:T(8,128)} %field_ref.3), custom_call_target="tpu_custom_call" | custom-call | flops 1024 | bytes 1024 | tf_op jit(solution)/shard_map/pallas_call | solution.py:204
  18.6 2.5 collective-permute-start.7
  21.9 19.5 %shard_map.79 = (f32[8,256,128]{2,1,0:T(8,128)}, f32[8,256,128]{2,1,0:T(8,128)}, f32[8,256,128]{2,1,0:T(8,128)}, f32[8,256,128]{2,1,0:T(8,128)}, f32[8,256,128]{...) custom-call(bf16[2,192,256]{2,1,0:T(8,128)(2,1)} %slice.3.weight_ref, ...), custom_call_target="tpu_custom_call" | custom-call | flops 1024 | bytes 1024 | tf_op jit(solution)/shard_map/pallas_call | solution.py:229
  41.4 6.7 %shard_map.82 = (f32[8,256,128]{2,1,0:T(8,128)}, f32[8,256,128]{2,1,0:T(8,128)}, f32[8,256,128]{2,1,0:T(8,128)}, f32[8,256,128]{2,1,0:T(8,128)}) custom-call(s32[1]{0:T(128)} %bitcast.seat_ref, f32[2,8,4,4,8,2048]{5,4,3,2,1,0:T(8,128)} %bitcast.8, f32[8,256,128]{2,1,0:T(8,128)} %get-tuple-element.108.refs_0_), custom_call_target="tpu_custom_call" | custom-call | flops 1024 | bytes 1024 | tf_op jit(solution)/shard_map/pallas_call | solution.py:263
  48.1 19.2 %collective-permute-done.8.refs_3_ = f32[8,256,128]{2,1,0:T(8,128)S(1)} collective-permute-done((f32[8,256,128]{2,1,0:T(8,128)}, f32[8,256,128]{2,1,0:T(8,128)S(1)}, u32[]{:S(2)}, u32[]{:S(2)}) %collective-permute-start.8) | collective-permute-done | bytes 1048608 | tf_op jit(solution)/shard_map/ppermute | solution.py:459
  68.4 8.3 %shard_map.83.refs_5_ = f32[64,8,16,128]{3,2,1,0:T(8,128)} custom-call(bf16[256,256]{1,0:T(8,128)(2,1)} %get-tuple-element.82.weight_ref, f32[8,256,128]{2,1,0:T(8,128)} %get-tuple-element.85.refs_0_, f32[8,256,128]{2,1,0:T(8,128)} %copy-done.9, f32[8,256,128]{2,1,0:T(8,128)} %copy-done.10, f32[8,256,128]{2,1,0:T(8,128)} %copy-done.11, ...), custom_call_target="tpu_custom_call" | custom-call | flops 1024 | bytes 1024 | tf_op jit(solution)/shard_map/pallas_call | solution.py:326
  76.6 5.9 all-to-all-start
  86.9 21.9 %collective-permute-done.4.refs_2_ = f32[8,256,128]{2,1,0:T(8,128)S(1)} collective-permute-done((f32[8,256,128]{2,1,0:T(8,128)}, f32[8,256,128]{2,1,0:T(8,128)S(1)}, u32[]{:S(2)}, u32[]{:S(2)}) %collective-permute-start.4) | collective-permute-done | bytes 1048608 | tf_op jit(solution)/shard_map/ppermute | solution.py:459
  109.1 6.6 %shard_map.81 = (f32[8,256,128]{2,1,0:T(8,128)}, f32[8,256,128]{2,1,0:T(8,128)}, f32[8,256,128]{2,1,0:T(8,128)}, f32[8,256,128]{2,1,0:T(8,128)}) custom-call(s32[1]{0:T(128)} %bitcast.seat_ref, f32[2,8,4,4,8,2048]{5,4,3,2,1,0:T(8,128)} %bitcast.9, f32[8,256,128]{2,1,0:T(8,128)} %get-tuple-element.108.refs_0_), custom_call_target="tpu_custom_call" | custom-call | flops 1024 | bytes 1024 | tf_op jit(solution)/shard_map/pallas_call | solution.py:263
  115.7 6.7 %shard_map.80 = (f32[8,256,128]{2,1,0:T(8,128)}, f32[8,256,128]{2,1,0:T(8,128)}, f32[8,256,128]{2,1,0:T(8,128)}, f32[8,256,128]{2,1,0:T(8,128)}) custom-call(s32[1]{0:T(128)} %bitcast.seat_ref, f32[2,8,4,4,8,2048]{5,4,3,2,1,0:T(8,128)} %bitcast.10, f32[8,256,128]{2,1,0:T(8,128)} %get-tuple-element.108.refs_0_), custom_call_target="tpu_custom_call" | custom-call | flops 1024 | bytes 1024 | tf_op jit(solution)/shard_map/pallas_call | solution.py:263
  122.4 7.9 %collective-permute-done.5.refs_3_ = f32[8,256,128]{2,1,0:T(8,128)S(1)} collective-permute-done((f32[8,256,128]{2,1,0:T(8,128)}, f32[8,256,128]{2,1,0:T(8,128)S(1)}, u32[]{:S(2)}, u32[]{:S(2)}) %collective-permute-start.5) | collective-permute-done | bytes 1048608 | tf_op jit(solution)/shard_map/ppermute | solution.py:459
  131.8 8.4 %shard_map.84.refs_5_ = f32[64,8,16,128]{3,2,1,0:T(8,128)} custom-call(bf16[256,256]{1,0:T(8,128)(2,1)} %get-tuple-element.82.weight_ref, f32[8,256,128]{2,1,0:T(8,128)} %get-tuple-element.95.refs_0_, f32[8,256,128]{2,1,0:T(8,128)} %copy-done.12, f32[8,256,128]{2,1,0:T(8,128)} %copy-done.13, f32[8,256,128]{2,1,0:T(8,128)} %copy-done.14, ...), custom_call_target="tpu_custom_call" | custom-call | flops 1024 | bytes 1024 | tf_op jit(solution)/shard_map/pallas_call | solution.py:326
  140.2 1.8 collective-permute-start.2
  142.0 11.8 %collective-permute-done.10.refs_2_ = f32[8,256,128]{2,1,0:T(8,128)} collective-permute-done((f32[8,256,128]{2,1,0:T(8,128)}, f32[8,256,128]{2,1,0:T(8,128)}, u32[]{:S(2)}, u32[]{:S(2)}) %collective-permute-start.10) | collective-permute-done | bytes 1048608 | tf_op jit(solution)/shard_map/ppermute | solution.py:459
  155.3 20.0 %collective-permute-done.11.refs_3_ = f32[8,256,128]{2,1,0:T(8,128)} collective-permute-done((f32[8,256,128]{2,1,0:T(8,128)}, f32[8,256,128]{2,1,0:T(8,128)}, u32[]{:S(2)}, u32[]{:S(2)}) %collective-permute-start.11) | collective-permute-done | bytes 1048608 | tf_op jit(solution)/shard_map/ppermute | solution.py:459
  175.3 2.1 collective-permute-start.17
  177.4 5.7 all-to-all-start.1
  183.1 17.7 %shard_map.85 = (f32[8,256,128]{2,1,0:T(8,128)}, f32[8,256,128]{2,1,0:T(8,128)}, f32[8,256,128]{2,1,0:T(8,128)}, f32[8,256,128]{2,1,0:T(8,128)}, f32[2,64,128]{2,1,0:T(8,128)}) custom-call(bf16[3,2,256,256]{3,2,1,0:T(8,128)(2,1)} %get-tuple-element.80.lane_ref, bf16[3,256,256]{2,1,0:T(8,128)(2,1)} %get-tuple-element.81.level_ref, ...), custom_call_target="tpu_custom_call" | custom-call | flops 199999995904 | bytes 1024 | tf_op jit(solution)/shard_map/pallas_call | solution.py:398
  200.9 19.3 %collective-permute-done.2.refs_3_ = f32[8,256,128]{2,1,0:T(8,128)} collective-permute-done((f32[8,256,128]{2,1,0:T(8,128)}, f32[8,256,128]{2,1,0:T(8,128)}, u32[]{:S(2)}, u32[]{:S(2)}) %collective-permute-start.2) | collective-permute-done | bytes 1048608 | tf_op jit(solution)/shard_map/ppermute | solution.py:459
  221.8 8.5 %shard_map.86.refs_5_ = f32[64,8,16,128]{3,2,1,0:T(8,128)} custom-call(bf16[256,256]{1,0:T(8,128)(2,1)} %get-tuple-element.82.weight_ref, f32[8,256,128]{2,1,0:T(8,128)} %get-tuple-element.90.refs_0_, f32[8,256,128]{2,1,0:T(8,128)} %collective-permute-done.refs_1_, f32[8,256,128]{2,1,0:T(8,128)} %collective-permute-done.1.refs_2_, ...), custom_call_target="tpu_custom_call" | custom-call | flops 1024 | bytes 1024 | tf_op jit(solution)/shard_map/pallas_call | solution.py:326
  231.1 45.3 %all-to-all-done.1 = f32[64,8,16,128]{3,2,1,0:T(8,128)} async-done(((f32[64,8,16,128]{3,2,1,0:T(8,128)}), f32[64,8,16,128]{3,2,1,0:T(8,128)}, u32[]{:S(2)}, u32[]{:S(2)}) %all-to-all-start.1) | async-done | bytes 4194336 | tf_op jit(solution)/shard_map/all_to_all | solution.py:559
  276.5 4.8 all-to-all-start.3
  281.3 17.7 %shard_map.88 = (f32[8,256,128]{2,1,0:T(8,128)}, f32[8,256,128]{2,1,0:T(8,128)}, f32[8,256,128]{2,1,0:T(8,128)}, f32[8,256,128]{2,1,0:T(8,128)}, f32[2,64,128]{2,1,0:T(8,128)}) custom-call(bf16[3,2,256,256]{3,2,1,0:T(8,128)(2,1)} %get-tuple-element.80.lane_ref, bf16[3,256,256]{2,1,0:T(8,128)(2,1)} %get-tuple-element.81.level_ref, ...), custom_call_target="tpu_custom_call" | custom-call | flops 199999995904 | bytes 1024 | tf_op jit(solution)/shard_map/pallas_call | solution.py:398
  301.3 8.9 %collective-permute-done.23.refs_6_.refs_3_ = f32[8,256,128]{2,1,0:T(8,128)} collective-permute-done((f32[8,256,128]{2,1,0:T(8,128)}, f32[8,256,128]{2,1,0:T(8,128)}, u32[]{:S(2)}, u32[]{:S(2)}) %collective-permute-start.23) | collective-permute-done | bytes 1048608 | tf_op jit(solution)/shard_map/ppermute | solution.py:459
  312.6 20.9 %collective-permute-done.28.refs_2_ = f32[8,256,128]{2,1,0:T(8,128)S(1)} collective-permute-done((f32[8,256,128]{2,1,0:T(8,128)}, f32[8,256,128]{2,1,0:T(8,128)S(1)}, u32[]{:S(2)}, u32[]{:S(2)}) %collective-permute-start.28) | collective-permute-done | bytes 1048608 | tf_op jit(solution)/shard_map/ppermute | solution.py:459
  333.5 21.6 %collective-permute-done.29.refs_3_ = f32[8,256,128]{2,1,0:T(8,128)S(1)} collective-permute-done((f32[8,256,128]{2,1,0:T(8,128)}, f32[8,256,128]{2,1,0:T(8,128)S(1)}, u32[]{:S(2)}, u32[]{:S(2)}) %collective-permute-start.29) | collective-permute-done | bytes 1048608 | tf_op jit(solution)/shard_map/ppermute | solution.py:459
  357.8 6.6 %shard_map.87 = (f32[8,256,128]{2,1,0:T(8,128)}, f32[8,256,128]{2,1,0:T(8,128)}, f32[8,256,128]{2,1,0:T(8,128)}, f32[8,256,128]{2,1,0:T(8,128)}) custom-call(s32[1]{0:T(128)} %bitcast.seat_ref, f32[2,8,4,4,8,2048]{5,4,3,2,1,0:T(8,128)} %bitcast.11, f32[8,256,128]{2,1,0:T(8,128)} %get-tuple-element.108.refs_0_), custom_call_target="tpu_custom_call" | custom-call | flops 1024 | bytes 1024 | tf_op jit(solution)/shard_map/pallas_call | solution.py:263
  364.4 6.6 %shard_map.91.refs_4_ = f32[2,8,4,4,8,2048]{5,4,3,2,1,0:T(8,128)} custom-call(s32[1]{0:T(128)} %bitcast.seat_ref, f32[8,256,128]{2,1,0:T(8,128)} %get-tuple-element.107.refs_6_.refs_4_.refs_0_, f32[8,256,128]{2,1,0:T(8,128)} %collective-permute-done.21.refs_4_.refs_1_, f32[8,256,128]{2,1,0:T(8,128)} %collective-permute-done.22.refs_5_.refs_2_, ...), custom_call_target="tpu_custom_call" | custom-call | flops 1024 | bytes 1024 | tf_op jit(solution)/shard_map/pallas_call | solution.py:439
  371.0 6.6 %shard_map.92.refs_4_ = f32[2,8,4,4,8,2048]{5,4,3,2,1,0:T(8,128)} custom-call(s32[1]{0:T(128)} %bitcast.seat_ref, f32[8,256,128]{2,1,0:T(8,128)} %get-tuple-element.117.refs_6_.refs_7_.refs_0_, f32[8,256,128]{2,1,0:T(8,128)} %copy-done.6, f32[8,256,128]{2,1,0:T(8,128)} %copy-done.7, f32[8,256,128]{2,1,0:T(8,128)} %copy-done.8, ...), custom_call_target="tpu_custom_call", output_to_operand_aliasing={{}: (5, {})} | custom-call | flops 1024 | bytes 1024 | tf_op jit(solution)/shard_map/pallas_call | solution.py:439
  378.4 21.6 %collective-permute-done.14.refs_3_ = f32[8,256,128]{2,1,0:T(8,128)S(1)} collective-permute-done((f32[8,256,128]{2,1,0:T(8,128)}, f32[8,256,128]{2,1,0:T(8,128)S(1)}, u32[]{:S(2)}, u32[]{:S(2)}) %collective-permute-start.14) | collective-permute-done | bytes 1048608 | tf_op jit(solution)/shard_map/ppermute | solution.py:459
  401.4 8.3 %shard_map.89 = f32[64,8,16,128]{3,2,1,0:T(8,128)} custom-call(bf16[256,256]{1,0:T(8,128)(2,1)} %get-tuple-element.82.weight_ref, f32[8,256,128]{2,1,0:T(8,128)} %get-tuple-element.108.refs_0_, f32[8,256,128]{2,1,0:T(8,128)} %copy-done, f32[8,256,128]{2,1,0:T(8,128)} %copy-done.1, f32[8,256,128]{2,1,0:T(8,128)} %copy-done.2, ...), custom_call_target="tpu_custom_call" | custom-call | flops 1024 | bytes 1024 | tf_op jit(solution)/shard_map/pallas_call | solution.py:326
  411.1 5.9 all-to-all-start.2
  417.1 6.4 %collective-permute-done.19.refs_2_ = f32[8,256,128]{2,1,0:T(8,128)} collective-permute-done((f32[8,256,128]{2,1,0:T(8,128)}, f32[8,256,128]{2,1,0:T(8,128)}, u32[]{:S(2)}, u32[]{:S(2)}) %collective-permute-start.19) | collective-permute-done | bytes 1048608 | tf_op jit(solution)/shard_map/ppermute | solution.py:459
  423.5 21.5 %collective-permute-done.20.refs_3_ = f32[8,256,128]{2,1,0:T(8,128)} collective-permute-done((f32[8,256,128]{2,1,0:T(8,128)}, f32[8,256,128]{2,1,0:T(8,128)}, u32[]{:S(2)}, u32[]{:S(2)}) %collective-permute-start.20) | collective-permute-done | bytes 1048608 | tf_op jit(solution)/shard_map/ppermute | solution.py:459
  445.0 17.8 %shard_map.90 = (f32[8,256,128]{2,1,0:T(8,128)}, f32[8,256,128]{2,1,0:T(8,128)}, f32[8,256,128]{2,1,0:T(8,128)}, f32[8,256,128]{2,1,0:T(8,128)}, f32[2,64,128]{2,1,0:T(8,128)}) custom-call(bf16[3,2,256,256]{3,2,1,0:T(8,128)(2,1)} %get-tuple-element.80.lane_ref, bf16[3,256,256]{2,1,0:T(8,128)(2,1)} %get-tuple-element.81.level_ref, ...), custom_call_target="tpu_custom_call" | custom-call | flops 199999995904 | bytes 1024 | tf_op jit(solution)/shard_map/pallas_call | solution.py:398
  462.8 5.6 collective-permute-done.25.refs_2_
  468.4 21.5 %collective-permute-done.26.refs_3_ = f32[8,256,128]{2,1,0:T(8,128)} collective-permute-done((f32[8,256,128]{2,1,0:T(8,128)}, f32[8,256,128]{2,1,0:T(8,128)}, u32[]{:S(2)}, u32[]{:S(2)}) %collective-permute-start.26) | collective-permute-done | bytes 1048608 | tf_op jit(solution)/shard_map/ppermute | solution.py:459
  491.8 18.6 %all-to-all-done.2 = f32[64,8,16,128]{3,2,1,0:T(8,128)} async-done(((f32[64,8,16,128]{3,2,1,0:T(8,128)}), f32[64,8,16,128]{3,2,1,0:T(8,128)}, u32[]{:S(2)}, u32[]{:S(2)}) %all-to-all-start.2) | async-done | bytes 4194336 | tf_op jit(solution)/shard_map/all_to_all | solution.py:559
  510.4 17.7 %shard_map.93 = (f32[8,256,128]{2,1,0:T(8,128)}, f32[8,256,128]{2,1,0:T(8,128)}, f32[8,256,128]{2,1,0:T(8,128)}, f32[8,256,128]{2,1,0:T(8,128)}, f32[2,64,128]{2,1,0:T(8,128)}) custom-call(bf16[3,2,256,256]{3,2,1,0:T(8,128)(2,1)} %get-tuple-element.80.lane_ref, bf16[3,256,256]{2,1,0:T(8,128)(2,1)} %get-tuple-element.81.level_ref, ...), custom_call_target="tpu_custom_call" | custom-call | flops 199999995904 | bytes 1024 | tf_op jit(solution)/shard_map/pallas_call | solution.py:398
  528.2 9.4 %collective-permute-done.32.refs_3_ = f32[8,256,128]{2,1,0:T(8,128)} collective-permute-done((f32[8,256,128]{2,1,0:T(8,128)}, f32[8,256,128]{2,1,0:T(8,128)}, u32[]{:S(2)}, u32[]{:S(2)}) %collective-permute-start.32) | collective-permute-done | bytes 1048608 | tf_op jit(solution)/shard_map/ppermute | solution.py:459
  539.6 2.4 shard_map.96
  544.4 2.1 collective-permute-start.37
  548.0 2.0 collective-permute-start.38
  551.6 2.9 collective-permute-start.39
  557.6 6.6 %shard_map.94.refs_4_ = f32[2,8,4,4,8,2048]{5,4,3,2,1,0:T(8,128)} custom-call(s32[1]{0:T(128)} %bitcast.seat_ref, f32[8,256,128]{2,1,0:T(8,128)} %get-tuple-element.150.refs_5_.refs_0_, f32[8,256,128]{2,1,0:T(8,128)} %collective-permute-done.30.refs_1_, f32[8,256,128]{2,1,0:T(8,128)} %collective-permute-done.31.refs_2_, ...), custom_call_target="tpu_custom_call", output_to_operand_aliasing={{}: (5, {})} | custom-call | flops 1024 | bytes 1024 | tf_op jit(solution)/shard_map/pallas_call | solution.py:439
  564.2 21.7 %collective-permute-done.40 = f32[4,64]{1,0:T(4,128)S(1)} collective-permute-done((f32[4,64]{1,0:T(4,128)S(1)}, f32[4,64]{1,0:T(4,128)S(1)}, u32[]{:S(2)}, u32[]{:S(2)}) %collective-permute-start.40) | collective-permute-done | bytes 1056 | tf_op jit(solution)/shard_map/ppermute | solution.py:503
  588.8 6.6 %shard_map.95 = f32[2,8,4,4,8,2048]{5,4,3,2,1,0:T(8,128)} custom-call(s32[1]{0:T(128)} %bitcast.seat_ref, f32[8,256,128]{2,1,0:T(8,128)} %get-tuple-element.146.refs_0_, f32[8,256,128]{2,1,0:T(8,128)} %copy-done.3, f32[8,256,128]{2,1,0:T(8,128)} %copy-done.4, f32[8,256,128]{2,1,0:T(8,128)} %copy-done.5, ...), custom_call_target="tpu_custom_call", output_to_operand_aliasing={{}: (5, {})} | custom-call | flops 1024 | bytes 1024 | tf_op jit(solution)/shard_map/pallas_call | solution.py:439
  (100 shorter events, 38.8 us)
Async XLA Ops:
  18.1 30.0 %collective-permute-start.6 = (f32[8,256,128]{2,1,0:T(8,128)}, f32[8,256,128]{2,1,0:T(8,128)S(1)}, u32[]{:S(2)}, u32[]{:S(2)}) collective-permute-start(f32[8,256,128]{2,1,0:T(8,128)} %get-tuple-element.100), channel_id=1, source_target_pairs={{0,8},{8,0},{16,24},{24,16},{1,9},{9,1},{17,25},{25,17},{2,10},{10... | collective-permute-start | bytes 3145736 | tf_op jit(solution)/shard_map/ppermute | solution.py:459
  18.6 29.5 %collective-permute-start.7 = (f32[8,256,128]{2,1,0:T(8,128)}, f32[8,256,128]{2,1,0:T(8,128)S(1)}, u32[]{:S(2)}, u32[]{:S(2)}) collective-permute-start(f32[8,256,128]{2,1,0:T(8,128)} %get-tuple-element.101), channel_id=1, source_target_pairs={{0,16},{8,24},{16,0},{24,8},{1,17},{9,25},{17,1},{25,9},{2,18},{10... | collective-permute-start | bytes 3145736 | tf_op jit(solution)/shard_map/ppermute | solution.py:459
  21.1 46.2 %collective-permute-start.8 = (f32[8,256,128]{2,1,0:T(8,128)}, f32[8,256,128]{2,1,0:T(8,128)S(1)}, u32[]{:S(2)}, u32[]{:S(2)}) collective-permute-start(f32[8,256,128]{2,1,0:T(8,128)} %get-tuple-element.102), channel_id=1, source_target_pairs={{0,24},{8,16},{16,8},{24,0},{1,25},{9,17},{17,9},{25,1},{2,26},{10... | collective-permute-start | bytes 3145736 | tf_op jit(solution)/shard_map/ppermute | solution.py:459
  76.6 100.8 %all-to-all-start = ((f32[64,8,16,128]{3,2,1,0:T(8,128)}), f32[64,8,16,128]{3,2,1,0:T(8,128)}, u32[]{:S(2)}, u32[]{:S(2)}) async-start(f32[64,8,16,128]{3,2,1,0:T(8,128)} %shard_map.83.refs_5_), calls=%async_computation | async-start | bytes 8388608 | tf_op jit(solution)/shard_map/all_to_all | solution.py:559
  82.5 2.9 collective-permute-start.3
  82.5 26.2 %collective-permute-start.4 = (f32[8,256,128]{2,1,0:T(8,128)}, f32[8,256,128]{2,1,0:T(8,128)S(1)}, u32[]{:S(2)}, u32[]{:S(2)}) collective-permute-start(f32[8,256,128]{2,1,0:T(8,128)} %get-tuple-element.97), channel_id=1, source_target_pairs={{0,16},{8,24},{16,0},{24,8},{1,17},{9,25},{17,1},{25,9},{2,18},{10... | collective-permute-start | bytes 3145736 | tf_op jit(solution)/shard_map/ppermute | solution.py:459
  84.1 46.3 %collective-permute-start.5 = (f32[8,256,128]{2,1,0:T(8,128)}, f32[8,256,128]{2,1,0:T(8,128)S(1)}, u32[]{:S(2)}, u32[]{:S(2)}) collective-permute-start(f32[8,256,128]{2,1,0:T(8,128)} %get-tuple-element.98), channel_id=1, source_target_pairs={{0,24},{8,16},{16,8},{24,0},{1,25},{9,17},{17,9},{25,1},{2,26},{10... | collective-permute-start | bytes 3145736 | tf_op jit(solution)/shard_map/ppermute | solution.py:459
  84.4 55.8 %collective-permute-start = (f32[8,256,128]{2,1,0:T(8,128)}, f32[8,256,128]{2,1,0:T(8,128)}, u32[]{:S(2)}, u32[]{:S(2)}) collective-permute-start(f32[8,256,128]{2,1,0:T(8,128)} %get-tuple-element.91), channel_id=1, source_target_pairs={{0,8},{8,0},{16,24},{24,16},{1,9},{9,1},{17,25},{25,17},{2,10},{10... | collective-permute-start | bytes 3145736 | tf_op jit(solution)/shard_map/ppermute | solution.py:459
  84.7 57.3 %collective-permute-start.9 = (f32[8,256,128]{2,1,0:T(8,128)}, f32[8,256,128]{2,1,0:T(8,128)}, u32[]{:S(2)}, u32[]{:S(2)}) collective-permute-start(f32[8,256,128]{2,1,0:T(8,128)} %get-tuple-element.104), channel_id=1, source_target_pairs={{0,8},{8,0},{16,24},{24,16},{1,9},{9,1},{17,25},{25,17},{2,10},{10... | collective-permute-start | bytes 3145736 | tf_op jit(solution)/shard_map/ppermute | solution.py:459
  85.4 30.4 %copy-start.12 = (f32[8,256,128]{2,1,0:T(8,128)}, f32[8,256,128]{2,1,0:T(8,128)S(1)}, u32[]{:S(2)}) copy-start(f32[8,256,128]{2,1,0:T(8,128)S(1)} %collective-permute-done.3.refs_1_) | copy-start | bytes 3145732
  85.4 68.4 %collective-permute-start.10 = (f32[8,256,128]{2,1,0:T(8,128)}, f32[8,256,128]{2,1,0:T(8,128)}, u32[]{:S(2)}, u32[]{:S(2)}) collective-permute-start(f32[8,256,128]{2,1,0:T(8,128)} %get-tuple-element.105), channel_id=1, source_target_pairs={{0,16},{8,24},{16,0},{24,8},{1,17},{9,25},{17,1},{25,9},{2,18},{10... | collective-permute-start | bytes 3145736 | tf_op jit(solution)/shard_map/ppermute | solution.py:459
  108.8 66.6 %collective-permute-start.11 = (f32[8,256,128]{2,1,0:T(8,128)}, f32[8,256,128]{2,1,0:T(8,128)}, u32[]{:S(2)}, u32[]{:S(2)}) collective-permute-start(f32[8,256,128]{2,1,0:T(8,128)} %get-tuple-element.106), channel_id=1, source_target_pairs={{0,24},{8,16},{16,8},{24,0},{1,25},{9,17},{17,9},{25,1},{2,26},{10... | collective-permute-start | bytes 3145736 | tf_op jit(solution)/shard_map/ppermute | solution.py:459
  130.3 70.5 %collective-permute-start.1 = (f32[8,256,128]{2,1,0:T(8,128)}, f32[8,256,128]{2,1,0:T(8,128)}, u32[]{:S(2)}, u32[]{:S(2)}) collective-permute-start(f32[8,256,128]{2,1,0:T(8,128)} %get-tuple-element.92), channel_id=1, source_target_pairs={{0,16},{8,24},{16,0},{24,8},{1,17},{9,25},{17,1},{25,9},{2,18},{10... | collective-permute-start | bytes 3145736 | tf_op jit(solution)/shard_map/ppermute | solution.py:459
  140.2 80.1 %collective-permute-start.2 = (f32[8,256,128]{2,1,0:T(8,128)}, f32[8,256,128]{2,1,0:T(8,128)}, u32[]{:S(2)}, u32[]{:S(2)}) collective-permute-start(f32[8,256,128]{2,1,0:T(8,128)} %get-tuple-element.93), channel_id=1, source_target_pairs={{0,24},{8,16},{16,8},{24,0},{1,25},{9,17},{17,9},{25,1},{2,26},{10... | collective-permute-start | bytes 3145736 | tf_op jit(solution)/shard_map/ppermute | solution.py:459
  142.0 88.2 %collective-permute-start.15 = (f32[8,256,128]{2,1,0:T(8,128)}, f32[8,256,128]{2,1,0:T(8,128)}, u32[]{:S(2)}, u32[]{:S(2)}) collective-permute-start(f32[8,256,128]{2,1,0:T(8,128)} %get-tuple-element.114), channel_id=1, source_target_pairs={{0,8},{8,0},{16,24},{24,16},{1,9},{9,1},{17,25},{25,17},{2,10},{10... | collective-permute-start | bytes 3145736 | tf_op jit(solution)/shard_map/ppermute | solution.py:459
  153.8 127.4 %collective-permute-start.16 = (f32[8,256,128]{2,1,0:T(8,128)}, f32[8,256,128]{2,1,0:T(8,128)}, u32[]{:S(2)}, u32[]{:S(2)}) collective-permute-start(f32[8,256,128]{2,1,0:T(8,128)} %get-tuple-element.115), channel_id=1, source_target_pairs={{0,16},{8,24},{16,0},{24,8},{1,17},{9,25},{17,1},{25,9},{2,18},{10... | collective-permute-start | bytes 3145736 | tf_op jit(solution)/shard_map/ppermute | solution.py:459
  175.3 105.9 %collective-permute-start.17 = (f32[8,256,128]{2,1,0:T(8,128)}, f32[8,256,128]{2,1,0:T(8,128)}, u32[]{:S(2)}, u32[]{:S(2)}) collective-permute-start(f32[8,256,128]{2,1,0:T(8,128)} %get-tuple-element.116), channel_id=1, source_target_pairs={{0,24},{8,16},{16,8},{24,0},{1,25},{9,17},{17,9},{25,1},{2,26},{10... | collective-permute-start | bytes 3145736 | tf_op jit(solution)/shard_map/ppermute | solution.py:459
  177.4 99.0 %all-to-all-start.1 = ((f32[64,8,16,128]{3,2,1,0:T(8,128)}), f32[64,8,16,128]{3,2,1,0:T(8,128)}, u32[]{:S(2)}, u32[]{:S(2)}) async-start(f32[64,8,16,128]{3,2,1,0:T(8,128)} %shard_map.84.refs_5_), calls=%async_computation.1 | async-start | bytes 8388608 | tf_op jit(solution)/shard_map/all_to_all | solution.py:559
  200.8 98.8 %collective-permute-start.21 = (f32[8,256,128]{2,1,0:T(8,128)}, f32[8,256,128]{2,1,0:T(8,128)}, u32[]{:S(2)}, u32[]{:S(2)}) collective-permute-start(f32[8,256,128]{2,1,0:T(8,128)} %get-tuple-element.121), channel_id=1, source_target_pairs={{0,8},{8,0},{16,24},{24,16},{1,9},{9,1},{17,25},{25,17},{2,10},{10... | collective-permute-start | bytes 3145736 | tf_op jit(solution)/shard_map/ppermute | solution.py:459
  220.3 80.7 %collective-permute-start.22 = (f32[8,256,128]{2,1,0:T(8,128)}, f32[8,256,128]{2,1,0:T(8,128)}, u32[]{:S(2)}, u32[]{:S(2)}) collective-permute-start(f32[8,256,128]{2,1,0:T(8,128)} %get-tuple-element.122), channel_id=1, source_target_pairs={{0,16},{8,24},{16,0},{24,8},{1,17},{9,25},{17,1},{25,9},{2,18},{10... | collective-permute-start | bytes 3145736 | tf_op jit(solution)/shard_map/ppermute | solution.py:459
  230.2 79.9 %collective-permute-start.23 = (f32[8,256,128]{2,1,0:T(8,128)}, f32[8,256,128]{2,1,0:T(8,128)}, u32[]{:S(2)}, u32[]{:S(2)}) collective-permute-start(f32[8,256,128]{2,1,0:T(8,128)} %get-tuple-element.123), channel_id=1, source_target_pairs={{0,24},{8,16},{16,8},{24,0},{1,25},{9,17},{17,9},{25,1},{2,26},{10... | collective-permute-start | bytes 3145736 | tf_op jit(solution)/shard_map/ppermute | solution.py:459
  276.5 134.7 %all-to-all-start.3 = ((f32[64,8,16,128]{3,2,1,0:T(8,128)}), f32[64,8,16,128]{3,2,1,0:T(8,128)}, u32[]{:S(2)}, u32[]{:S(2)}) async-start(f32[64,8,16,128]{3,2,1,0:T(8,128)} %shard_map.86.refs_5_), calls=%async_computation.3 | async-start | bytes 8388608 | tf_op jit(solution)/shard_map/all_to_all | solution.py:559
  299.0 12.6 %collective-permute-start.27 = (f32[8,256,128]{2,1,0:T(8,128)}, f32[8,256,128]{2,1,0:T(8,128)S(1)}, u32[]{:S(2)}, u32[]{:S(2)}) collective-permute-start(f32[8,256,128]{2,1,0:T(8,128)} %get-tuple-element.135), channel_id=1, source_target_pairs={{0,8},{8,0},{16,24},{24,16},{1,9},{9,1},{17,25},{25,17},{2,10},{10... | collective-permute-start | bytes 3145736 | tf_op jit(solution)/shard_map/ppermute | solution.py:459
  299.1 34.4 %collective-permute-start.28 = (f32[8,256,128]{2,1,0:T(8,128)}, f32[8,256,128]{2,1,0:T(8,128)S(1)}, u32[]{:S(2)}, u32[]{:S(2)}) collective-permute-start(f32[8,256,128]{2,1,0:T(8,128)} %get-tuple-element.136), channel_id=1, source_target_pairs={{0,16},{8,24},{16,0},{24,8},{1,17},{9,25},{17,1},{25,9},{2,18},{10... | collective-permute-start | bytes 3145736 | tf_op jit(solution)/shard_map/ppermute | solution.py:459
  299.7 55.4 %collective-permute-start.29 = (f32[8,256,128]{2,1,0:T(8,128)}, f32[8,256,128]{2,1,0:T(8,128)S(1)}, u32[]{:S(2)}, u32[]{:S(2)}) collective-permute-start(f32[8,256,128]{2,1,0:T(8,128)} %get-tuple-element.137), channel_id=1, source_target_pairs={{0,24},{8,16},{16,8},{24,0},{1,25},{9,17},{17,9},{25,1},{2,26},{10... | collective-permute-start | bytes 3145736 | tf_op jit(solution)/shard_map/ppermute | solution.py:459
  301.0 55.5 %collective-permute-start.12 = (f32[8,256,128]{2,1,0:T(8,128)}, f32[8,256,128]{2,1,0:T(8,128)S(1)}, u32[]{:S(2)}, u32[]{:S(2)}) collective-permute-start(f32[8,256,128]{2,1,0:T(8,128)} %get-tuple-element.109), channel_id=1, source_target_pairs={{0,8},{8,0},{16,24},{24,16},{1,9},{9,1},{17,25},{25,17},{2,10},{10... | collective-permute-start | bytes 3145736 | tf_op jit(solution)/shard_map/ppermute | solution.py:459
  310.2 68.2 %collective-permute-start.13 = (f32[8,256,128]{2,1,0:T(8,128)}, f32[8,256,128]{2,1,0:T(8,128)S(1)}, u32[]{:S(2)}, u32[]{:S(2)}) collective-permute-start(f32[8,256,128]{2,1,0:T(8,128)} %get-tuple-element.110), channel_id=1, source_target_pairs={{0,16},{8,24},{16,0},{24,8},{1,17},{9,25},{17,1},{25,9},{2,18},{10... | collective-permute-start | bytes 3145736 | tf_op jit(solution)/shard_map/ppermute | solution.py:459
  311.7 44.8 %copy-start.6 = (f32[8,256,128]{2,1,0:T(8,128)}, f32[8,256,128]{2,1,0:T(8,128)S(1)}, u32[]{:S(2)}) copy-start(f32[8,256,128]{2,1,0:T(8,128)S(1)} %collective-permute-done.27.refs_1_) | copy-start | bytes 3145732
  311.7 88.3 %collective-permute-start.14 = (f32[8,256,128]{2,1,0:T(8,128)}, f32[8,256,128]{2,1,0:T(8,128)S(1)}, u32[]{:S(2)}, u32[]{:S(2)}) collective-permute-start(f32[8,256,128]{2,1,0:T(8,128)} %get-tuple-element.111), channel_id=1, source_target_pairs={{0,24},{8,16},{16,8},{24,0},{1,25},{9,17},{17,9},{25,1},{2,26},{10... | collective-permute-start | bytes 3145736 | tf_op jit(solution)/shard_map/ppermute | solution.py:459
  333.5 23.0 %copy-start.7 = (f32[8,256,128]{2,1,0:T(8,128)}, f32[8,256,128]{2,1,0:T(8,128)S(1)}, u32[]{:S(2)}) copy-start(f32[8,256,128]{2,1,0:T(8,128)S(1)} %collective-permute-done.28.refs_2_) | copy-start | bytes 3145732
  333.5 76.3 %collective-permute-start.18 = (f32[8,256,128]{2,1,0:T(8,128)}, f32[8,256,128]{2,1,0:T(8,128)}, u32[]{:S(2)}, u32[]{:S(2)}) collective-permute-start(f32[8,256,128]{2,1,0:T(8,128)} %get-tuple-element.118), channel_id=1, source_target_pairs={{0,8},{8,0},{16,24},{24,16},{1,9},{9,1},{17,25},{25,17},{2,10},{10... | collective-permute-start | bytes 3145736 | tf_op jit(solution)/shard_map/ppermute | solution.py:459
  355.0 68.4 %collective-permute-start.19 = (f32[8,256,128]{2,1,0:T(8,128)}, f32[8,256,128]{2,1,0:T(8,128)}, u32[]{:S(2)}, u32[]{:S(2)}) collective-permute-start(f32[8,256,128]{2,1,0:T(8,128)} %get-tuple-element.119), channel_id=1, source_target_pairs={{0,16},{8,24},{16,0},{24,8},{1,17},{9,25},{17,1},{25,9},{2,18},{10... | collective-permute-start | bytes 3145736 | tf_op jit(solution)/shard_map/ppermute | solution.py:459
  356.5 88.5 %collective-permute-start.20 = (f32[8,256,128]{2,1,0:T(8,128)}, f32[8,256,128]{2,1,0:T(8,128)}, u32[]{:S(2)}, u32[]{:S(2)}) collective-permute-start(f32[8,256,128]{2,1,0:T(8,128)} %get-tuple-element.120), channel_id=1, source_target_pairs={{0,24},{8,16},{16,8},{24,0},{1,25},{9,17},{17,9},{25,1},{2,26},{10... | collective-permute-start | bytes 3145736 | tf_op jit(solution)/shard_map/ppermute | solution.py:459
  378.4 84.4 %collective-permute-start.24 = (f32[8,256,128]{2,1,0:T(8,128)}, f32[8,256,128]{2,1,0:T(8,128)}, u32[]{:S(2)}, u32[]{:S(2)}) collective-permute-start(f32[8,256,128]{2,1,0:T(8,128)} %get-tuple-element.128), channel_id=1, source_target_pairs={{0,8},{8,0},{16,24},{24,16},{1,9},{9,1},{17,25},{25,17},{2,10},{10... | collective-permute-start | bytes 3145736 | tf_op jit(solution)/shard_map/ppermute | solution.py:459
  400.0 68.4 %collective-permute-start.25 = (f32[8,256,128]{2,1,0:T(8,128)}, f32[8,256,128]{2,1,0:T(8,128)}, u32[]{:S(2)}, u32[]{:S(2)}) collective-permute-start(f32[8,256,128]{2,1,0:T(8,128)} %get-tuple-element.129), channel_id=1, source_target_pairs={{0,16},{8,24},{16,0},{24,8},{1,17},{9,25},{17,1},{25,9},{2,18},{10... | collective-permute-start | bytes 3145736 | tf_op jit(solution)/shard_map/ppermute | solution.py:459
  409.8 80.2 %collective-permute-start.26 = (f32[8,256,128]{2,1,0:T(8,128)}, f32[8,256,128]{2,1,0:T(8,128)}, u32[]{:S(2)}, u32[]{:S(2)}) collective-permute-start(f32[8,256,128]{2,1,0:T(8,128)} %get-tuple-element.130), channel_id=1, source_target_pairs={{0,24},{8,16},{16,8},{24,0},{1,25},{9,17},{17,9},{25,1},{2,26},{10... | collective-permute-start | bytes 3145736 | tf_op jit(solution)/shard_map/ppermute | solution.py:459
  411.1 99.3 %all-to-all-start.2 = ((f32[64,8,16,128]{3,2,1,0:T(8,128)}), f32[64,8,16,128]{3,2,1,0:T(8,128)}, u32[]{:S(2)}, u32[]{:S(2)}) async-start(f32[64,8,16,128]{3,2,1,0:T(8,128)} %shard_map.89), calls=%async_computation.2 | async-start | bytes 8388608 | tf_op jit(solution)/shard_map/all_to_all | solution.py:559
  489.9 38.2 %collective-permute-start.30 = (f32[8,256,128]{2,1,0:T(8,128)}, f32[8,256,128]{2,1,0:T(8,128)}, u32[]{:S(2)}, u32[]{:S(2)}) collective-permute-start(f32[8,256,128]{2,1,0:T(8,128)} %get-tuple-element.143), channel_id=1, source_target_pairs={{0,8},{8,0},{16,24},{24,16},{1,9},{9,1},{17,25},{25,17},{2,10},{10... | collective-permute-start | bytes 3145736 | tf_op jit(solution)/shard_map/ppermute | solution.py:459
  490.2 37.9 %collective-permute-start.31 = (f32[8,256,128]{2,1,0:T(8,128)}, f32[8,256,128]{2,1,0:T(8,128)}, u32[]{:S(2)}, u32[]{:S(2)}) collective-permute-start(f32[8,256,128]{2,1,0:T(8,128)} %get-tuple-element.144), channel_id=1, source_target_pairs={{0,16},{8,24},{16,0},{24,8},{1,17},{9,25},{17,1},{25,9},{2,18},{10... | collective-permute-start | bytes 3145736 | tf_op jit(solution)/shard_map/ppermute | solution.py:459
  491.7 45.9 %collective-permute-start.32 = (f32[8,256,128]{2,1,0:T(8,128)}, f32[8,256,128]{2,1,0:T(8,128)}, u32[]{:S(2)}, u32[]{:S(2)}) collective-permute-start(f32[8,256,128]{2,1,0:T(8,128)} %get-tuple-element.145), channel_id=1, source_target_pairs={{0,24},{8,16},{16,8},{24,0},{1,25},{9,17},{17,9},{25,1},{2,26},{10... | collective-permute-start | bytes 3145736 | tf_op jit(solution)/shard_map/ppermute | solution.py:459
  537.6 48.9 %collective-permute-start.33 = (f32[8,256,128]{2,1,0:T(8,128)}, f32[8,256,128]{2,1,0:T(8,128)S(1)}, u32[]{:S(2)}, u32[]{:S(2)}) collective-permute-start(f32[8,256,128]{2,1,0:T(8,128)} %get-tuple-element.147), channel_id=1, source_target_pairs={{0,8},{8,0},{16,24},{24,16},{1,9},{9,1},{17,25},{25,17},{2,10},{10... | collective-permute-start | bytes 3145736 | tf_op jit(solution)/shard_map/ppermute | solution.py:459
  538.1 48.4 %collective-permute-start.34 = (f32[8,256,128]{2,1,0:T(8,128)}, f32[8,256,128]{2,1,0:T(8,128)S(1)}, u32[]{:S(2)}, u32[]{:S(2)}) collective-permute-start(f32[8,256,128]{2,1,0:T(8,128)} %get-tuple-element.148), channel_id=1, source_target_pairs={{0,16},{8,24},{16,0},{24,8},{1,17},{9,25},{17,1},{25,9},{2,18},{10... | collective-permute-start | bytes 3145736 | tf_op jit(solution)/shard_map/ppermute | solution.py:459
  539.6 46.9 %collective-permute-start.35 = (f32[8,256,128]{2,1,0:T(8,128)}, f32[8,256,128]{2,1,0:T(8,128)S(1)}, u32[]{:S(2)}, u32[]{:S(2)}) collective-permute-start(f32[8,256,128]{2,1,0:T(8,128)} %get-tuple-element.149), channel_id=1, source_target_pairs={{0,24},{8,16},{16,8},{24,0},{1,25},{9,17},{17,9},{25,1},{2,26},{10... | collective-permute-start | bytes 3145736 | tf_op jit(solution)/shard_map/ppermute | solution.py:459
  542.0 1.7 collective-permute-start.36
  544.4 3.7 collective-permute-start.37
  548.0 3.6 collective-permute-start.38
  551.6 4.5 collective-permute-start.39
  556.1 29.8 %collective-permute-start.40 = (f32[4,64]{1,0:T(4,128)S(1)}, f32[4,64]{1,0:T(4,128)S(1)}, u32[]{:S(2)}, u32[]{:S(2)}) collective-permute-start(f32[4,64]{1,0:T(4,128)S(1)} %add.18), channel_id=1, source_target_pairs={{0,16},{8,24},{16,0},{24,8},{1,17},{9,25},{17,1},{25,9},{2,18},{10... | collective-permute-start | bytes 3080 | tf_op jit(solution)/shard_map/ppermute | solution.py:503
  (13 other events, 100.4 us)
where the time goes:
time: 598 us; the launch traced here: 595 us
  waiting for transfers between devices  330 us (55%)
  Pallas kernels  196 us (33%)
  starting transfers between devices  62.2 us (10%)
    ppermute x36, waiting for transfers between devices, swap(): moved.append(lax.ppermute(pieces[step], 'grp', pairs))  239 us
    pallas_call x4, Pallas kernels, close_columns(): pl.pallas_call(functools.partial(close_kernel, parts, size), grid=(firsts...  71 us
    all_to_all x4, waiting for transfers between devices, per_device(): lax.all_to_all(field, 'dev', split_axis=0, concat_axis=0, tiled=True)  64 us
    pallas_call x4, Pallas kernels, turn_columns(): pl.pallas_call(functools.partial(turn_kernel, parts, size), grid=(firsts,...  33.5 us
    ppermute x36, starting transfers between devices, swap(): moved.append(lax.ppermute(pieces[step], 'grp', pairs))  30.8 us
    ppermute x5, waiting for transfers between devices, grand_total(): value = value + lax.ppermute(value, axis, pairs)  27.4 us
    pallas_call x4, Pallas kernels, cut_pieces(): pl.pallas_call(functools.partial(cut_kernel, size, len(waited)), grid=(fi...  26.5 us
    pallas_call x4, Pallas kernels, place_pieces(): pl.pallas_call(functools.partial(place_kernel, parts, size, aliased), gri...  26.5 us
  transfers between devices with their start and end apart: 45, of which 24 were waited for; matrix products, arithmetic and copies ran while one was open for 0% of the time, Pallas kernels for 28%

commit v1 on v0

--- a/solution.py
+++ b/solution.py
@@ -452,6 +452,37 @@
     )(seat, *pieces, *([held] if aliased else []))
 
 
+def place_one_kernel(size, seat_ref, piece_ref, held_ref, out_ref):
+    del seat_ref, held_ref
+    for half in range(2):
+        for level in range(out_ref.shape[-1] // WIDE):
+            start = (2 * level + half) * size
+            out_ref[half, :, level * WIDE:(level + 1) * WIDE] = piece_ref[start:start + size, :]
+
+
+def place_one(piece, seat, held, chunk, step, shape, size):
+    cols = shape[-1]
+    return pl.pallas_call(
+        functools.partial(place_one_kernel, size),
+        grid_spec=pltpu.PrefetchScalarGridSpec(
+            num_scalar_prefetch=1,
+            grid=(shape[1],),
+            in_specs=[
+                pl.BlockSpec((None,) + piece.shape[1:], lambda i, own: (i, 0, 0)),
+                pl.BlockSpec(memory_space=pl.ANY),
+            ],
+            out_specs=pl.BlockSpec(
+                (2, None, None, None, size, cols),
+                lambda i, own: (0, i, lax.bitwise_xor(own[0], step), chunk, 0, 0),
+            ),
+        ),
+        out_shape=jax.ShapeDtypeStruct(shape, F32),
+        input_output_aliases={2: 0},
+        compiler_params=PARAMS,
+        cost_estimate=SMALL,
+    )(seat, piece, held)
+
+
 def swap(pieces, parts):
     moved = [pieces[0]]
     for step in range(1, parts):
@@ -522,11 +553,15 @@
             costate, opened, parts, size, 1, chunks - 1, list(state_cut[0][:1])
         )
     rho = [
-        cut_pieces(density, seats, parts, chunk, size, list(state_cut[-1][:1]))
+        cut_pieces(density, seats, parts, chunk, size, list(state_cut[-1][:1]) if chunk else [])
         for chunk in range(chunks)
     ]
+    rho_there = [swap(pieces, parts) for pieces in rho]
+    ahead = parts // 2
+    state_cut[0], rho_there[0][ahead] = lax.optimization_barrier(
+        (state_cut[0], rho_there[0][ahead])
+    )
     state = [swap(pieces, parts) for pieces in state_cut[:3]]
-    rho_there = [swap(pieces, parts) for pieces in rho]
 
     shape = (2, rows // WIDE, parts, chunks, size, cols)
     fields, closed, made, grads = [], [], [], []
@@ -542,7 +577,8 @@
             out, rho_there[-1] = lax.optimization_barrier((out, rho_there[-1]))
         if chunk == chunks - 1 and chunk > 1:
             out, made[-1] = lax.optimization_barrier((out, made[-1]))
-        made.append(swap(out, parts))
+        if chunk > 0 or chunks < 4:
+            made.append(swap(out, parts))
         grads.append(grad)
 
     for chunk in range(chunks):
@@ -556,13 +592,19 @@
         if chunk + 1 == len(state) < chunks:
             pieces, field = lax.optimization_barrier((state_cut[chunk + 1], field))
             state.append(swap(pieces, parts))
+            out, state[-1] = lax.optimization_barrier((closed[0], state[-1]))
+            made.append(swap(out, parts))
         fields.append(lax.all_to_all(field, "dev", split_axis=0, concat_axis=0, tiled=True))
     whole = None
     for chunk in range(chunks):
         while len(made) < min(chunk + 2, chunks):
             waited = list(made[-2][1:]) if len(made) > 1 else []
             close(len(made), [whole] if 0 < chunk == chunks - 2 else waited)
-        whole = place_pieces(made[chunk], seats, whole, chunk, shape, size)
+        if chunk < chunks - 1 or whole is None:
+            whole = place_pieces(made[chunk], seats, whole, chunk, shape, size)
+        else:
+            for step in range(parts):
+                whole = place_one(made[chunk][step], seats, whole, chunk, step, shape, size)
     grad = grand_total(device_grad(grads, seats, parts, []))
     return whole.reshape(costate.shape), grad.reshape(2, 2, LEVELS)
 

time: 598 us -> 624 us (1.043)
  Pallas kernels: 196 us -> 210 us
  waiting for transfers between devices: 330 us -> 338 us
    pallas_call x0 -> x4, Pallas kernels: none -> 20.7 us  [place_one(): pl.pallas_call(functools.partial(place_one_kernel, size), grid_spec=pltpu...]
    ppermute x36, waiting for transfers between devices: 239 us -> 252 us  [swap(): moved.append(lax.ppermute(pieces[step], 'grp', pairs))]
    pallas_call x4 -> x3, Pallas kernels: 26.5 us -> 19.8 us  [place_pieces(): pl.pallas_call(functools.partial(place_kernel, parts, size, aliased), gri...]
  transfers between devices with their start and end apart: 45 -> 45, of which waited for: 24 -> 25; matrix products, arithmetic and copies ran while one was open for 0% -> 0% of each run, Pallas kernels for 28% -> 31%
where the time goes in v1:
time: 624 us; the launch traced here: 621 us
  waiting for transfers between devices  338 us (54%)
  Pallas kernels  210 us (34%)
  starting transfers between devices  64.6 us (10%)
    ppermute x36, waiting for transfers between devices, swap(): moved.append(lax.ppermute(pieces[step], 'grp', pairs))  252 us
    pallas_call x4, Pallas kernels, close_columns(): pl.pallas_call(functools.partial(close_kernel, parts, size), grid=(firsts...  71 us
    all_to_all x4, waiting for transfers between devices, per_device(): lax.all_to_all(field, 'dev', split_axis=0, concat_axis=0, tiled=True)  63.4 us
    pallas_call x4, Pallas kernels, turn_columns(): pl.pallas_call(functools.partial(turn_kernel, parts, size), grid=(firsts,...  33.4 us
    ppermute x36, starting transfers between devices, swap(): moved.append(lax.ppermute(pieces[step], 'grp', pairs))  33.2 us
    pallas_call x4, Pallas kernels, cut_pieces(): pl.pallas_call(functools.partial(cut_kernel, size, len(waited)), grid=(fi...  26.6 us
    ppermute x5, waiting for transfers between devices, grand_total(): value = value + lax.ppermute(value, axis, pairs)  22 us
    all_to_all x4, starting transfers between devices, per_device(): lax.all_to_all(field, 'dev', split_axis=0, concat_axis=0, tiled=True)  22 us
  transfers between devices with their start and end apart: 45, of which 25 were waited for; matrix products, arithmetic and copies ran while one was open for 0% of the time, Pallas kernels for 31%

profile of v1, /device:TPU:0, one launch (start us, length us, event | category | flops | bytes accessed | tf_op | source)
XLA Modules:
  0.0 621.1 jit_solution(15549789417817724636)
XLA Ops:
  0.6 6.6 %shard_map.79 = (f32[8,256,128]{2,1,0:T(8,128)}, f32[8,256,128]{2,1,0:T(8,128)}, f32[8,256,128]{2,1,0:T(8,128)}, f32[8,256,128]{2,1,0:T(8,128)}) custom-call(s32[1]{0:T(128)} %bitcast.seat_ref, f32[2,8,4,4,8,2048]{5,4,3,2,1,0:T(8,128)} %bitcast.9), custom_call_target="tpu_custom_call" | custom-call | flops 1024 | bytes 1024 | tf_op jit(solution)/shard_map/pallas_call | solution.py:263
  7.3 2.9 collective-permute-start
  10.9 4.6 shard_map.77
  15.4 12.3 %shard_map.78 = (f32[8,256,128]{2,1,0:T(8,128)}, f32[8,256,128]{2,1,0:T(8,128)}, f32[8,256,128]{2,1,0:T(8,128)}, f32[8,256,128]{2,1,0:T(8,128)}) custom-call(bf16[512,128]{1,0:T(8,128)(2,1)} %get-tuple-element.96.weight_ref, f32[2,1024,2048]{2,1,0:T(8,128)} %field_ref.3), custom_call_target="tpu_custom_call" | custom-call | flops 1024 | bytes 1024 | tf_op jit(solution)/shard_map/pallas_call | solution.py:204
  27.7 5.9 collective-permute-done.refs_2_
  37.5 23.3 %collective-permute-done.2.refs_2_ = f32[8,256,128]{2,1,0:T(8,128)S(1)} collective-permute-done((f32[8,256,128]{2,1,0:T(8,128)}, f32[8,256,128]{2,1,0:T(8,128)S(1)}, u32[]{:S(2)}, u32[]{:S(2)}) %collective-permute-start.2) | collective-permute-done | bytes 1048608 | tf_op jit(solution)/shard_map/ppermute | solution.py:490
  60.8 21.7 %collective-permute-done.3.refs_3_ = f32[8,256,128]{2,1,0:T(8,128)S(1)} collective-permute-done((f32[8,256,128]{2,1,0:T(8,128)}, f32[8,256,128]{2,1,0:T(8,128)S(1)}, u32[]{:S(2)}, u32[]{:S(2)}) %collective-permute-start.3) | collective-permute-done | bytes 1048608 | tf_op jit(solution)/shard_map/ppermute | solution.py:490
  83.5 8.3 %shard_map.80.refs_5_ = f32[64,8,16,128]{3,2,1,0:T(8,128)} custom-call(bf16[256,256]{1,0:T(8,128)(2,1)} %get-tuple-element.95.weight_ref, f32[8,256,128]{2,1,0:T(8,128)} %get-tuple-element.102.refs_0_, f32[8,256,128]{2,1,0:T(8,128)} %copy-done.7, f32[8,256,128]{2,1,0:T(8,128)} %copy-done.8, f32[8,256,128]{2,1,0:T(8,128)} %copy-done.9, ...), custom_call_target="tpu_custom_call" | custom-call | flops 1024 | bytes 1024 | tf_op jit(solution)/shard_map/pallas_call | solution.py:326
  91.8 6.1 all-to-all-start
  98.6 19.5 %shard_map.82 = (f32[8,256,128]{2,1,0:T(8,128)}, f32[8,256,128]{2,1,0:T(8,128)}, f32[8,256,128]{2,1,0:T(8,128)}, f32[8,256,128]{2,1,0:T(8,128)}, f32[8,256,128]{...) custom-call(bf16[2,192,256]{2,1,0:T(8,128)(2,1)} %slice.3.weight_ref, ...), custom_call_target="tpu_custom_call" | custom-call | flops 1024 | bytes 1024 | tf_op jit(solution)/shard_map/pallas_call | solution.py:229
  122.0 6.6 %shard_map.84 = (f32[8,256,128]{2,1,0:T(8,128)}, f32[8,256,128]{2,1,0:T(8,128)}, f32[8,256,128]{2,1,0:T(8,128)}, f32[8,256,128]{2,1,0:T(8,128)}) custom-call(s32[1]{0:T(128)} %bitcast.seat_ref, f32[2,8,4,4,8,2048]{5,4,3,2,1,0:T(8,128)} %bitcast.10, f32[8,256,128]{2,1,0:T(8,128)} %get-tuple-element.133.refs_0_), custom_call_target="tpu_custom_call" | custom-call | flops 1024 | bytes 1024 | tf_op jit(solution)/shard_map/pallas_call | solution.py:263
  128.6 6.6 %shard_map.83 = (f32[8,256,128]{2,1,0:T(8,128)}, f32[8,256,128]{2,1,0:T(8,128)}, f32[8,256,128]{2,1,0:T(8,128)}, f32[8,256,128]{2,1,0:T(8,128)}) custom-call(s32[1]{0:T(128)} %bitcast.seat_ref, f32[2,8,4,4,8,2048]{5,4,3,2,1,0:T(8,128)} %bitcast.11, f32[8,256,128]{2,1,0:T(8,128)} %get-tuple-element.133.refs_0_), custom_call_target="tpu_custom_call" | custom-call | flops 1024 | bytes 1024 | tf_op jit(solution)/shard_map/pallas_call | solution.py:263
  135.2 9.2 %collective-permute-done.10.refs_2_ = f32[8,256,128]{2,1,0:T(8,128)S(1)} collective-permute-done((f32[8,256,128]{2,1,0:T(8,128)}, f32[8,256,128]{2,1,0:T(8,128)S(1)}, u32[]{:S(2)}, u32[]{:S(2)}) %collective-permute-start.10) | collective-permute-done | bytes 1048608 | tf_op jit(solution)/shard_map/ppermute | solution.py:490
  145.9 20.1 %collective-permute-done.11.refs_3_ = f32[8,256,128]{2,1,0:T(8,128)S(1)} collective-permute-done((f32[8,256,128]{2,1,0:T(8,128)}, f32[8,256,128]{2,1,0:T(8,128)S(1)}, u32[]{:S(2)}, u32[]{:S(2)}) %collective-permute-start.11) | collective-permute-done | bytes 1048608 | tf_op jit(solution)/shard_map/ppermute | solution.py:490
  168.2 8.4 %shard_map.85.refs_5_ = f32[64,8,16,128]{3,2,1,0:T(8,128)} custom-call(bf16[256,256]{1,0:T(8,128)(2,1)} %get-tuple-element.95.weight_ref, f32[8,256,128]{2,1,0:T(8,128)} %get-tuple-element.124.refs_0_, f32[8,256,128]{2,1,0:T(8,128)} %copy-done.10, f32[8,256,128]{2,1,0:T(8,128)} %copy-done.11, f32[8,256,128]{2,1,0:T(8,128)} %copy-done.12, ...), custom_call_target="tpu_custom_call" | custom-call | flops 1024 | bytes 1024 | tf_op jit(solution)/shard_map/pallas_call | solution.py:326
  176.6 12.0 %collective-permute-done.5.refs_3_ = f32[8,256,128]{2,1,0:T(8,128)} collective-permute-done((f32[8,256,128]{2,1,0:T(8,128)}, f32[8,256,128]{2,1,0:T(8,128)}, u32[]{:S(2)}, u32[]{:S(2)}) %collective-permute-start.5) | collective-permute-done | bytes 1048608 | tf_op jit(solution)/shard_map/ppermute | solution.py:490
  191.5 5.1 all-to-all-start.1
  196.6 17.7 %shard_map.81 = (f32[8,256,128]{2,1,0:T(8,128)}, f32[8,256,128]{2,1,0:T(8,128)}, f32[8,256,128]{2,1,0:T(8,128)}, f32[8,256,128]{2,1,0:T(8,128)}, f32[2,64,128]{2,1,0:T(8,128)}) custom-call(bf16[3,2,256,256]{3,2,1,0:T(8,128)(2,1)} %get-tuple-element.93.lane_ref, bf16[3,256,256]{2,1,0:T(8,128)(2,1)} %get-tuple-element.94.level_ref, ...), custom_call_target="tpu_custom_call" | custom-call | flops 199999995904 | bytes 1024 | tf_op jit(solution)/shard_map/pallas_call | solution.py:398
  214.4 19.1 %collective-permute-done.8.refs_3_ = f32[8,256,128]{2,1,0:T(8,128)} collective-permute-done((f32[8,256,128]{2,1,0:T(8,128)}, f32[8,256,128]{2,1,0:T(8,128)}, u32[]{:S(2)}, u32[]{:S(2)}) %collective-permute-start.8) | collective-permute-done | bytes 1048608 | tf_op jit(solution)/shard_map/ppermute | solution.py:490
  233.5 8.4 %shard_map.86.refs_5_ = f32[64,8,16,128]{3,2,1,0:T(8,128)} custom-call(bf16[256,256]{1,0:T(8,128)(2,1)} %get-tuple-element.95.weight_ref, f32[8,256,128]{2,1,0:T(8,128)} %get-tuple-element.119.refs_0_, f32[8,256,128]{2,1,0:T(8,128)} %collective-permute-done.6.refs_1_, f32[8,256,128]{2,1,0:T(8,128)} %collective-permute-done.7.refs_2_, ...), custom_call_target="tpu_custom_call" | custom-call | flops 1024 | bytes 1024 | tf_op jit(solution)/shard_map/pallas_call | solution.py:326
  244.3 45.8 %all-to-all-done.1 = f32[64,8,16,128]{3,2,1,0:T(8,128)} async-done(((f32[64,8,16,128]{3,2,1,0:T(8,128)}), f32[64,8,16,128]{3,2,1,0:T(8,128)}, u32[]{:S(2)}, u32[]{:S(2)}) %all-to-all-start.1) | async-done | bytes 4194336 | tf_op jit(solution)/shard_map/all_to_all | solution.py:597
  290.1 4.8 all-to-all-start.3
  295.0 17.8 %shard_map.88 = (f32[8,256,128]{2,1,0:T(8,128)}, f32[8,256,128]{2,1,0:T(8,128)}, f32[8,256,128]{2,1,0:T(8,128)}, f32[8,256,128]{2,1,0:T(8,128)}, f32[2,64,128]{2,1,0:T(8,128)}) custom-call(bf16[3,2,256,256]{3,2,1,0:T(8,128)(2,1)} %get-tuple-element.93.lane_ref, bf16[3,256,256]{2,1,0:T(8,128)(2,1)} %get-tuple-element.94.level_ref, ...), custom_call_target="tpu_custom_call" | custom-call | flops 199999995904 | bytes 1024 | tf_op jit(solution)/shard_map/pallas_call | solution.py:398
  314.4 8.9 %collective-permute-done.14.refs_3_ = f32[8,256,128]{2,1,0:T(8,128)} collective-permute-done((f32[8,256,128]{2,1,0:T(8,128)}, f32[8,256,128]{2,1,0:T(8,128)}, u32[]{:S(2)}, u32[]{:S(2)}) %collective-permute-start.14) | collective-permute-done | bytes 1048608 | tf_op jit(solution)/shard_map/ppermute | solution.py:490
  327.6 22.6 %collective-permute-done.22.refs_5_.refs_2_ = f32[8,256,128]{2,1,0:T(8,128)S(1)} collective-permute-done((f32[8,256,128]{2,1,0:T(8,128)}, f32[8,256,128]{2,1,0:T(8,128)S(1)}, u32[]{:S(2)}, u32[]{:S(2)}) %collective-permute-start.22) | collective-permute-done | bytes 1048608 | tf_op jit(solution)/shard_map/ppermute | solution.py:490
  351.6 20.1 %collective-permute-done.23.refs_6_.refs_3_ = f32[8,256,128]{2,1,0:T(8,128)S(1)} collective-permute-done((f32[8,256,128]{2,1,0:T(8,128)}, f32[8,256,128]{2,1,0:T(8,128)S(1)}, u32[]{:S(2)}, u32[]{:S(2)}) %collective-permute-start.23) | collective-permute-done | bytes 1048608 | tf_op jit(solution)/shard_map/ppermute | solution.py:490
  373.5 6.7 %shard_map.87 = (f32[8,256,128]{2,1,0:T(8,128)}, f32[8,256,128]{2,1,0:T(8,128)}, f32[8,256,128]{2,1,0:T(8,128)}, f32[8,256,128]{2,1,0:T(8,128)}) custom-call(s32[1]{0:T(128)} %bitcast.seat_ref, f32[2,8,4,4,8,2048]{5,4,3,2,1,0:T(8,128)} %bitcast.12, f32[8,256,128]{2,1,0:T(8,128)} %get-tuple-element.133.refs_0_), custom_call_target="tpu_custom_call" | custom-call | flops 1024 | bytes 1024 | tf_op jit(solution)/shard_map/pallas_call | solution.py:263
  380.2 8.4 %shard_map.89 = f32[64,8,16,128]{3,2,1,0:T(8,128)} custom-call(bf16[256,256]{1,0:T(8,128)(2,1)} %get-tuple-element.95.weight_ref, f32[8,256,128]{2,1,0:T(8,128)} %get-tuple-element.133.refs_0_, f32[8,256,128]{2,1,0:T(8,128)} %collective-permute-done.12.refs_1_, f32[8,256,128]{2,1,0:T(8,128)} %collective-permute-done.13.refs_2_, ...), custom_call_target="tpu_custom_call" | custom-call | flops 1024 | bytes 1024 | tf_op jit(solution)/shard_map/pallas_call | solution.py:326
  388.6 6.6 %shard_map.91.refs_4_ = f32[2,8,4,4,8,2048]{5,4,3,2,1,0:T(8,128)} custom-call(s32[1]{0:T(128)} %bitcast.seat_ref, f32[8,256,128]{2,1,0:T(8,128)} %get-tuple-element.163.refs_6_.refs_4_.refs_0_, f32[8,256,128]{2,1,0:T(8,128)} %copy-done, f32[8,256,128]{2,1,0:T(8,128)} %copy-done.1, f32[8,256,128]{2,1,0:T(8,128)} %copy-done.2), custom_call_target="tpu_custom_call" | custom-call | flops 1024 | bytes 1024 | tf_op jit(solution)/shard_map/pallas_call | solution.py:439
  395.3 21.4 %collective-permute-done.29.refs_3_ = f32[8,256,128]{2,1,0:T(8,128)} collective-permute-done((f32[8,256,128]{2,1,0:T(8,128)}, f32[8,256,128]{2,1,0:T(8,128)}, u32[]{:S(2)}, u32[]{:S(2)}) %collective-permute-start.29) | collective-permute-done | bytes 1048608 | tf_op jit(solution)/shard_map/ppermute | solution.py:490
  417.2 6.6 %shard_map.92.refs_4_ = f32[2,8,4,4,8,2048]{5,4,3,2,1,0:T(8,128)} custom-call(s32[1]{0:T(128)} %bitcast.seat_ref, f32[8,256,128]{2,1,0:T(8,128)} %get-tuple-element.142.refs_6_.refs_7_.refs_0_, f32[8,256,128]{2,1,0:T(8,128)} %copy-done.3, f32[8,256,128]{2,1,0:T(8,128)} %collective-permute-done.28.refs_2_, ...), custom_call_target="tpu_custom_call", output_to_operand_aliasing={{}: (5, {})} | custom-call | flops 1024 | bytes 1024 | tf_op jit(solution)/shard_map/pallas_call | solution.py:439
  425.5 6.0 all-to-all-start.2
  431.5 8.7 %collective-permute-done.19.refs_2_ = f32[8,256,128]{2,1,0:T(8,128)} collective-permute-done((f32[8,256,128]{2,1,0:T(8,128)}, f32[8,256,128]{2,1,0:T(8,128)}, u32[]{:S(2)}, u32[]{:S(2)}) %collective-permute-start.19) | collective-permute-done | bytes 1048608 | tf_op jit(solution)/shard_map/ppermute | solution.py:490
  440.1 21.5 %collective-permute-done.20.refs_3_ = f32[8,256,128]{2,1,0:T(8,128)} collective-permute-done((f32[8,256,128]{2,1,0:T(8,128)}, f32[8,256,128]{2,1,0:T(8,128)}, u32[]{:S(2)}, u32[]{:S(2)}) %collective-permute-start.20) | collective-permute-done | bytes 1048608 | tf_op jit(solution)/shard_map/ppermute | solution.py:490
  461.6 17.8 %shard_map.90 = (f32[8,256,128]{2,1,0:T(8,128)}, f32[8,256,128]{2,1,0:T(8,128)}, f32[8,256,128]{2,1,0:T(8,128)}, f32[8,256,128]{2,1,0:T(8,128)}, f32[2,64,128]{2,1,0:T(8,128)}) custom-call(bf16[3,2,256,256]{3,2,1,0:T(8,128)(2,1)} %get-tuple-element.93.lane_ref, bf16[3,256,256]{2,1,0:T(8,128)(2,1)} %get-tuple-element.94.level_ref, ...), custom_call_target="tpu_custom_call" | custom-call | flops 199999995904 | bytes 1024 | tf_op jit(solution)/shard_map/pallas_call | solution.py:398
  479.4 5.7 collective-permute-done.25.refs_2_
  485.1 20.5 %collective-permute-done.26.refs_3_ = f32[8,256,128]{2,1,0:T(8,128)} collective-permute-done((f32[8,256,128]{2,1,0:T(8,128)}, f32[8,256,128]{2,1,0:T(8,128)}, u32[]{:S(2)}, u32[]{:S(2)}) %collective-permute-start.26) | collective-permute-done | bytes 1048608 | tf_op jit(solution)/shard_map/ppermute | solution.py:490
  507.9 17.0 %all-to-all-done.2 = f32[64,8,16,128]{3,2,1,0:T(8,128)} async-done(((f32[64,8,16,128]{3,2,1,0:T(8,128)}), f32[64,8,16,128]{3,2,1,0:T(8,128)}, u32[]{:S(2)}, u32[]{:S(2)}) %all-to-all-start.2) | async-done | bytes 4194336 | tf_op jit(solution)/shard_map/all_to_all | solution.py:597
  524.9 17.7 %shard_map.93 = (f32[8,256,128]{2,1,0:T(8,128)}, f32[8,256,128]{2,1,0:T(8,128)}, f32[8,256,128]{2,1,0:T(8,128)}, f32[8,256,128]{2,1,0:T(8,128)}, f32[2,64,128]{2,1,0:T(8,128)}) custom-call(bf16[3,2,256,256]{3,2,1,0:T(8,128)(2,1)} %get-tuple-element.93.lane_ref, bf16[3,256,256]{2,1,0:T(8,128)(2,1)} %get-tuple-element.94.level_ref, ...), custom_call_target="tpu_custom_call" | custom-call | flops 199999995904 | bytes 1024 | tf_op jit(solution)/shard_map/pallas_call | solution.py:398
  542.6 10.7 %collective-permute-done.32.refs_3_ = f32[8,256,128]{2,1,0:T(8,128)} collective-permute-done((f32[8,256,128]{2,1,0:T(8,128)}, f32[8,256,128]{2,1,0:T(8,128)}, u32[]{:S(2)}, u32[]{:S(2)}) %collective-permute-start.32) | collective-permute-done | bytes 1048608 | tf_op jit(solution)/shard_map/ppermute | solution.py:490
  555.6 2.4 shard_map.99
  567.8 2.9 collective-permute-start.39
  573.8 6.6 %shard_map.94.held_ref = f32[2,8,4,4,8,2048]{5,4,3,2,1,0:T(8,128)} custom-call(s32[1]{0:T(128)} %bitcast.seat_ref, f32[8,256,128]{2,1,0:T(8,128)} %get-tuple-element.176.refs_5_.refs_0_, f32[8,256,128]{2,1,0:T(8,128)} %collective-permute-done.30.refs_1_, f32[8,256,128]{2,1,0:T(8,128)} %collective-permute-done.31.refs_2_, ...), custom_call_target="tpu_custom_call", output_to_operand_aliasing={{}: (5, {})} | custom-call | flops 1024 | bytes 1024 | tf_op jit(solution)/shard_map/pallas_call | solution.py:439
  580.4 5.2 shard_map.95.held_ref
  585.6 16.3 %collective-permute-done.40 = f32[4,64]{1,0:T(4,128)S(1)} collective-permute-done((f32[4,64]{1,0:T(4,128)S(1)}, f32[4,64]{1,0:T(4,128)S(1)}, u32[]{:S(2)}, u32[]{:S(2)}) %collective-permute-start.40) | collective-permute-done | bytes 1056 | tf_op jit(solution)/shard_map/ppermute | solution.py:534
  603.5 5.2 shard_map.96.held_ref
  609.7 5.2 shard_map.97.held_ref
  615.9 5.2 shard_map.98
  (101 shorter events, 51.3 us)
Async XLA Ops:
  7.3 26.3 %collective-permute-start = (f32[8,256,128]{2,1,0:T(8,128)}, f32[8,256,128]{2,1,0:T(8,128)S(1)}, u32[]{:S(2)}, u32[]{:S(2)}) collective-permute-start(f32[8,256,128]{2,1,0:T(8,128)} %get-tuple-element.101), channel_id=1, source_target_pairs={{0,16},{8,24},{16,0},{24,8},{1,17},{9,25},{17,1},{25,9},{2,18},{10... | collective-permute-start | bytes 3145736 | tf_op jit(solution)/shard_map/ppermute | solution.py:490
  15.4 82.4 %copy-start.13 = (bf16[2,256,256]{2,1,0:T(8,128)(2,1)S(1)}, bf16[2,256,256]{2,1,0:T(8,128)(2,1)}, u32[]{:S(2)}) copy-start(bf16[2,256,256]{2,1,0:T(8,128)(2,1)} %get-tuple-element.114) | copy-start | bytes 786436
  34.6 2.9 collective-permute-start.1
  34.6 26.2 %collective-permute-start.2 = (f32[8,256,128]{2,1,0:T(8,128)}, f32[8,256,128]{2,1,0:T(8,128)S(1)}, u32[]{:S(2)}, u32[]{:S(2)}) collective-permute-start(f32[8,256,128]{2,1,0:T(8,128)} %get-tuple-element.104), channel_id=1, source_target_pairs={{0,16},{8,24},{16,0},{24,8},{1,17},{9,25},{17,1},{25,9},{2,18},{10... | collective-permute-start | bytes 3145736 | tf_op jit(solution)/shard_map/ppermute | solution.py:490
  36.4 46.1 %collective-permute-start.3 = (f32[8,256,128]{2,1,0:T(8,128)}, f32[8,256,128]{2,1,0:T(8,128)S(1)}, u32[]{:S(2)}, u32[]{:S(2)}) collective-permute-start(f32[8,256,128]{2,1,0:T(8,128)} %get-tuple-element.105), channel_id=1, source_target_pairs={{0,24},{8,16},{16,8},{24,0},{1,25},{9,17},{17,9},{25,1},{2,26},{10... | collective-permute-start | bytes 3145736 | tf_op jit(solution)/shard_map/ppermute | solution.py:490
  37.5 45.0 %copy-start.7 = (f32[8,256,128]{2,1,0:T(8,128)}, f32[8,256,128]{2,1,0:T(8,128)S(1)}, u32[]{:S(2)}) copy-start(f32[8,256,128]{2,1,0:T(8,128)S(1)} %collective-permute-done.1.refs_1_) | copy-start | bytes 3145732
  91.8 99.7 %all-to-all-start = ((f32[64,8,16,128]{3,2,1,0:T(8,128)}), f32[64,8,16,128]{3,2,1,0:T(8,128)}, u32[]{:S(2)}, u32[]{:S(2)}) async-start(f32[64,8,16,128]{3,2,1,0:T(8,128)} %shard_map.80.refs_5_), calls=%async_computation | async-start | bytes 8388608 | tf_op jit(solution)/shard_map/all_to_all | solution.py:597
  118.1 3.5 collective-permute-start.9
  118.1 26.2 %collective-permute-start.10 = (f32[8,256,128]{2,1,0:T(8,128)}, f32[8,256,128]{2,1,0:T(8,128)S(1)}, u32[]{:S(2)}, u32[]{:S(2)}) collective-permute-start(f32[8,256,128]{2,1,0:T(8,128)} %get-tuple-element.126), channel_id=1, source_target_pairs={{0,16},{8,24},{16,0},{24,8},{1,17},{9,25},{17,1},{25,9},{2,18},{10... | collective-permute-start | bytes 3145736 | tf_op jit(solution)/shard_map/ppermute | solution.py:490
  119.7 46.3 %collective-permute-start.11 = (f32[8,256,128]{2,1,0:T(8,128)}, f32[8,256,128]{2,1,0:T(8,128)S(1)}, u32[]{:S(2)}, u32[]{:S(2)}) collective-permute-start(f32[8,256,128]{2,1,0:T(8,128)} %get-tuple-element.127), channel_id=1, source_target_pairs={{0,24},{8,16},{16,8},{24,0},{1,25},{9,17},{17,9},{25,1},{2,26},{10... | collective-permute-start | bytes 3145736 | tf_op jit(solution)/shard_map/ppermute | solution.py:490
  120.0 56.6 %collective-permute-start.4 = (f32[8,256,128]{2,1,0:T(8,128)}, f32[8,256,128]{2,1,0:T(8,128)}, u32[]{:S(2)}, u32[]{:S(2)}) collective-permute-start(f32[8,256,128]{2,1,0:T(8,128)} %get-tuple-element.107), channel_id=1, source_target_pairs={{0,8},{8,0},{16,24},{24,16},{1,9},{9,1},{17,25},{25,17},{2,10},{10... | collective-permute-start | bytes 3145736 | tf_op jit(solution)/shard_map/ppermute | solution.py:490
  120.4 68.2 %collective-permute-start.5 = (f32[8,256,128]{2,1,0:T(8,128)}, f32[8,256,128]{2,1,0:T(8,128)}, u32[]{:S(2)}, u32[]{:S(2)}) collective-permute-start(f32[8,256,128]{2,1,0:T(8,128)} %get-tuple-element.109), channel_id=1, source_target_pairs={{0,24},{8,16},{16,8},{24,0},{1,25},{9,17},{17,9},{25,1},{2,26},{10... | collective-permute-start | bytes 3145736 | tf_op jit(solution)/shard_map/ppermute | solution.py:490
  121.6 68.4 %collective-permute-start.6 = (f32[8,256,128]{2,1,0:T(8,128)}, f32[8,256,128]{2,1,0:T(8,128)}, u32[]{:S(2)}, u32[]{:S(2)}) collective-permute-start(f32[8,256,128]{2,1,0:T(8,128)} %get-tuple-element.120), channel_id=1, source_target_pairs={{0,8},{8,0},{16,24},{24,16},{1,9},{9,1},{17,25},{25,17},{2,10},{10... | collective-permute-start | bytes 3145736 | tf_op jit(solution)/shard_map/ppermute | solution.py:490
  144.4 70.0 %collective-permute-start.7 = (f32[8,256,128]{2,1,0:T(8,128)}, f32[8,256,128]{2,1,0:T(8,128)}, u32[]{:S(2)}, u32[]{:S(2)}) collective-permute-start(f32[8,256,128]{2,1,0:T(8,128)} %get-tuple-element.121), channel_id=1, source_target_pairs={{0,16},{8,24},{16,0},{24,8},{1,17},{9,25},{17,1},{25,9},{2,18},{10... | collective-permute-start | bytes 3145736 | tf_op jit(solution)/shard_map/ppermute | solution.py:490
  166.0 67.5 %collective-permute-start.8 = (f32[8,256,128]{2,1,0:T(8,128)}, f32[8,256,128]{2,1,0:T(8,128)}, u32[]{:S(2)}, u32[]{:S(2)}) collective-permute-start(f32[8,256,128]{2,1,0:T(8,128)} %get-tuple-element.122), channel_id=1, source_target_pairs={{0,24},{8,16},{16,8},{24,0},{1,25},{9,17},{17,9},{25,1},{2,26},{10... | collective-permute-start | bytes 3145736 | tf_op jit(solution)/shard_map/ppermute | solution.py:490
  176.6 118.3 %collective-permute-start.15 = (f32[8,256,128]{2,1,0:T(8,128)}, f32[8,256,128]{2,1,0:T(8,128)}, u32[]{:S(2)}, u32[]{:S(2)}) collective-permute-start(f32[8,256,128]{2,1,0:T(8,128)} %get-tuple-element.139), channel_id=1, source_target_pairs={{0,8},{8,0},{16,24},{24,16},{1,9},{9,1},{17,25},{25,17},{2,10},{10... | collective-permute-start | bytes 3145736 | tf_op jit(solution)/shard_map/ppermute | solution.py:490
  188.5 106.5 %collective-permute-start.16 = (f32[8,256,128]{2,1,0:T(8,128)}, f32[8,256,128]{2,1,0:T(8,128)}, u32[]{:S(2)}, u32[]{:S(2)}) collective-permute-start(f32[8,256,128]{2,1,0:T(8,128)} %get-tuple-element.140), channel_id=1, source_target_pairs={{0,16},{8,24},{16,0},{24,8},{1,17},{9,25},{17,1},{25,9},{2,18},{10... | collective-permute-start | bytes 3145736 | tf_op jit(solution)/shard_map/ppermute | solution.py:490
  190.0 105.0 %collective-permute-start.17 = (f32[8,256,128]{2,1,0:T(8,128)}, f32[8,256,128]{2,1,0:T(8,128)}, u32[]{:S(2)}, u32[]{:S(2)}) collective-permute-start(f32[8,256,128]{2,1,0:T(8,128)} %get-tuple-element.141), channel_id=1, source_target_pairs={{0,24},{8,16},{16,8},{24,0},{1,25},{9,17},{17,9},{25,1},{2,26},{10... | collective-permute-start | bytes 3145736 | tf_op jit(solution)/shard_map/ppermute | solution.py:490
  191.5 98.6 %all-to-all-start.1 = ((f32[64,8,16,128]{3,2,1,0:T(8,128)}), f32[64,8,16,128]{3,2,1,0:T(8,128)}, u32[]{:S(2)}, u32[]{:S(2)}) async-start(f32[64,8,16,128]{3,2,1,0:T(8,128)} %shard_map.85.refs_5_), calls=%async_computation.1 | async-start | bytes 8388608 | tf_op jit(solution)/shard_map/all_to_all | solution.py:597
  241.8 72.6 %collective-permute-start.12 = (f32[8,256,128]{2,1,0:T(8,128)}, f32[8,256,128]{2,1,0:T(8,128)}, u32[]{:S(2)}, u32[]{:S(2)}) collective-permute-start(f32[8,256,128]{2,1,0:T(8,128)} %get-tuple-element.130), channel_id=1, source_target_pairs={{0,8},{8,0},{16,24},{24,16},{1,9},{9,1},{17,25},{25,17},{2,10},{10... | collective-permute-start | bytes 3145736 | tf_op jit(solution)/shard_map/ppermute | solution.py:490
  242.8 71.6 %collective-permute-start.13 = (f32[8,256,128]{2,1,0:T(8,128)}, f32[8,256,128]{2,1,0:T(8,128)}, u32[]{:S(2)}, u32[]{:S(2)}) collective-permute-start(f32[8,256,128]{2,1,0:T(8,128)} %get-tuple-element.131), channel_id=1, source_target_pairs={{0,16},{8,24},{16,0},{24,8},{1,17},{9,25},{17,1},{25,9},{2,18},{10... | collective-permute-start | bytes 3145736 | tf_op jit(solution)/shard_map/ppermute | solution.py:490
  290.1 135.4 %all-to-all-start.3 = ((f32[64,8,16,128]{3,2,1,0:T(8,128)}), f32[64,8,16,128]{3,2,1,0:T(8,128)}, u32[]{:S(2)}, u32[]{:S(2)}) async-start(f32[64,8,16,128]{3,2,1,0:T(8,128)} %shard_map.86.refs_5_), calls=%async_computation.3 | async-start | bytes 8388608 | tf_op jit(solution)/shard_map/all_to_all | solution.py:597
  294.9 28.4 %collective-permute-start.14 = (f32[8,256,128]{2,1,0:T(8,128)}, f32[8,256,128]{2,1,0:T(8,128)}, u32[]{:S(2)}, u32[]{:S(2)}) collective-permute-start(f32[8,256,128]{2,1,0:T(8,128)} %get-tuple-element.132), channel_id=1, source_target_pairs={{0,24},{8,16},{16,8},{24,0},{1,25},{9,17},{17,9},{25,1},{2,26},{10... | collective-permute-start | bytes 3145736 | tf_op jit(solution)/shard_map/ppermute | solution.py:490
  312.8 14.0 %collective-permute-start.27 = (f32[8,256,128]{2,1,0:T(8,128)}, f32[8,256,128]{2,1,0:T(8,128)S(1)}, u32[]{:S(2)}, u32[]{:S(2)}) collective-permute-start(f32[8,256,128]{2,1,0:T(8,128)} %get-tuple-element.160), channel_id=1, source_target_pairs={{0,8},{8,0},{16,24},{24,16},{1,9},{9,1},{17,25},{25,17},{2,10},{10... | collective-permute-start | bytes 3145736 | tf_op jit(solution)/shard_map/ppermute | solution.py:490
  323.3 4.1 collective-permute-start.21
  323.9 26.2 %collective-permute-start.22 = (f32[8,256,128]{2,1,0:T(8,128)}, f32[8,256,128]{2,1,0:T(8,128)S(1)}, u32[]{:S(2)}, u32[]{:S(2)}) collective-permute-start(f32[8,256,128]{2,1,0:T(8,128)} %get-tuple-element.147), channel_id=1, source_target_pairs={{0,16},{8,24},{16,0},{24,8},{1,17},{9,25},{17,1},{25,9},{2,18},{10... | collective-permute-start | bytes 3145736 | tf_op jit(solution)/shard_map/ppermute | solution.py:490
  325.4 46.3 %collective-permute-start.23 = (f32[8,256,128]{2,1,0:T(8,128)}, f32[8,256,128]{2,1,0:T(8,128)S(1)}, u32[]{:S(2)}, u32[]{:S(2)}) collective-permute-start(f32[8,256,128]{2,1,0:T(8,128)} %get-tuple-element.148), channel_id=1, source_target_pairs={{0,24},{8,16},{16,8},{24,0},{1,25},{9,17},{17,9},{25,1},{2,26},{10... | collective-permute-start | bytes 3145736 | tf_op jit(solution)/shard_map/ppermute | solution.py:490
  325.4 69.8 %collective-permute-start.28 = (f32[8,256,128]{2,1,0:T(8,128)}, f32[8,256,128]{2,1,0:T(8,128)}, u32[]{:S(2)}, u32[]{:S(2)}) collective-permute-start(f32[8,256,128]{2,1,0:T(8,128)} %get-tuple-element.161), channel_id=1, source_target_pairs={{0,16},{8,24},{16,0},{24,8},{1,17},{9,25},{17,1},{25,9},{2,18},{10... | collective-permute-start | bytes 3145736 | tf_op jit(solution)/shard_map/ppermute | solution.py:490
  326.8 89.9 %collective-permute-start.29 = (f32[8,256,128]{2,1,0:T(8,128)}, f32[8,256,128]{2,1,0:T(8,128)}, u32[]{:S(2)}, u32[]{:S(2)}) collective-permute-start(f32[8,256,128]{2,1,0:T(8,128)} %get-tuple-element.162), channel_id=1, source_target_pairs={{0,24},{8,16},{16,8},{24,0},{1,25},{9,17},{17,9},{25,1},{2,26},{10... | collective-permute-start | bytes 3145736 | tf_op jit(solution)/shard_map/ppermute | solution.py:490
  327.4 61.2 %copy-start = (f32[8,256,128]{2,1,0:T(8,128)}, f32[8,256,128]{2,1,0:T(8,128)S(1)}, u32[]{:S(2)}) copy-start(f32[8,256,128]{2,1,0:T(8,128)S(1)} %collective-permute-done.21.refs_4_.refs_1_) | copy-start | bytes 3145732
  327.4 96.4 %collective-permute-start.18 = (f32[8,256,128]{2,1,0:T(8,128)}, f32[8,256,128]{2,1,0:T(8,128)}, u32[]{:S(2)}, u32[]{:S(2)}) collective-permute-start(f32[8,256,128]{2,1,0:T(8,128)} %get-tuple-element.143), channel_id=1, source_target_pairs={{0,8},{8,0},{16,24},{24,16},{1,9},{9,1},{17,25},{25,17},{2,10},{10... | collective-permute-start | bytes 3145736 | tf_op jit(solution)/shard_map/ppermute | solution.py:490
  350.2 90.0 %collective-permute-start.19 = (f32[8,256,128]{2,1,0:T(8,128)}, f32[8,256,128]{2,1,0:T(8,128)}, u32[]{:S(2)}, u32[]{:S(2)}) collective-permute-start(f32[8,256,128]{2,1,0:T(8,128)} %get-tuple-element.144), channel_id=1, source_target_pairs={{0,16},{8,24},{16,0},{24,8},{1,17},{9,25},{17,1},{25,9},{2,18},{10... | collective-permute-start | bytes 3145736 | tf_op jit(solution)/shard_map/ppermute | solution.py:490
  371.7 89.9 %collective-permute-start.20 = (f32[8,256,128]{2,1,0:T(8,128)}, f32[8,256,128]{2,1,0:T(8,128)}, u32[]{:S(2)}, u32[]{:S(2)}) collective-permute-start(f32[8,256,128]{2,1,0:T(8,128)} %get-tuple-element.145), channel_id=1, source_target_pairs={{0,24},{8,16},{16,8},{24,0},{1,25},{9,17},{17,9},{25,1},{2,26},{10... | collective-permute-start | bytes 3145736 | tf_op jit(solution)/shard_map/ppermute | solution.py:490
  395.2 84.1 %collective-permute-start.24 = (f32[8,256,128]{2,1,0:T(8,128)}, f32[8,256,128]{2,1,0:T(8,128)}, u32[]{:S(2)}, u32[]{:S(2)}) collective-permute-start(f32[8,256,128]{2,1,0:T(8,128)} %get-tuple-element.153), channel_id=1, source_target_pairs={{0,8},{8,0},{16,24},{24,16},{1,9},{9,1},{17,25},{25,17},{2,10},{10... | collective-permute-start | bytes 3145736 | tf_op jit(solution)/shard_map/ppermute | solution.py:490
  416.7 68.4 %collective-permute-start.25 = (f32[8,256,128]{2,1,0:T(8,128)}, f32[8,256,128]{2,1,0:T(8,128)}, u32[]{:S(2)}, u32[]{:S(2)}) collective-permute-start(f32[8,256,128]{2,1,0:T(8,128)} %get-tuple-element.154), channel_id=1, source_target_pairs={{0,16},{8,24},{16,0},{24,8},{1,17},{9,25},{17,1},{25,9},{2,18},{10... | collective-permute-start | bytes 3145736 | tf_op jit(solution)/shard_map/ppermute | solution.py:490
  423.9 81.8 %collective-permute-start.26 = (f32[8,256,128]{2,1,0:T(8,128)}, f32[8,256,128]{2,1,0:T(8,128)}, u32[]{:S(2)}, u32[]{:S(2)}) collective-permute-start(f32[8,256,128]{2,1,0:T(8,128)} %get-tuple-element.155), channel_id=1, source_target_pairs={{0,24},{8,16},{16,8},{24,0},{1,25},{9,17},{17,9},{25,1},{2,26},{10... | collective-permute-start | bytes 3145736 | tf_op jit(solution)/shard_map/ppermute | solution.py:490
  425.5 99.4 %all-to-all-start.2 = ((f32[64,8,16,128]{3,2,1,0:T(8,128)}), f32[64,8,16,128]{3,2,1,0:T(8,128)}, u32[]{:S(2)}, u32[]{:S(2)}) async-start(f32[64,8,16,128]{3,2,1,0:T(8,128)} %shard_map.89), calls=%async_computation.2 | async-start | bytes 8388608 | tf_op jit(solution)/shard_map/all_to_all | solution.py:597
  505.6 37.0 %collective-permute-start.30 = (f32[8,256,128]{2,1,0:T(8,128)}, f32[8,256,128]{2,1,0:T(8,128)}, u32[]{:S(2)}, u32[]{:S(2)}) collective-permute-start(f32[8,256,128]{2,1,0:T(8,128)} %get-tuple-element.169), channel_id=1, source_target_pairs={{0,8},{8,0},{16,24},{24,16},{1,9},{9,1},{17,25},{25,17},{2,10},{10... | collective-permute-start | bytes 3145736 | tf_op jit(solution)/shard_map/ppermute | solution.py:490
  506.4 36.2 %collective-permute-start.31 = (f32[8,256,128]{2,1,0:T(8,128)}, f32[8,256,128]{2,1,0:T(8,128)}, u32[]{:S(2)}, u32[]{:S(2)}) collective-permute-start(f32[8,256,128]{2,1,0:T(8,128)} %get-tuple-element.170), channel_id=1, source_target_pairs={{0,16},{8,24},{16,0},{24,8},{1,17},{9,25},{17,1},{25,9},{2,18},{10... | collective-permute-start | bytes 3145736 | tf_op jit(solution)/shard_map/ppermute | solution.py:490
  507.9 45.4 %collective-permute-start.32 = (f32[8,256,128]{2,1,0:T(8,128)}, f32[8,256,128]{2,1,0:T(8,128)}, u32[]{:S(2)}, u32[]{:S(2)}) collective-permute-start(f32[8,256,128]{2,1,0:T(8,128)} %get-tuple-element.171), channel_id=1, source_target_pairs={{0,24},{8,16},{16,8},{24,0},{1,25},{9,17},{17,9},{25,1},{2,26},{10... | collective-permute-start | bytes 3145736 | tf_op jit(solution)/shard_map/ppermute | solution.py:490
  553.3 49.2 %collective-permute-start.35 = (f32[8,256,128]{2,1,0:T(8,128)}, f32[8,256,128]{2,1,0:T(8,128)S(1)}, u32[]{:S(2)}, u32[]{:S(2)}) collective-permute-start(f32[8,256,128]{2,1,0:T(8,128)} %get-tuple-element.174), channel_id=1, source_target_pairs={{0,8},{8,0},{16,24},{24,16},{1,9},{9,1},{17,25},{25,17},{2,10},{10... | collective-permute-start | bytes 3145736 | tf_op jit(solution)/shard_map/ppermute | solution.py:490
  554.1 54.6 %collective-permute-start.34 = (f32[8,256,128]{2,1,0:T(8,128)}, f32[8,256,128]{2,1,0:T(8,128)S(1)}, u32[]{:S(2)}, u32[]{:S(2)}) collective-permute-start(f32[8,256,128]{2,1,0:T(8,128)} %get-tuple-element.173), channel_id=1, source_target_pairs={{0,16},{8,24},{16,0},{24,8},{1,17},{9,25},{17,1},{25,9},{2,18},{10... | collective-permute-start | bytes 3145736 | tf_op jit(solution)/shard_map/ppermute | solution.py:490
  555.6 59.3 %collective-permute-start.33 = (f32[8,256,128]{2,1,0:T(8,128)}, f32[8,256,128]{2,1,0:T(8,128)S(1)}, u32[]{:S(2)}, u32[]{:S(2)}) collective-permute-start(f32[8,256,128]{2,1,0:T(8,128)} %get-tuple-element.172), channel_id=1, source_target_pairs={{0,24},{8,16},{16,8},{24,0},{1,25},{9,17},{17,9},{25,1},{2,26},{10... | collective-permute-start | bytes 3145736 | tf_op jit(solution)/shard_map/ppermute | solution.py:490
  558.0 1.7 collective-permute-start.36
  560.4 3.9 collective-permute-start.37
  564.2 3.6 collective-permute-start.38
  567.8 4.5 collective-permute-start.39
  572.3 29.6 %collective-permute-start.40 = (f32[4,64]{1,0:T(4,128)S(1)}, f32[4,64]{1,0:T(4,128)S(1)}, u32[]{:S(2)}, u32[]{:S(2)}) collective-permute-start(f32[4,64]{1,0:T(4,128)S(1)} %add.18), channel_id=1, source_target_pairs={{0,16},{8,24},{16,0},{24,8},{1,17},{9,25},{17,1},{25,9},{2,18},{10... | collective-permute-start | bytes 3080 | tf_op jit(solution)/shard_map/ppermute | solution.py:534
  (12 other events, 166.7 us)

commit v2 on v0

--- a/solution.py
+++ b/solution.py
@@ -9,6 +9,7 @@
 
 LEVELS = 64
 TRANSMON = 2
+GROUP = 4
 WIDE = LEVELS * TRANSMON
 PAIR = 2 * WIDE
 HIGH = lax.Precision.HIGHEST
@@ -181,34 +182,39 @@
 
 def open_first_kernel(size, weight_ref, field_ref, *out_refs):
     levels = field_ref.shape[2] // WIDE
-    rows = []
-    for level in range(levels):
-        place = slice(level * WIDE, (level + 1) * WIDE)
-        real_high, real_low = split_value(field_ref[0, :, place])
-        imag_high, imag_low = split_value(field_ref[1, :, place])
-        rows.append(jnp.concatenate([real_high, imag_high, real_low, imag_low], axis=1))
-    made = mxu(jnp.concatenate(rows, axis=0), weight_ref[...])
-    middle = made.shape[1] // 2
     tall = 2 * size
-    for level in range(levels):
-        turned = made[level * WIDE:(level + 1) * WIDE].T
-        turned = turned[:middle] + turned[middle:]
-        for step, out in enumerate(out_refs):
-            out[level * tall:(level + 1) * tall, :] = turned[step * tall:(step + 1) * tall]
+    for first in range(field_ref.shape[1] // WIDE):
+        rows = []
+        down = slice(first * WIDE, (first + 1) * WIDE)
+        for level in range(levels):
+            place = slice(level * WIDE, (level + 1) * WIDE)
+            real_high, real_low = split_value(field_ref[0, down, place])
+            imag_high, imag_low = split_value(field_ref[1, down, place])
+            rows.append(jnp.concatenate([real_high, imag_high, real_low, imag_low], axis=1))
+        made = mxu(jnp.concatenate(rows, axis=0), weight_ref[...])
+        middle = made.shape[1] // 2
+        for level in range(levels):
+            turned = made[level * WIDE:(level + 1) * WIDE].T
+            turned = turned[:middle] + turned[middle:]
+            for step, out in enumerate(out_refs):
+                out[first, level * tall:(level + 1) * tall, :] = turned[
+                    step * tall:(step + 1) * tall
+                ]
 
 
 def open_first(field, weights, parts, size):
     rows, cols = field.shape[1:]
     firsts = rows // WIDE
     tall = cols // WIDE * 2 * size
+    group = min(2, firsts)
     outs = pl.pallas_call(
         functools.partial(open_first_kernel, size),
-        grid=(firsts,),
+        grid=(firsts // group,),
         in_specs=[
             pl.BlockSpec(weights.shape, lambda i: (0, 0)),
-            pl.BlockSpec((2, WIDE, cols), lambda i: (0, i, 0)),
+            pl.BlockSpec((2, group * WIDE, cols), lambda i: (0, i, 0)),
         ],
-        out_specs=[pl.BlockSpec((None, tall, WIDE), lambda i: (i, 0, 0))] * parts,
+        out_specs=[pl.BlockSpec((group, tall, WIDE), lambda i: (i, 0, 0))] * parts,
         out_shape=[jax.ShapeDtypeStruct((firsts, tall, WIDE), F32)] * parts,
         compiler_params=PARAMS,
         cost_estimate=SMALL,
@@ -245,30 +251,32 @@
 def cut_kernel(size, waited, seat_ref, field_ref, *refs):
     seat = seat_ref[0]
     levels = field_ref.shape[-1] // WIDE
-    for step, out in enumerate(refs[waited:]):
-        part = lax.bitwise_xor(seat, step)
-        for half in range(2):
-            for level in range(levels):
-                start = (2 * level + half) * size
-                out[start:start + size, :] = field_ref[
-                    half, part, :, level * WIDE:(level + 1) * WIDE
-                ]
+    for first in range(field_ref.shape[1]):
+        for step, out in enumerate(refs[waited:]):
+            part = lax.bitwise_xor(seat, step)
+            for half in range(2):
+                for level in range(levels):
+                    start = (2 * level + half) * size
+                    out[first, start:start + size, :] = field_ref[
+                        half, first, part, :, level * WIDE:(level + 1) * WIDE
+                    ]
 
 
 def cut_pieces(field, seat, parts, chunk, size, waited):
     rows, cols = field.shape[1:]
     firsts = rows // WIDE
+    group = min(GROUP, firsts)
     chunks = WIDE // parts // size
     tall = cols // WIDE * 2 * size
     return pl.pallas_call(
         functools.partial(cut_kernel, size, len(waited)),
-        grid=(firsts,),
+        grid=(firsts // group,),
         in_specs=[
             pl.BlockSpec(memory_space=pltpu.SMEM),
-            pl.BlockSpec((2, None, parts, None, size, cols), lambda i: (0, i, 0, chunk, 0, 0)),
+            pl.BlockSpec((2, group, parts, None, size, cols), lambda i: (0, i, 0, chunk, 0, 0)),
         ]
         + [pl.BlockSpec(memory_space=pl.ANY)] * len(waited),
-        out_specs=[pl.BlockSpec((None, tall, WIDE), lambda i: (i, 0, 0))] * parts,
+        out_specs=[pl.BlockSpec((group, tall, WIDE), lambda i: (i, 0, 0))] * parts,
         out_shape=[jax.ShapeDtypeStruct((firsts, tall, WIDE), F32)] * parts,
         compiler_params=PARAMS,
         cost_estimate=SMALL,
@@ -302,34 +310,36 @@
     return jnp.concatenate(columns, axis=1)
 
 
-def scatter_levels(ref, size, half, value):
+def scatter_levels(ref, size, half, value, start=0, apart=None):
     for place in range(size):
-        ref[pl.ds(half * size + place, LEVELS, stride=2 * size), :] = value[
-            :, place * WIDE:(place + 1) * WIDE
-        ]
-
-
-def turn_kernel(parts, size, weight_ref, *refs):
-    pieces = refs[:parts]
-    out_ref = refs[-1].reshape(LEVELS * 2 * size, WIDE)
-    made = level_apply(
-        weight_ref[...], gather_levels(pieces, size, 0), gather_levels(pieces, size, 1)
-    )
-    scatter_levels(out_ref, size, 0, made[:LEVELS])
-    scatter_levels(out_ref, size, 1, made[LEVELS:])
+        rows = pl.ds(start + half * size + place, LEVELS, stride=apart or 2 * size)
+        ref[rows, :] = value[:, place * WIDE:(place + 1) * WIDE]
+
+
+def turn_kernel(parts, size, group, weight_ref, *refs):
+    apart = group * 2 * size
+    out_ref = refs[-1].reshape(LEVELS * apart, WIDE)
+    for first in range(group):
+        pieces = [ref.at[first] for ref in refs[:parts]]
+        made = level_apply(
+            weight_ref[...], gather_levels(pieces, size, 0), gather_levels(pieces, size, 1)
+        )
+        scatter_levels(out_ref, size, 0, made[:LEVELS], first * 2 * size, apart)
+        scatter_levels(out_ref, size, 1, made[LEVELS:], first * 2 * size, apart)
 
 
 def turn_columns(pieces, weights, size, waited):
     firsts = pieces[0].shape[0]
+    group = min(GROUP, firsts)
     parts = len(pieces)
     block = pieces[0].shape[1:]
     return pl.pallas_call(
-        functools.partial(turn_kernel, parts, size),
-        grid=(firsts,),
+        functools.partial(turn_kernel, parts, size, group),
+        grid=(firsts // group,),
         in_specs=[pl.BlockSpec((PAIR, PAIR), lambda i: (0, 0))]
-        + [pl.BlockSpec((None,) + block, lambda i: (i, 0, 0))] * parts
+        + [pl.BlockSpec((group,) + block, lambda i: (i, 0, 0))] * parts
         + [pl.BlockSpec(memory_space=pl.ANY)] * len(waited),
-        out_specs=pl.BlockSpec((LEVELS, None, 2 * size, WIDE), lambda i: (0, i, 0, 0)),
+        out_specs=pl.BlockSpec((LEVELS, group, 2 * size, WIDE), lambda i: (0, i, 0, 0)),
         out_shape=jax.ShapeDtypeStruct((LEVELS, firsts, 2 * size, WIDE), F32),
         compiler_params=PARAMS,
         cost_estimate=SMALL,
@@ -415,41 +425,40 @@
     return list(outs[:parts]), outs[parts]
 
 
-def place_kernel(parts, size, aliased, seat_ref, *refs):
+def place_kernel(parts, size, seat_ref, *refs):
     pieces = refs[:parts]
-    out_ref = refs[parts + aliased]
+    out_ref = refs[-1]
     seat = seat_ref[0]
-    levels = pieces[0].shape[0] // (2 * size)
-    for step in range(parts):
-        part = lax.bitwise_xor(seat, step)
-        for half in range(2):
-            for level in range(levels):
-                start = level * 2 * size + half * size
-                out_ref[half, part, :, level * WIDE:(level + 1) * WIDE] = pieces[step][
-                    start:start + size, :
-                ]
-
-
-def place_pieces(pieces, seat, held, chunk, shape, size):
+    levels = out_ref.shape[-1] // WIDE
+    for first in range(out_ref.shape[1]):
+        for step in range(parts):
+            part = lax.bitwise_xor(seat, step)
+            for half in range(2):
+                for level in range(levels):
+                    start = (2 * level + half) * size
+                    out_ref[half, first, part, :, level * WIDE:(level + 1) * WIDE] = pieces[step][
+                        first, start:start + size, :
+                    ]
+
+
+def place_pieces(pieces, seat, held, chunk, shape, size, waited):
     parts = len(pieces)
-    firsts, chunks = shape[1], shape[3]
-    aliased = 0 if held is None else 1
-    piece = pieces[0]
+    group = min(GROUP, shape[1])
     cols = shape[-1]
     return pl.pallas_call(
-        functools.partial(place_kernel, parts, size, aliased),
-        grid=(firsts,),
+        functools.partial(place_kernel, parts, size),
+        grid=(shape[1] // group,),
         in_specs=[pl.BlockSpec(memory_space=pltpu.SMEM)]
-        + [pl.BlockSpec((None,) + piece.shape[1:], lambda i: (i, 0, 0))] * parts
-        + [pl.BlockSpec(memory_space=pl.ANY)] * aliased,
+        + [pl.BlockSpec((group,) + pieces[0].shape[1:], lambda i: (i, 0, 0))] * parts
+        + [pl.BlockSpec(memory_space=pl.ANY)],
         out_specs=pl.BlockSpec(
-            (2, None, parts, None, size, cols), lambda i: (0, i, 0, chunk, 0, 0)
+            (2, group, parts, None, size, cols), lambda i: (0, i, 0, chunk, 0, 0)
         ),
         out_shape=jax.ShapeDtypeStruct(shape, F32),
-        input_output_aliases={parts + 1: 0} if aliased else {},
-        compiler_params=PARAMS,
-        cost_estimate=SMALL,
-    )(seat, *pieces, *([held] if aliased else []))
+        input_output_aliases={} if held is None else {parts + 1: 0},
+        compiler_params=PARAMS,
+        cost_estimate=SMALL,
+    )(seat, *pieces, waited if held is None else held)
 
 
 def swap(pieces, parts):
@@ -522,11 +531,15 @@
             costate, opened, parts, size, 1, chunks - 1, list(state_cut[0][:1])
         )
     rho = [
-        cut_pieces(density, seats, parts, chunk, size, list(state_cut[-1][:1]))
+        cut_pieces(density, seats, parts, chunk, size, list(state_cut[-1][:1]) if chunk else [])
         for chunk in range(chunks)
     ]
+    rho_there = [swap(pieces, parts) for pieces in rho]
+    ahead = parts // 2
+    state_cut[0], rho_there[0][ahead] = lax.optimization_barrier(
+        (state_cut[0], rho_there[0][ahead])
+    )
     state = [swap(pieces, parts) for pieces in state_cut[:3]]
-    rho_there = [swap(pieces, parts) for pieces in rho]
 
     shape = (2, rows // WIDE, parts, chunks, size, cols)
     fields, closed, made, grads = [], [], [], []
@@ -542,11 +555,14 @@
             out, rho_there[-1] = lax.optimization_barrier((out, rho_there[-1]))
         if chunk == chunks - 1 and chunk > 1:
             out, made[-1] = lax.optimization_barrier((out, made[-1]))
-        made.append(swap(out, parts))
+        if chunk > 0 or chunks < 4:
+            made.append(swap(out, parts))
         grads.append(grad)
 
     for chunk in range(chunks):
         waited = [rho[chunk][0]]
+        if chunk == 0:
+            waited += [pieces[0] for pieces in state_cut[1:2]]
         if chunk > 0:
             waited.append(field)
         if chunk > 1:
@@ -556,13 +572,15 @@
         if chunk + 1 == len(state) < chunks:
             pieces, field = lax.optimization_barrier((state_cut[chunk + 1], field))
             state.append(swap(pieces, parts))
+            out, rho_there[2] = lax.optimization_barrier((closed[0], rho_there[2]))
+            made.append(swap(out, parts))
         fields.append(lax.all_to_all(field, "dev", split_axis=0, concat_axis=0, tiled=True))
     whole = None
     for chunk in range(chunks):
         while len(made) < min(chunk + 2, chunks):
             waited = list(made[-2][1:]) if len(made) > 1 else []
             close(len(made), [whole] if 0 < chunk == chunks - 2 else waited)
-        whole = place_pieces(made[chunk], seats, whole, chunk, shape, size)
+        whole = place_pieces(made[chunk], seats, whole, chunk, shape, size, field)
     grad = grand_total(device_grad(grads, seats, parts, []))
     return whole.reshape(costate.shape), grad.reshape(2, 2, LEVELS)
 

time: 598 us -> 615 us (1.028)
  waiting for transfers between devices: 330 us -> 383 us
  Pallas kernels: 196 us -> 167 us
  starting transfers between devices: 62.2 us -> 54.8 us
    ppermute x36, waiting for transfers between devices: 239 us -> 280 us  [swap(): moved.append(lax.ppermute(pieces[step], 'grp', pairs))]
    pallas_call x9, Pallas kernels: 72.2 us -> 55.2 us  [the longest x4 30.1 us: turn_columns(): pl.pallas_call(functools.partial(turn_kernel, parts, size, group), grid=(...]
    pallas_call x4, Pallas kernels: 26.5 us -> 14.9 us  [cut_pieces(): pl.pallas_call(functools.partial(cut_kernel, size, len(waited)), grid=(fi...]
    ppermute x5, waiting for transfers between devices: 27.4 us -> 35.5 us  [grand_total(): value = value + lax.ppermute(value, axis, pairs)]
  transfers between devices with their start and end apart: 45 -> 45, of which waited for: 24 -> 23; matrix products, arithmetic and copies ran while one was open for 0% -> 0% of each run, Pallas kernels for 28% -> 25%
where the time goes in v2:
time: 615 us; the launch traced here: 613 us
  waiting for transfers between devices  383 us (62%)
  Pallas kernels  167 us (27%)
  starting transfers between devices  54.8 us (9%)
    ppermute x36, waiting for transfers between devices, swap(): moved.append(lax.ppermute(pieces[step], 'grp', pairs))  280 us
    pallas_call x4, Pallas kernels, close_columns(): pl.pallas_call(functools.partial(close_kernel, parts, size), grid=(firsts...  70.9 us
    all_to_all x4, waiting for transfers between devices, per_device(): lax.all_to_all(field, 'dev', split_axis=0, concat_axis=0, tiled=True)  67.7 us
    ppermute x5, waiting for transfers between devices, grand_total(): value = value + lax.ppermute(value, axis, pairs)  35.5 us
    pallas_call x4, Pallas kernels, turn_columns(): pl.pallas_call(functools.partial(turn_kernel, parts, size, group), grid=(...  30.1 us
    ppermute x36, starting transfers between devices, swap(): moved.append(lax.ppermute(pieces[step], 'grp', pairs))  27.5 us
    all_to_all x4, starting transfers between devices, per_device(): lax.all_to_all(field, 'dev', split_axis=0, concat_axis=0, tiled=True)  23.2 us
    pallas_call x1, Pallas kernels, open_state(): pl.pallas_call(functools.partial(open_kernel, count, len(waited)), grid=(...  19.5 us
  transfers between devices with their start and end apart: 45, of which 23 were waited for; matrix products, arithmetic and copies ran while one was open for 0% of the time, Pallas kernels for 25%

profile of v2, /device:TPU:0, one launch (start us, length us, event | category | flops | bytes accessed | tf_op | source)
XLA Modules:
  0.0 613.3 jit_solution(1921451864616793063)
XLA Ops:
  0.6 3.8 shard_map.82
  4.4 2.9 collective-permute-start.6
  8.0 4.6 shard_map.77
  12.5 10.4 %shard_map.78 = (f32[8,256,128]{2,1,0:T(8,128)}, f32[8,256,128]{2,1,0:T(8,128)}, f32[8,256,128]{2,1,0:T(8,128)}, f32[8,256,128]{2,1,0:T(8,128)}) custom-call(bf16[512,128]{1,0:T(8,128)(2,1)} %get-tuple-element.97.weight_ref, f32[2,1024,2048]{2,1,0:T(8,128)} %field_ref.3), custom_call_target="tpu_custom_call" | custom-call | flops 1024 | bytes 1024 | tf_op jit(solution)/shard_map/pallas_call | solution.py:210
  22.9 7.8 %collective-permute-done.6.refs_2_ = f32[8,256,128]{2,1,0:T(8,128)S(1)} collective-permute-done((f32[8,256,128]{2,1,0:T(8,128)}, f32[8,256,128]{2,1,0:T(8,128)S(1)}, u32[]{:S(2)}, u32[]{:S(2)}) %collective-permute-start.6) | collective-permute-done | bytes 1048608 | tf_op jit(solution)/shard_map/ppermute | solution.py:468
  31.7 1.7 collective-permute-start.8
  34.3 19.5 %shard_map.79 = (f32[8,256,128]{2,1,0:T(8,128)}, f32[8,256,128]{2,1,0:T(8,128)}, f32[8,256,128]{2,1,0:T(8,128)}, f32[8,256,128]{2,1,0:T(8,128)}, f32[8,256,128]{...) custom-call(bf16[2,192,256]{2,1,0:T(8,128)(2,1)} %slice.3.weight_ref, ...), custom_call_target="tpu_custom_call" | custom-call | flops 1024 | bytes 1024 | tf_op jit(solution)/shard_map/pallas_call | solution.py:235
  53.8 4.1 collective-permute-done.8.refs_2_
  57.9 21.7 %collective-permute-done.9.refs_3_ = f32[8,256,128]{2,1,0:T(8,128)S(1)} collective-permute-done((f32[8,256,128]{2,1,0:T(8,128)}, f32[8,256,128]{2,1,0:T(8,128)S(1)}, u32[]{:S(2)}, u32[]{:S(2)}) %collective-permute-start.9) | collective-permute-done | bytes 1048608 | tf_op jit(solution)/shard_map/ppermute | solution.py:468
  80.5 7.5 %shard_map.83.refs_5_ = f32[64,8,16,128]{3,2,1,0:T(8,128)} custom-call(bf16[256,256]{1,0:T(8,128)(2,1)} %get-tuple-element.95.weight_ref, f32[8,256,128]{2,1,0:T(8,128)} %get-tuple-element.117.refs_0_, f32[8,256,128]{2,1,0:T(8,128)} %copy-done.9, f32[8,256,128]{2,1,0:T(8,128)} %copy-done.10, f32[8,256,128]{2,1,0:T(8,128)} %copy-done.11, ...), custom_call_target="tpu_custom_call" | custom-call | flops 1024 | bytes 1024 | tf_op jit(solution)/shard_map/pallas_call | solution.py:336
  88.1 6.1 all-to-all-start
  97.9 3.7 shard_map.80
  102.2 18.6 %collective-permute-done.4.refs_2_ = f32[8,256,128]{2,1,0:T(8,128)S(1)} collective-permute-done((f32[8,256,128]{2,1,0:T(8,128)}, f32[8,256,128]{2,1,0:T(8,128)S(1)}, u32[]{:S(2)}, u32[]{:S(2)}) %collective-permute-start.4) | collective-permute-done | bytes 1048608 | tf_op jit(solution)/shard_map/ppermute | solution.py:468
  120.9 21.6 %collective-permute-done.5.refs_3_ = f32[8,256,128]{2,1,0:T(8,128)S(1)} collective-permute-done((f32[8,256,128]{2,1,0:T(8,128)}, f32[8,256,128]{2,1,0:T(8,128)S(1)}, u32[]{:S(2)}, u32[]{:S(2)}) %collective-permute-start.5) | collective-permute-done | bytes 1048608 | tf_op jit(solution)/shard_map/ppermute | solution.py:468
  143.6 3.7 shard_map.81
  147.3 7.5 %shard_map.84.refs_5_ = f32[64,8,16,128]{3,2,1,0:T(8,128)} custom-call(bf16[256,256]{1,0:T(8,128)(2,1)} %get-tuple-element.95.weight_ref, f32[8,256,128]{2,1,0:T(8,128)} %get-tuple-element.108.refs_5_.refs_0_, f32[8,256,128]{2,1,0:T(8,128)} %copy-done.6, f32[8,256,128]{2,1,0:T(8,128)} %copy-done.7, f32[8,256,128]{2,1,0:T(8,128)} %copy-done.8, ...), custom_call_target="tpu_custom_call" | custom-call | flops 1024 | bytes 1024 | tf_op jit(solution)/shard_map/pallas_call | solution.py:336
  154.8 10.1 %collective-permute-done.11.refs_3_ = f32[8,256,128]{2,1,0:T(8,128)} collective-permute-done((f32[8,256,128]{2,1,0:T(8,128)}, f32[8,256,128]{2,1,0:T(8,128)}, u32[]{:S(2)}, u32[]{:S(2)}) %collective-permute-start.11) | collective-permute-done | bytes 1048608 | tf_op jit(solution)/shard_map/ppermute | solution.py:468
  167.2 21.1 %collective-permute-done.1.refs_2_ = f32[8,256,128]{2,1,0:T(8,128)} collective-permute-done((f32[8,256,128]{2,1,0:T(8,128)}, f32[8,256,128]{2,1,0:T(8,128)}, u32[]{:S(2)}, u32[]{:S(2)}) %collective-permute-start.1) | collective-permute-done | bytes 1048608 | tf_op jit(solution)/shard_map/ppermute | solution.py:468
  188.4 21.5 %collective-permute-done.2.refs_3_ = f32[8,256,128]{2,1,0:T(8,128)} collective-permute-done((f32[8,256,128]{2,1,0:T(8,128)}, f32[8,256,128]{2,1,0:T(8,128)}, u32[]{:S(2)}, u32[]{:S(2)}) %collective-permute-start.2) | collective-permute-done | bytes 1048608 | tf_op jit(solution)/shard_map/ppermute | solution.py:468
  212.0 6.0 all-to-all-start.1
  218.0 17.7 %shard_map.85 = (f32[8,256,128]{2,1,0:T(8,128)}, f32[8,256,128]{2,1,0:T(8,128)}, f32[8,256,128]{2,1,0:T(8,128)}, f32[8,256,128]{2,1,0:T(8,128)}, f32[2,64,128]{2,1,0:T(8,128)}) custom-call(bf16[3,2,256,256]{3,2,1,0:T(8,128)(2,1)} %get-tuple-element.93.lane_ref, bf16[3,256,256]{2,1,0:T(8,128)(2,1)} %get-tuple-element.94.level_ref, ...), custom_call_target="tpu_custom_call" | custom-call | flops 199999995904 | bytes 1024 | tf_op jit(solution)/shard_map/pallas_call | solution.py:408
  235.8 7.6 %shard_map.86.refs_5_ = f32[64,8,16,128]{3,2,1,0:T(8,128)} custom-call(bf16[256,256]{1,0:T(8,128)(2,1)} %get-tuple-element.95.weight_ref, f32[8,256,128]{2,1,0:T(8,128)} %get-tuple-element.103.refs_0_, f32[8,256,128]{2,1,0:T(8,128)} %collective-permute-done.refs_1_, f32[8,256,128]{2,1,0:T(8,128)} %collective-permute-done.1.refs_2_, ...), custom_call_target="tpu_custom_call" | custom-call | flops 1024 | bytes 1024 | tf_op jit(solution)/shard_map/pallas_call | solution.py:336
  243.3 34.9 %collective-permute-done.19.refs_2_ = f32[8,256,128]{2,1,0:T(8,128)} collective-permute-done((f32[8,256,128]{2,1,0:T(8,128)}, f32[8,256,128]{2,1,0:T(8,128)}, u32[]{:S(2)}, u32[]{:S(2)}) %collective-permute-start.19) | collective-permute-done | bytes 1048608 | tf_op jit(solution)/shard_map/ppermute | solution.py:468
  278.3 20.7 %collective-permute-done.20.refs_3_ = f32[8,256,128]{2,1,0:T(8,128)} collective-permute-done((f32[8,256,128]{2,1,0:T(8,128)}, f32[8,256,128]{2,1,0:T(8,128)}, u32[]{:S(2)}, u32[]{:S(2)}) %collective-permute-start.20) | collective-permute-done | bytes 1048608 | tf_op jit(solution)/shard_map/ppermute | solution.py:468
  300.5 11.0 %all-to-all-done.1 = f32[64,8,16,128]{3,2,1,0:T(8,128)} async-done(((f32[64,8,16,128]{3,2,1,0:T(8,128)}), f32[64,8,16,128]{3,2,1,0:T(8,128)}, u32[]{:S(2)}, u32[]{:S(2)}) %all-to-all-start.1) | async-done | bytes 4194336 | tf_op jit(solution)/shard_map/all_to_all | solution.py:577
  311.5 4.6 all-to-all-start.3
  318.3 17.7 %shard_map.88 = (f32[8,256,128]{2,1,0:T(8,128)}, f32[8,256,128]{2,1,0:T(8,128)}, f32[8,256,128]{2,1,0:T(8,128)}, f32[8,256,128]{2,1,0:T(8,128)}, f32[2,64,128]{2,1,0:T(8,128)}) custom-call(bf16[3,2,256,256]{3,2,1,0:T(8,128)(2,1)} %get-tuple-element.93.lane_ref, bf16[3,256,256]{2,1,0:T(8,128)(2,1)} %get-tuple-element.94.level_ref, ...), custom_call_target="tpu_custom_call" | custom-call | flops 199999995904 | bytes 1024 | tf_op jit(solution)/shard_map/pallas_call | solution.py:408
  336.8 10.5 %collective-permute-done.14.refs_3_ = f32[8,256,128]{2,1,0:T(8,128)} collective-permute-done((f32[8,256,128]{2,1,0:T(8,128)}, f32[8,256,128]{2,1,0:T(8,128)}, u32[]{:S(2)}, u32[]{:S(2)}) %collective-permute-start.14) | collective-permute-done | bytes 1048608 | tf_op jit(solution)/shard_map/ppermute | solution.py:468
  349.3 3.7 shard_map.87
  352.9 7.6 %shard_map.89.refs_4_ = f32[64,8,16,128]{3,2,1,0:T(8,128)} custom-call(bf16[256,256]{1,0:T(8,128)(2,1)} %get-tuple-element.95.weight_ref, f32[8,256,128]{2,1,0:T(8,128)} %get-tuple-element.126.refs_0_, f32[8,256,128]{2,1,0:T(8,128)} %collective-permute-done.12.refs_1_, f32[8,256,128]{2,1,0:T(8,128)} %collective-permute-done.13.refs_2_, ...), custom_call_target="tpu_custom_call" | custom-call | flops 1024 | bytes 1024 | tf_op jit(solution)/shard_map/pallas_call | solution.py:336
  360.5 9.8 %collective-permute-done.22.refs_5_.refs_2_ = f32[8,256,128]{2,1,0:T(8,128)} collective-permute-done((f32[8,256,128]{2,1,0:T(8,128)}, f32[8,256,128]{2,1,0:T(8,128)}, u32[]{:S(2)}, u32[]{:S(2)}) %collective-permute-start.22) | collective-permute-done | bytes 1048608 | tf_op jit(solution)/shard_map/ppermute | solution.py:468
  370.3 21.8 %collective-permute-done.23.refs_6_.refs_3_ = f32[8,256,128]{2,1,0:T(8,128)S(1)} collective-permute-done((f32[8,256,128]{2,1,0:T(8,128)}, f32[8,256,128]{2,1,0:T(8,128)S(1)}, u32[]{:S(2)}, u32[]{:S(2)}) %collective-permute-start.23) | collective-permute-done | bytes 1048608 | tf_op jit(solution)/shard_map/ppermute | solution.py:468
  393.6 3.7 shard_map.91.refs_4_
  398.3 16.8 %collective-permute-done.28.refs_2_ = f32[8,256,128]{2,1,0:T(8,128)S(1)} collective-permute-done((f32[8,256,128]{2,1,0:T(8,128)}, f32[8,256,128]{2,1,0:T(8,128)S(1)}, u32[]{:S(2)}, u32[]{:S(2)}) %collective-permute-start.28) | collective-permute-done | bytes 1048608 | tf_op jit(solution)/shard_map/ppermute | solution.py:468
  415.1 22.0 %collective-permute-done.29.refs_3_ = f32[8,256,128]{2,1,0:T(8,128)} collective-permute-done((f32[8,256,128]{2,1,0:T(8,128)}, f32[8,256,128]{2,1,0:T(8,128)}, u32[]{:S(2)}, u32[]{:S(2)}) %collective-permute-start.29) | collective-permute-done | bytes 1048608 | tf_op jit(solution)/shard_map/ppermute | solution.py:468
  437.2 3.7 shard_map.92.refs_4_
  440.8 6.5 %all-to-all-start.2 = ((f32[64,8,16,128]{3,2,1,0:T(8,128)}), f32[64,8,16,128]{3,2,1,0:T(8,128)}, u32[]{:S(2)}, u32[]{:S(2)}) async-start(f32[64,8,16,128]{3,2,1,0:T(8,128)} %shard_map.89.refs_4_), calls=%async_computation.2 | async-start | bytes 8388608 | tf_op jit(solution)/shard_map/all_to_all | solution.py:577
  447.3 17.8 %shard_map.90 = (f32[8,256,128]{2,1,0:T(8,128)}, f32[8,256,128]{2,1,0:T(8,128)}, f32[8,256,128]{2,1,0:T(8,128)}, f32[8,256,128]{2,1,0:T(8,128)}, f32[2,64,128]{2,1,0:T(8,128)}) custom-call(bf16[3,2,256,256]{3,2,1,0:T(8,128)(2,1)} %get-tuple-element.93.lane_ref, bf16[3,256,256]{2,1,0:T(8,128)(2,1)} %get-tuple-element.94.level_ref, ...), custom_call_target="tpu_custom_call" | custom-call | flops 199999995904 | bytes 1024 | tf_op jit(solution)/shard_map/pallas_call | solution.py:408
  465.1 17.0 %collective-permute-done.26.refs_3_ = f32[8,256,128]{2,1,0:T(8,128)} collective-permute-done((f32[8,256,128]{2,1,0:T(8,128)}, f32[8,256,128]{2,1,0:T(8,128)}, u32[]{:S(2)}, u32[]{:S(2)}) %collective-permute-start.26) | collective-permute-done | bytes 1048608 | tf_op jit(solution)/shard_map/ppermute | solution.py:468
  484.0 56.7 %all-to-all-done.2 = f32[64,8,16,128]{3,2,1,0:T(8,128)} async-done(((f32[64,8,16,128]{3,2,1,0:T(8,128)}), f32[64,8,16,128]{3,2,1,0:T(8,128)}, u32[]{:S(2)}, u32[]{:S(2)}) %all-to-all-start.2) | async-done | bytes 4194336 | tf_op jit(solution)/shard_map/all_to_all | solution.py:577
  540.7 17.7 %shard_map.93 = (f32[8,256,128]{2,1,0:T(8,128)}, f32[8,256,128]{2,1,0:T(8,128)}, f32[8,256,128]{2,1,0:T(8,128)}, f32[8,256,128]{2,1,0:T(8,128)}, f32[2,64,128]{2,1,0:T(8,128)}) custom-call(bf16[3,2,256,256]{3,2,1,0:T(8,128)(2,1)} %get-tuple-element.93.lane_ref, bf16[3,256,256]{2,1,0:T(8,128)(2,1)} %get-tuple-element.94.level_ref, ...), custom_call_target="tpu_custom_call" | custom-call | flops 199999995904 | bytes 1024 | tf_op jit(solution)/shard_map/pallas_call | solution.py:408
  560.3 2.4 shard_map.96
  566.3 2.1 collective-permute-done.37
  568.4 3.6 collective-permute-done.38
  572.8 3.7 collective-permute-done.39
  578.0 3.7 shard_map.94.refs_4_
  581.7 25.1 %collective-permute-done.40 = f32[4,64]{1,0:T(4,128)S(1)} collective-permute-done((f32[4,64]{1,0:T(4,128)S(1)}, f32[4,64]{1,0:T(4,128)S(1)}, u32[]{:S(2)}, u32[]{:S(2)}) %collective-permute-start.40) | collective-permute-done | bytes 1056 | tf_op jit(solution)/shard_map/ppermute | solution.py:512
  609.7 3.7 shard_map.95
  (96 shorter events, 34.3 us)
Async XLA Ops:
  4.4 26.3 %collective-permute-start.6 = (f32[8,256,128]{2,1,0:T(8,128)}, f32[8,256,128]{2,1,0:T(8,128)S(1)}, u32[]{:S(2)}, u32[]{:S(2)}) collective-permute-start(f32[8,256,128]{2,1,0:T(8,128)} %get-tuple-element.116), channel_id=1, source_target_pairs={{0,16},{8,24},{16,0},{24,8},{1,17},{9,25},{17,1},{25,9},{2,18},{10... | collective-permute-start | bytes 3145736 | tf_op jit(solution)/shard_map/ppermute | solution.py:468
  31.7 22.1 %collective-permute-start.7 = (f32[8,256,128]{2,1,0:T(8,128)}, f32[8,256,128]{2,1,0:T(8,128)S(1)}, u32[]{:S(2)}, u32[]{:S(2)}) collective-permute-start(f32[8,256,128]{2,1,0:T(8,128)} %get-tuple-element.118), channel_id=1, source_target_pairs={{0,8},{8,0},{16,24},{24,16},{1,9},{9,1},{17,25},{25,17},{2,10},{10... | collective-permute-start | bytes 3145736 | tf_op jit(solution)/shard_map/ppermute | solution.py:468
  31.7 26.2 %collective-permute-start.8 = (f32[8,256,128]{2,1,0:T(8,128)}, f32[8,256,128]{2,1,0:T(8,128)S(1)}, u32[]{:S(2)}, u32[]{:S(2)}) collective-permute-start(f32[8,256,128]{2,1,0:T(8,128)} %get-tuple-element.119), channel_id=1, source_target_pairs={{0,16},{8,24},{16,0},{24,8},{1,17},{9,25},{17,1},{25,9},{2,18},{10... | collective-permute-start | bytes 3145736 | tf_op jit(solution)/shard_map/ppermute | solution.py:468
  33.4 46.1 %collective-permute-start.9 = (f32[8,256,128]{2,1,0:T(8,128)}, f32[8,256,128]{2,1,0:T(8,128)S(1)}, u32[]{:S(2)}, u32[]{:S(2)}) collective-permute-start(f32[8,256,128]{2,1,0:T(8,128)} %get-tuple-element.120), channel_id=1, source_target_pairs={{0,24},{8,16},{16,8},{24,0},{1,25},{9,17},{17,9},{25,1},{2,26},{10... | collective-permute-start | bytes 3145736 | tf_op jit(solution)/shard_map/ppermute | solution.py:468
  88.1 124.0 %all-to-all-start = ((f32[64,8,16,128]{3,2,1,0:T(8,128)}), f32[64,8,16,128]{3,2,1,0:T(8,128)}, u32[]{:S(2)}, u32[]{:S(2)}) async-start(f32[64,8,16,128]{3,2,1,0:T(8,128)} %shard_map.83.refs_5_), calls=%async_computation | async-start | bytes 8388608 | tf_op jit(solution)/shard_map/all_to_all | solution.py:577
  94.1 7.5 %collective-permute-start.10 = (f32[8,256,128]{2,1,0:T(8,128)}, f32[8,256,128]{2,1,0:T(8,128)}, u32[]{:S(2)}, u32[]{:S(2)}) collective-permute-start(f32[8,256,128]{2,1,0:T(8,128)} %get-tuple-element.122), channel_id=1, source_target_pairs={{0,8},{8,0},{16,24},{24,16},{1,9},{9,1},{17,25},{25,17},{2,10},{10... | collective-permute-start | bytes 3145736 | tf_op jit(solution)/shard_map/ppermute | solution.py:468
  94.1 7.5 %collective-permute-start.3 = (f32[8,256,128]{2,1,0:T(8,128)}, f32[8,256,128]{2,1,0:T(8,128)S(1)}, u32[]{:S(2)}, u32[]{:S(2)}) collective-permute-start(f32[8,256,128]{2,1,0:T(8,128)} %get-tuple-element.109), channel_id=1, source_target_pairs={{0,8},{8,0},{16,24},{24,16},{1,9},{9,1},{17,25},{25,17},{2,10},{10... | collective-permute-start | bytes 3145736 | tf_op jit(solution)/shard_map/ppermute | solution.py:468
  94.6 26.2 %collective-permute-start.4 = (f32[8,256,128]{2,1,0:T(8,128)}, f32[8,256,128]{2,1,0:T(8,128)S(1)}, u32[]{:S(2)}, u32[]{:S(2)}) collective-permute-start(f32[8,256,128]{2,1,0:T(8,128)} %get-tuple-element.110), channel_id=1, source_target_pairs={{0,16},{8,24},{16,0},{24,8},{1,17},{9,25},{17,1},{25,9},{2,18},{10... | collective-permute-start | bytes 3145736 | tf_op jit(solution)/shard_map/ppermute | solution.py:468
  96.1 46.3 %collective-permute-start.5 = (f32[8,256,128]{2,1,0:T(8,128)}, f32[8,256,128]{2,1,0:T(8,128)S(1)}, u32[]{:S(2)}, u32[]{:S(2)}) collective-permute-start(f32[8,256,128]{2,1,0:T(8,128)} %get-tuple-element.111), channel_id=1, source_target_pairs={{0,24},{8,16},{16,8},{24,0},{1,25},{9,17},{17,9},{25,1},{2,26},{10... | collective-permute-start | bytes 3145736 | tf_op jit(solution)/shard_map/ppermute | solution.py:468
  96.1 68.8 %collective-permute-start.11 = (f32[8,256,128]{2,1,0:T(8,128)}, f32[8,256,128]{2,1,0:T(8,128)}, u32[]{:S(2)}, u32[]{:S(2)}) collective-permute-start(f32[8,256,128]{2,1,0:T(8,128)} %get-tuple-element.124), channel_id=1, source_target_pairs={{0,24},{8,16},{16,8},{24,0},{1,25},{9,17},{17,9},{25,1},{2,26},{10... | collective-permute-start | bytes 3145736 | tf_op jit(solution)/shard_map/ppermute | solution.py:468
  101.6 64.1 %collective-permute-start = (f32[8,256,128]{2,1,0:T(8,128)}, f32[8,256,128]{2,1,0:T(8,128)}, u32[]{:S(2)}, u32[]{:S(2)}) collective-permute-start(f32[8,256,128]{2,1,0:T(8,128)} %get-tuple-element.104), channel_id=1, source_target_pairs={{0,8},{8,0},{16,24},{24,16},{1,9},{9,1},{17,25},{25,17},{2,10},{10... | collective-permute-start | bytes 3145736 | tf_op jit(solution)/shard_map/ppermute | solution.py:468
  101.6 45.7 %copy-start.6 = (f32[8,256,128]{2,1,0:T(8,128)}, f32[8,256,128]{2,1,0:T(8,128)S(1)}, u32[]{:S(2)}) copy-start(f32[8,256,128]{2,1,0:T(8,128)S(1)} %collective-permute-done.3.refs_1_) | copy-start | bytes 3145732
  101.6 86.8 %collective-permute-start.1 = (f32[8,256,128]{2,1,0:T(8,128)}, f32[8,256,128]{2,1,0:T(8,128)}, u32[]{:S(2)}, u32[]{:S(2)}) collective-permute-start(f32[8,256,128]{2,1,0:T(8,128)} %get-tuple-element.105), channel_id=1, source_target_pairs={{0,16},{8,24},{16,0},{24,8},{1,17},{9,25},{17,1},{25,9},{2,18},{10... | collective-permute-start | bytes 3145736 | tf_op jit(solution)/shard_map/ppermute | solution.py:468
  120.9 26.4 %copy-start.7 = (f32[8,256,128]{2,1,0:T(8,128)}, f32[8,256,128]{2,1,0:T(8,128)S(1)}, u32[]{:S(2)}) copy-start(f32[8,256,128]{2,1,0:T(8,128)S(1)} %collective-permute-done.4.refs_2_) | copy-start | bytes 3145732
  120.9 89.0 %collective-permute-start.2 = (f32[8,256,128]{2,1,0:T(8,128)}, f32[8,256,128]{2,1,0:T(8,128)}, u32[]{:S(2)}, u32[]{:S(2)}) collective-permute-start(f32[8,256,128]{2,1,0:T(8,128)} %get-tuple-element.106), channel_id=1, source_target_pairs={{0,24},{8,16},{16,8},{24,0},{1,25},{9,17},{17,9},{25,1},{2,26},{10... | collective-permute-start | bytes 3145736 | tf_op jit(solution)/shard_map/ppermute | solution.py:468
  142.5 68.1 %collective-permute-start.18 = (f32[8,256,128]{2,1,0:T(8,128)}, f32[8,256,128]{2,1,0:T(8,128)}, u32[]{:S(2)}, u32[]{:S(2)}) collective-permute-start(f32[8,256,128]{2,1,0:T(8,128)} %get-tuple-element.139), channel_id=1, source_target_pairs={{0,8},{8,0},{16,24},{24,16},{1,9},{9,1},{17,25},{25,17},{2,10},{10... | collective-permute-start | bytes 3145736 | tf_op jit(solution)/shard_map/ppermute | solution.py:468
  164.9 151.1 %collective-permute-start.15 = (f32[8,256,128]{2,1,0:T(8,128)}, f32[8,256,128]{2,1,0:T(8,128)}, u32[]{:S(2)}, u32[]{:S(2)}) collective-permute-start(f32[8,256,128]{2,1,0:T(8,128)} %get-tuple-element.132), channel_id=1, source_target_pairs={{0,8},{8,0},{16,24},{24,16},{1,9},{9,1},{17,25},{25,17},{2,10},{10... | collective-permute-start | bytes 3145736 | tf_op jit(solution)/shard_map/ppermute | solution.py:468
  165.7 150.4 %collective-permute-start.16 = (f32[8,256,128]{2,1,0:T(8,128)}, f32[8,256,128]{2,1,0:T(8,128)}, u32[]{:S(2)}, u32[]{:S(2)}) collective-permute-start(f32[8,256,128]{2,1,0:T(8,128)} %get-tuple-element.133), channel_id=1, source_target_pairs={{0,16},{8,24},{16,0},{24,8},{1,17},{9,25},{17,1},{25,9},{2,18},{10... | collective-permute-start | bytes 3145736 | tf_op jit(solution)/shard_map/ppermute | solution.py:468
  188.4 128.4 %collective-permute-start.17 = (f32[8,256,128]{2,1,0:T(8,128)}, f32[8,256,128]{2,1,0:T(8,128)}, u32[]{:S(2)}, u32[]{:S(2)}) collective-permute-start(f32[8,256,128]{2,1,0:T(8,128)} %get-tuple-element.134), channel_id=1, source_target_pairs={{0,24},{8,16},{16,8},{24,0},{1,25},{9,17},{17,9},{25,1},{2,26},{10... | collective-permute-start | bytes 3145736 | tf_op jit(solution)/shard_map/ppermute | solution.py:468
  209.9 68.4 %collective-permute-start.19 = (f32[8,256,128]{2,1,0:T(8,128)}, f32[8,256,128]{2,1,0:T(8,128)}, u32[]{:S(2)}, u32[]{:S(2)}) collective-permute-start(f32[8,256,128]{2,1,0:T(8,128)} %get-tuple-element.140), channel_id=1, source_target_pairs={{0,16},{8,24},{16,0},{24,8},{1,17},{9,25},{17,1},{25,9},{2,18},{10... | collective-permute-start | bytes 3145736 | tf_op jit(solution)/shard_map/ppermute | solution.py:468
  210.6 88.4 %collective-permute-start.20 = (f32[8,256,128]{2,1,0:T(8,128)}, f32[8,256,128]{2,1,0:T(8,128)}, u32[]{:S(2)}, u32[]{:S(2)}) collective-permute-start(f32[8,256,128]{2,1,0:T(8,128)} %get-tuple-element.141), channel_id=1, source_target_pairs={{0,24},{8,16},{16,8},{24,0},{1,25},{9,17},{17,9},{25,1},{2,26},{10... | collective-permute-start | bytes 3145736 | tf_op jit(solution)/shard_map/ppermute | solution.py:468
  212.0 99.4 %all-to-all-start.1 = ((f32[64,8,16,128]{3,2,1,0:T(8,128)}), f32[64,8,16,128]{3,2,1,0:T(8,128)}, u32[]{:S(2)}, u32[]{:S(2)}) async-start(f32[64,8,16,128]{3,2,1,0:T(8,128)} %shard_map.84.refs_5_), calls=%async_computation.1 | async-start | bytes 8388608 | tf_op jit(solution)/shard_map/all_to_all | solution.py:577
  278.3 57.8 %collective-permute-start.12 = (f32[8,256,128]{2,1,0:T(8,128)}, f32[8,256,128]{2,1,0:T(8,128)}, u32[]{:S(2)}, u32[]{:S(2)}) collective-permute-start(f32[8,256,128]{2,1,0:T(8,128)} %get-tuple-element.127), channel_id=1, source_target_pairs={{0,8},{8,0},{16,24},{24,16},{1,9},{9,1},{17,25},{25,17},{2,10},{10... | collective-permute-start | bytes 3145736 | tf_op jit(solution)/shard_map/ppermute | solution.py:468
  299.0 37.2 %collective-permute-start.13 = (f32[8,256,128]{2,1,0:T(8,128)}, f32[8,256,128]{2,1,0:T(8,128)}, u32[]{:S(2)}, u32[]{:S(2)}) collective-permute-start(f32[8,256,128]{2,1,0:T(8,128)} %get-tuple-element.128), channel_id=1, source_target_pairs={{0,16},{8,24},{16,0},{24,8},{1,17},{9,25},{17,1},{25,9},{2,18},{10... | collective-permute-start | bytes 3145736 | tf_op jit(solution)/shard_map/ppermute | solution.py:468
  311.5 129.4 %all-to-all-start.3 = ((f32[64,8,16,128]{3,2,1,0:T(8,128)}), f32[64,8,16,128]{3,2,1,0:T(8,128)}, u32[]{:S(2)}, u32[]{:S(2)}) async-start(f32[64,8,16,128]{3,2,1,0:T(8,128)} %shard_map.86.refs_5_), calls=%async_computation.3 | async-start | bytes 8388608 | tf_op jit(solution)/shard_map/all_to_all | solution.py:577
  316.1 31.2 %collective-permute-start.14 = (f32[8,256,128]{2,1,0:T(8,128)}, f32[8,256,128]{2,1,0:T(8,128)}, u32[]{:S(2)}, u32[]{:S(2)}) collective-permute-start(f32[8,256,128]{2,1,0:T(8,128)} %get-tuple-element.129), channel_id=1, source_target_pairs={{0,24},{8,16},{16,8},{24,0},{1,25},{9,17},{17,9},{25,1},{2,26},{10... | collective-permute-start | bytes 3145736 | tf_op jit(solution)/shard_map/ppermute | solution.py:468
  316.2 32.6 %collective-permute-start.21 = (f32[8,256,128]{2,1,0:T(8,128)}, f32[8,256,128]{2,1,0:T(8,128)}, u32[]{:S(2)}, u32[]{:S(2)}) collective-permute-start(f32[8,256,128]{2,1,0:T(8,128)} %get-tuple-element.146), channel_id=1, source_target_pairs={{0,8},{8,0},{16,24},{24,16},{1,9},{9,1},{17,25},{25,17},{2,10},{10... | collective-permute-start | bytes 3145736 | tf_op jit(solution)/shard_map/ppermute | solution.py:468
  316.8 53.4 %collective-permute-start.22 = (f32[8,256,128]{2,1,0:T(8,128)}, f32[8,256,128]{2,1,0:T(8,128)}, u32[]{:S(2)}, u32[]{:S(2)}) collective-permute-start(f32[8,256,128]{2,1,0:T(8,128)} %get-tuple-element.147), channel_id=1, source_target_pairs={{0,16},{8,24},{16,0},{24,8},{1,17},{9,25},{17,1},{25,9},{2,18},{10... | collective-permute-start | bytes 3145736 | tf_op jit(solution)/shard_map/ppermute | solution.py:468
  336.1 56.0 %collective-permute-start.23 = (f32[8,256,128]{2,1,0:T(8,128)}, f32[8,256,128]{2,1,0:T(8,128)S(1)}, u32[]{:S(2)}, u32[]{:S(2)}) collective-permute-start(f32[8,256,128]{2,1,0:T(8,128)} %get-tuple-element.148), channel_id=1, source_target_pairs={{0,24},{8,16},{16,8},{24,0},{1,25},{9,17},{17,9},{25,1},{2,26},{10... | collective-permute-start | bytes 3145736 | tf_op jit(solution)/shard_map/ppermute | solution.py:468
  336.1 61.1 %collective-permute-start.27 = (f32[8,256,128]{2,1,0:T(8,128)}, f32[8,256,128]{2,1,0:T(8,128)S(1)}, u32[]{:S(2)}, u32[]{:S(2)}) collective-permute-start(f32[8,256,128]{2,1,0:T(8,128)} %get-tuple-element.160), channel_id=1, source_target_pairs={{0,8},{8,0},{16,24},{24,16},{1,9},{9,1},{17,25},{25,17},{2,10},{10... | collective-permute-start | bytes 3145736 | tf_op jit(solution)/shard_map/ppermute | solution.py:468
  347.3 67.8 %collective-permute-start.28 = (f32[8,256,128]{2,1,0:T(8,128)}, f32[8,256,128]{2,1,0:T(8,128)S(1)}, u32[]{:S(2)}, u32[]{:S(2)}) collective-permute-start(f32[8,256,128]{2,1,0:T(8,128)} %get-tuple-element.161), channel_id=1, source_target_pairs={{0,16},{8,24},{16,0},{24,8},{1,17},{9,25},{17,1},{25,9},{2,18},{10... | collective-permute-start | bytes 3145736 | tf_op jit(solution)/shard_map/ppermute | solution.py:468
  348.8 88.4 %collective-permute-start.29 = (f32[8,256,128]{2,1,0:T(8,128)}, f32[8,256,128]{2,1,0:T(8,128)}, u32[]{:S(2)}, u32[]{:S(2)}) collective-permute-start(f32[8,256,128]{2,1,0:T(8,128)} %get-tuple-element.162), channel_id=1, source_target_pairs={{0,24},{8,16},{16,8},{24,0},{1,25},{9,17},{17,9},{25,1},{2,26},{10... | collective-permute-start | bytes 3145736 | tf_op jit(solution)/shard_map/ppermute | solution.py:468
  370.3 94.8 %collective-permute-start.24 = (f32[8,256,128]{2,1,0:T(8,128)}, f32[8,256,128]{2,1,0:T(8,128)}, u32[]{:S(2)}, u32[]{:S(2)}) collective-permute-start(f32[8,256,128]{2,1,0:T(8,128)} %get-tuple-element.153), channel_id=1, source_target_pairs={{0,8},{8,0},{16,24},{24,16},{1,9},{9,1},{17,25},{25,17},{2,10},{10... | collective-permute-start | bytes 3145736 | tf_op jit(solution)/shard_map/ppermute | solution.py:468
  392.1 73.0 %collective-permute-start.25 = (f32[8,256,128]{2,1,0:T(8,128)}, f32[8,256,128]{2,1,0:T(8,128)}, u32[]{:S(2)}, u32[]{:S(2)}) collective-permute-start(f32[8,256,128]{2,1,0:T(8,128)} %get-tuple-element.154), channel_id=1, source_target_pairs={{0,16},{8,24},{16,0},{24,8},{1,17},{9,25},{17,1},{25,9},{2,18},{10... | collective-permute-start | bytes 3145736 | tf_op jit(solution)/shard_map/ppermute | solution.py:468
  397.3 39.9 %copy-start.4 = (f32[8,256,128]{2,1,0:T(8,128)}, f32[8,256,128]{2,1,0:T(8,128)S(1)}, u32[]{:S(2)}) copy-start(f32[8,256,128]{2,1,0:T(8,128)S(1)} %collective-permute-done.27.refs_1_) | copy-start | bytes 3145732
  397.3 84.8 %collective-permute-start.26 = (f32[8,256,128]{2,1,0:T(8,128)}, f32[8,256,128]{2,1,0:T(8,128)}, u32[]{:S(2)}, u32[]{:S(2)}) collective-permute-start(f32[8,256,128]{2,1,0:T(8,128)} %get-tuple-element.155), channel_id=1, source_target_pairs={{0,24},{8,16},{16,8},{24,0},{1,25},{9,17},{17,9},{25,1},{2,26},{10... | collective-permute-start | bytes 3145736 | tf_op jit(solution)/shard_map/ppermute | solution.py:468
  440.8 99.8 %all-to-all-start.2 = ((f32[64,8,16,128]{3,2,1,0:T(8,128)}), f32[64,8,16,128]{3,2,1,0:T(8,128)}, u32[]{:S(2)}, u32[]{:S(2)}) async-start(f32[64,8,16,128]{3,2,1,0:T(8,128)} %shard_map.89.refs_4_), calls=%async_computation.2 | async-start | bytes 8388608 | tf_op jit(solution)/shard_map/all_to_all | solution.py:577
  482.1 76.3 %collective-permute-start.30 = (f32[8,256,128]{2,1,0:T(8,128)}, f32[8,256,128]{2,1,0:T(8,128)}, u32[]{:S(2)}, u32[]{:S(2)}) collective-permute-start(f32[8,256,128]{2,1,0:T(8,128)} %get-tuple-element.169), channel_id=1, source_target_pairs={{0,8},{8,0},{16,24},{24,16},{1,9},{9,1},{17,25},{25,17},{2,10},{10... | collective-permute-start | bytes 3145736 | tf_op jit(solution)/shard_map/ppermute | solution.py:468
  482.5 75.9 %collective-permute-start.31 = (f32[8,256,128]{2,1,0:T(8,128)}, f32[8,256,128]{2,1,0:T(8,128)}, u32[]{:S(2)}, u32[]{:S(2)}) collective-permute-start(f32[8,256,128]{2,1,0:T(8,128)} %get-tuple-element.170), channel_id=1, source_target_pairs={{0,16},{8,24},{16,0},{24,8},{1,17},{9,25},{17,1},{25,9},{2,18},{10... | collective-permute-start | bytes 3145736 | tf_op jit(solution)/shard_map/ppermute | solution.py:468
  484.0 74.4 %collective-permute-start.32 = (f32[8,256,128]{2,1,0:T(8,128)}, f32[8,256,128]{2,1,0:T(8,128)}, u32[]{:S(2)}, u32[]{:S(2)}) collective-permute-start(f32[8,256,128]{2,1,0:T(8,128)} %get-tuple-element.171), channel_id=1, source_target_pairs={{0,24},{8,16},{16,8},{24,0},{1,25},{9,17},{17,9},{25,1},{2,26},{10... | collective-permute-start | bytes 3145736 | tf_op jit(solution)/shard_map/ppermute | solution.py:468
  558.4 49.0 %collective-permute-start.33 = (f32[8,256,128]{2,1,0:T(8,128)}, f32[8,256,128]{2,1,0:T(8,128)S(1)}, u32[]{:S(2)}, u32[]{:S(2)}) collective-permute-start(f32[8,256,128]{2,1,0:T(8,128)} %get-tuple-element.173), channel_id=1, source_target_pairs={{0,8},{8,0},{16,24},{24,16},{1,9},{9,1},{17,25},{25,17},{2,10},{10... | collective-permute-start | bytes 3145736 | tf_op jit(solution)/shard_map/ppermute | solution.py:468
  558.5 48.9 %collective-permute-start.34 = (f32[8,256,128]{2,1,0:T(8,128)}, f32[8,256,128]{2,1,0:T(8,128)S(1)}, u32[]{:S(2)}, u32[]{:S(2)}) collective-permute-start(f32[8,256,128]{2,1,0:T(8,128)} %get-tuple-element.174), channel_id=1, source_target_pairs={{0,16},{8,24},{16,0},{24,8},{1,17},{9,25},{17,1},{25,9},{2,18},{10... | collective-permute-start | bytes 3145736 | tf_op jit(solution)/shard_map/ppermute | solution.py:468
  560.1 47.3 %collective-permute-start.35 = (f32[8,256,128]{2,1,0:T(8,128)}, f32[8,256,128]{2,1,0:T(8,128)S(1)}, u32[]{:S(2)}, u32[]{:S(2)}) collective-permute-start(f32[8,256,128]{2,1,0:T(8,128)} %get-tuple-element.175), channel_id=1, source_target_pairs={{0,24},{8,16},{16,8},{24,0},{1,25},{9,17},{17,9},{25,1},{2,26},{10... | collective-permute-start | bytes 3145736 | tf_op jit(solution)/shard_map/ppermute | solution.py:468
  562.7 1.4 collective-permute-start.36
  564.8 3.6 collective-permute-start.37
  568.4 3.6 collective-permute-start.38
  572.0 4.5 collective-permute-start.39
  576.5 30.3 %collective-permute-start.40 = (f32[4,64]{1,0:T(4,128)S(1)}, f32[4,64]{1,0:T(4,128)S(1)}, u32[]{:S(2)}, u32[]{:S(2)}) collective-permute-start(f32[4,64]{1,0:T(4,128)S(1)} %add.18), channel_id=1, source_target_pairs={{0,16},{8,24},{16,0},{24,8},{1,17},{9,25},{17,1},{25,9},{2,18},{10... | collective-permute-start | bytes 3080 | tf_op jit(solution)/shard_map/ppermute | solution.py:512
  (11 other events, 102.2 us)

commit v3 on v2

--- a/solution.py
+++ b/solution.py
@@ -577,10 +577,9 @@
         fields.append(lax.all_to_all(field, "dev", split_axis=0, concat_axis=0, tiled=True))
     whole = None
     for chunk in range(chunks):
-        while len(made) < min(chunk + 2, chunks):
-            waited = list(made[-2][1:]) if len(made) > 1 else []
-            close(len(made), [whole] if 0 < chunk == chunks - 2 else waited)
-        whole = place_pieces(made[chunk], seats, whole, chunk, shape, size, field)
+        while len(made) < min(max(chunk + 2, chunks - 1), chunks):
+            close(len(made), [whole] if 0 < chunk == chunks - 2 else [])
+        whole = place_pieces(made[chunk], seats, whole, chunk, shape, size, closed[-1][0])
     grad = grand_total(device_grad(grads, seats, parts, []))
     return whole.reshape(costate.shape), grad.reshape(2, 2, LEVELS)
 

time: 615 us -> 594 us (0.966)
  waiting for transfers between devices: 383 us -> 355 us
  starting transfers between devices: 54.8 us -> 61.2 us
    all_to_all x4, waiting for transfers between devices: 67.7 us -> 23.1 us  [per_device(): lax.all_to_all(field, 'dev', split_axis=0, concat_axis=0, tiled=True)]
    ppermute x36, waiting for transfers between devices: 280 us -> 301 us  [swap(): moved.append(lax.ppermute(pieces[step], 'grp', pairs))]
  transfers between devices with their start and end apart: 45 -> 45, of which waited for: 23 -> 22; matrix products, arithmetic and copies ran while one was open for 0% -> 0% of each run, Pallas kernels for 25% -> 26%
where the time goes in v3:
time: 594 us; the launch traced here: 592 us
  waiting for transfers between devices  355 us (60%)
  Pallas kernels  168 us (28%)
  starting transfers between devices  61.2 us (10%)
    ppermute x36, waiting for transfers between devices, swap(): moved.append(lax.ppermute(pieces[step], 'grp', pairs))  301 us
    pallas_call x4, Pallas kernels, close_columns(): pl.pallas_call(functools.partial(close_kernel, parts, size), grid=(firsts...  71.3 us
    ppermute x5, waiting for transfers between devices, grand_total(): value = value + lax.ppermute(value, axis, pairs)  31 us
    pallas_call x4, Pallas kernels, turn_columns(): pl.pallas_call(functools.partial(turn_kernel, parts, size, group), grid=(...  30.2 us
    ppermute x36, starting transfers between devices, swap(): moved.append(lax.ppermute(pieces[step], 'grp', pairs))  29.6 us
    all_to_all x4, waiting for transfers between devices, per_device(): lax.all_to_all(field, 'dev', split_axis=0, concat_axis=0, tiled=True)  23.1 us
    all_to_all x4, starting transfers between devices, per_device(): lax.all_to_all(field, 'dev', split_axis=0, concat_axis=0, tiled=True)  22.9 us
    pallas_call x1, Pallas kernels, open_state(): pl.pallas_call(functools.partial(open_kernel, count, len(waited)), grid=(...  19.5 us
  transfers between devices with their start and end apart: 45, of which 22 were waited for; matrix products, arithmetic and copies ran while one was open for 0% of the time, Pallas kernels for 26%

profile of v3, /device:TPU:0, one launch (start us, length us, event | category | flops | bytes accessed | tf_op | source)
XLA Modules:
  0.0 592.3 jit_solution(7567686194790921492)
XLA Ops:
  0.6 3.8 shard_map.82
  4.4 2.9 collective-permute-start.6
  8.0 4.6 shard_map.77
  12.6 10.4 %shard_map.78 = (f32[8,256,128]{2,1,0:T(8,128)}, f32[8,256,128]{2,1,0:T(8,128)}, f32[8,256,128]{2,1,0:T(8,128)}, f32[8,256,128]{2,1,0:T(8,128)}) custom-call(bf16[512,128]{1,0:T(8,128)(2,1)} %get-tuple-element.97.weight_ref, f32[2,1024,2048]{2,1,0:T(8,128)} %field_ref.3), custom_call_target="tpu_custom_call" | custom-call | flops 1024 | bytes 1024 | tf_op jit(solution)/shard_map/pallas_call | solution.py:210
  23.0 7.7 %collective-permute-done.6.refs_2_ = f32[8,256,128]{2,1,0:T(8,128)S(1)} collective-permute-done((f32[8,256,128]{2,1,0:T(8,128)}, f32[8,256,128]{2,1,0:T(8,128)S(1)}, u32[]{:S(2)}, u32[]{:S(2)}) %collective-permute-start.6) | collective-permute-done | bytes 1048608 | tf_op jit(solution)/shard_map/ppermute | solution.py:468
  34.3 19.5 %shard_map.79 = (f32[8,256,128]{2,1,0:T(8,128)}, f32[8,256,128]{2,1,0:T(8,128)}, f32[8,256,128]{2,1,0:T(8,128)}, f32[8,256,128]{2,1,0:T(8,128)}, f32[8,256,128]{...) custom-call(bf16[2,192,256]{2,1,0:T(8,128)(2,1)} %slice.3.weight_ref, ...), custom_call_target="tpu_custom_call" | custom-call | flops 1024 | bytes 1024 | tf_op jit(solution)/shard_map/pallas_call | solution.py:235
  53.8 4.1 collective-permute-done.8.refs_2_
  57.9 21.7 %collective-permute-done.9.refs_3_ = f32[8,256,128]{2,1,0:T(8,128)S(1)} collective-permute-done((f32[8,256,128]{2,1,0:T(8,128)}, f32[8,256,128]{2,1,0:T(8,128)S(1)}, u32[]{:S(2)}, u32[]{:S(2)}) %collective-permute-start.9) | collective-permute-done | bytes 1048608 | tf_op jit(solution)/shard_map/ppermute | solution.py:468
  80.6 7.5 %shard_map.83.refs_5_ = f32[64,8,16,128]{3,2,1,0:T(8,128)} custom-call(bf16[256,256]{1,0:T(8,128)(2,1)} %get-tuple-element.95.weight_ref, f32[8,256,128]{2,1,0:T(8,128)} %get-tuple-element.117.refs_0_, f32[8,256,128]{2,1,0:T(8,128)} %copy-done.8, f32[8,256,128]{2,1,0:T(8,128)} %copy-done.9, f32[8,256,128]{2,1,0:T(8,128)} %copy-done.10, ...), custom_call_target="tpu_custom_call" | custom-call | flops 1024 | bytes 1024 | tf_op jit(solution)/shard_map/pallas_call | solution.py:336
  88.1 6.1 %all-to-all-start = ((f32[64,8,16,128]{3,2,1,0:T(8,128)}), f32[64,8,16,128]{3,2,1,0:T(8,128)}, u32[]{:S(2)}, u32[]{:S(2)}) async-start(f32[64,8,16,128]{3,2,1,0:T(8,128)} %shard_map.83.refs_5_), calls=%async_computation | async-start | bytes 8388608 | tf_op jit(solution)/shard_map/all_to_all | solution.py:577
  98.0 3.7 shard_map.81
  101.7 3.7 shard_map.80
  105.4 15.0 %collective-permute-done.4.refs_2_ = f32[8,256,128]{2,1,0:T(8,128)S(1)} collective-permute-done((f32[8,256,128]{2,1,0:T(8,128)}, f32[8,256,128]{2,1,0:T(8,128)S(1)}, u32[]{:S(2)}, u32[]{:S(2)}) %collective-permute-start.4) | collective-permute-done | bytes 1048608 | tf_op jit(solution)/shard_map/ppermute | solution.py:468
  121.9 20.1 %collective-permute-done.5.refs_3_ = f32[8,256,128]{2,1,0:T(8,128)S(1)} collective-permute-done((f32[8,256,128]{2,1,0:T(8,128)}, f32[8,256,128]{2,1,0:T(8,128)S(1)}, u32[]{:S(2)}, u32[]{:S(2)}) %collective-permute-start.5) | collective-permute-done | bytes 1048608 | tf_op jit(solution)/shard_map/ppermute | solution.py:468
  142.0 2.2 collective-permute-start.2
  144.2 7.5 %shard_map.84.refs_5_ = f32[64,8,16,128]{3,2,1,0:T(8,128)} custom-call(bf16[256,256]{1,0:T(8,128)(2,1)} %get-tuple-element.95.weight_ref, f32[8,256,128]{2,1,0:T(8,128)} %get-tuple-element.108.refs_5_.refs_0_, f32[8,256,128]{2,1,0:T(8,128)} %copy-done.5, f32[8,256,128]{2,1,0:T(8,128)} %copy-done.6, f32[8,256,128]{2,1,0:T(8,128)} %copy-done.7, ...), custom_call_target="tpu_custom_call" | custom-call | flops 1024 | bytes 1024 | tf_op jit(solution)/shard_map/pallas_call | solution.py:336
  151.8 12.8 %collective-permute-done.11.refs_3_ = f32[8,256,128]{2,1,0:T(8,128)} collective-permute-done((f32[8,256,128]{2,1,0:T(8,128)}, f32[8,256,128]{2,1,0:T(8,128)}, u32[]{:S(2)}, u32[]{:S(2)}) %collective-permute-start.11) | collective-permute-done | bytes 1048608 | tf_op jit(solution)/shard_map/ppermute | solution.py:468
  166.6 21.2 %all-to-all-done = f32[64,8,16,128]{3,2,1,0:T(8,128)} async-done(((f32[64,8,16,128]{3,2,1,0:T(8,128)}), f32[64,8,16,128]{3,2,1,0:T(8,128)}, u32[]{:S(2)}, u32[]{:S(2)}) %all-to-all-start) | async-done | bytes 4194336 | tf_op jit(solution)/shard_map/all_to_all | solution.py:577
  187.8 4.8 all-to-all-start.1
  192.6 17.8 %shard_map.85 = (f32[8,256,128]{2,1,0:T(8,128)}, f32[8,256,128]{2,1,0:T(8,128)}, f32[8,256,128]{2,1,0:T(8,128)}, f32[8,256,128]{2,1,0:T(8,128)}, f32[2,64,128]{2,1,0:T(8,128)}) custom-call(bf16[3,2,256,256]{3,2,1,0:T(8,128)(2,1)} %get-tuple-element.93.lane_ref, bf16[3,256,256]{2,1,0:T(8,128)(2,1)} %get-tuple-element.94.level_ref, ...), custom_call_target="tpu_custom_call" | custom-call | flops 199999995904 | bytes 1024 | tf_op jit(solution)/shard_map/pallas_call | solution.py:408
  212.0 7.6 %shard_map.86.refs_5_ = f32[64,8,16,128]{3,2,1,0:T(8,128)} custom-call(bf16[256,256]{1,0:T(8,128)(2,1)} %get-tuple-element.95.weight_ref, f32[8,256,128]{2,1,0:T(8,128)} %get-tuple-element.103.refs_0_, f32[8,256,128]{2,1,0:T(8,128)} %collective-permute-done.refs_1_, f32[8,256,128]{2,1,0:T(8,128)} %collective-permute-done.1.refs_2_, ...), custom_call_target="tpu_custom_call" | custom-call | flops 1024 | bytes 1024 | tf_op jit(solution)/shard_map/pallas_call | solution.py:336
  219.9 12.9 %collective-permute-done.19.refs_2_ = f32[8,256,128]{2,1,0:T(8,128)} collective-permute-done((f32[8,256,128]{2,1,0:T(8,128)}, f32[8,256,128]{2,1,0:T(8,128)}, u32[]{:S(2)}, u32[]{:S(2)}) %collective-permute-start.19) | collective-permute-done | bytes 1048608 | tf_op jit(solution)/shard_map/ppermute | solution.py:468
  232.9 21.5 %collective-permute-done.20.refs_3_ = f32[8,256,128]{2,1,0:T(8,128)} collective-permute-done((f32[8,256,128]{2,1,0:T(8,128)}, f32[8,256,128]{2,1,0:T(8,128)}, u32[]{:S(2)}, u32[]{:S(2)}) %collective-permute-start.20) | collective-permute-done | bytes 1048608 | tf_op jit(solution)/shard_map/ppermute | solution.py:468
  255.9 3.7 shard_map.87
  260.3 17.5 %collective-permute-done.16.refs_2_ = f32[8,256,128]{2,1,0:T(8,128)} collective-permute-done((f32[8,256,128]{2,1,0:T(8,128)}, f32[8,256,128]{2,1,0:T(8,128)}, u32[]{:S(2)}, u32[]{:S(2)}) %collective-permute-start.16) | collective-permute-done | bytes 1048608 | tf_op jit(solution)/shard_map/ppermute | solution.py:468
  279.3 20.0 %collective-permute-done.17.refs_3_ = f32[8,256,128]{2,1,0:T(8,128)} collective-permute-done((f32[8,256,128]{2,1,0:T(8,128)}, f32[8,256,128]{2,1,0:T(8,128)}, u32[]{:S(2)}, u32[]{:S(2)}) %collective-permute-start.17) | collective-permute-done | bytes 1048608 | tf_op jit(solution)/shard_map/ppermute | solution.py:468
  301.2 5.9 all-to-all-start.3
  307.2 15.4 %collective-permute-done.13.refs_2_ = f32[8,256,128]{2,1,0:T(8,128)S(1)} collective-permute-done((f32[8,256,128]{2,1,0:T(8,128)S(1)}, f32[8,256,128]{2,1,0:T(8,128)S(1)}, u32[]{:S(2)}, u32[]{:S(2)}) %collective-permute-start.13) | collective-permute-done | bytes 1048608 | tf_op jit(solution)/shard_map/ppermute | solution.py:468
  322.6 18.1 %shard_map.88 = (f32[8,256,128]{2,1,0:T(8,128)}, f32[8,256,128]{2,1,0:T(8,128)}, f32[8,256,128]{2,1,0:T(8,128)}, f32[8,256,128]{2,1,0:T(8,128)}, f32[2,64,128]{2,1,0:T(8,128)}) custom-call(bf16[3,2,256,256]{3,2,1,0:T(8,128)(2,1)} %get-tuple-element.93.lane_ref, bf16[3,256,256]{2,1,0:T(8,128)(2,1)} %get-tuple-element.94.level_ref, ...), custom_call_target="tpu_custom_call" | custom-call | flops 199999995904 | bytes 1024 | tf_op jit(solution)/shard_map/pallas_call | solution.py:408
  340.7 48.5 %collective-permute-done.14.refs_3_ = f32[8,256,128]{2,1,0:T(8,128)} collective-permute-done((f32[8,256,128]{2,1,0:T(8,128)}, f32[8,256,128]{2,1,0:T(8,128)}, u32[]{:S(2)}, u32[]{:S(2)}) %collective-permute-start.14) | collective-permute-done | bytes 1048608 | tf_op jit(solution)/shard_map/ppermute | solution.py:468
  389.5 7.6 %shard_map.89 = f32[64,8,16,128]{3,2,1,0:T(8,128)} custom-call(bf16[256,256]{1,0:T(8,128)(2,1)} %get-tuple-element.95.weight_ref, f32[8,256,128]{2,1,0:T(8,128)} %get-tuple-element.126.refs_0_, f32[8,256,128]{2,1,0:T(8,128)} %copy-done, f32[8,256,128]{2,1,0:T(8,128)} %copy-done.1, f32[8,256,128]{2,1,0:T(8,128)} %collective-permute-done.14.refs_3_, ...), custom_call_target="tpu_custom_call" | custom-call | flops 1024 | bytes 1024 | tf_op jit(solution)/shard_map/pallas_call | solution.py:336
  400.7 6.2 %all-to-all-start.2 = ((f32[64,8,16,128]{3,2,1,0:T(8,128)}), f32[64,8,16,128]{3,2,1,0:T(8,128)}, u32[]{:S(2)}, u32[]{:S(2)}) async-start(f32[64,8,16,128]{3,2,1,0:T(8,128)} %shard_map.89), calls=%async_computation.2 | async-start | bytes 8388608 | tf_op jit(solution)/shard_map/all_to_all | solution.py:577
  406.9 17.8 %shard_map.90 = (f32[8,256,128]{2,1,0:T(8,128)}, f32[8,256,128]{2,1,0:T(8,128)}, f32[8,256,128]{2,1,0:T(8,128)}, f32[8,256,128]{2,1,0:T(8,128)}, f32[2,64,128]{2,1,0:T(8,128)}) custom-call(bf16[3,2,256,256]{3,2,1,0:T(8,128)(2,1)} %get-tuple-element.93.lane_ref, bf16[3,256,256]{2,1,0:T(8,128)(2,1)} %get-tuple-element.94.level_ref, ...), custom_call_target="tpu_custom_call" | custom-call | flops 199999995904 | bytes 1024 | tf_op jit(solution)/shard_map/pallas_call | solution.py:408
  424.7 43.7 %collective-permute-done.28.refs_2_ = f32[8,256,128]{2,1,0:T(8,128)} collective-permute-done((f32[8,256,128]{2,1,0:T(8,128)}, f32[8,256,128]{2,1,0:T(8,128)}, u32[]{:S(2)}, u32[]{:S(2)}) %collective-permute-start.28) | collective-permute-done | bytes 1048608 | tf_op jit(solution)/shard_map/ppermute | solution.py:468
  468.4 21.0 %collective-permute-done.29.refs_3_ = f32[8,256,128]{2,1,0:T(8,128)} collective-permute-done((f32[8,256,128]{2,1,0:T(8,128)}, f32[8,256,128]{2,1,0:T(8,128)}, u32[]{:S(2)}, u32[]{:S(2)}) %collective-permute-start.29) | collective-permute-done | bytes 1048608 | tf_op jit(solution)/shard_map/ppermute | solution.py:468
  490.7 3.7 shard_map.91.refs_4_
  495.0 3.7 shard_map.92.refs_4_
  498.6 1.9 all-to-all-done.2
  500.6 17.7 %shard_map.93 = (f32[8,256,128]{2,1,0:T(8,128)}, f32[8,256,128]{2,1,0:T(8,128)}, f32[8,256,128]{2,1,0:T(8,128)}, f32[8,256,128]{2,1,0:T(8,128)}, f32[2,64,128]{2,1,0:T(8,128)}) custom-call(bf16[3,2,256,256]{3,2,1,0:T(8,128)(2,1)} %get-tuple-element.93.lane_ref, bf16[3,256,256]{2,1,0:T(8,128)(2,1)} %get-tuple-element.94.level_ref, ...), custom_call_target="tpu_custom_call" | custom-call | flops 199999995904 | bytes 1024 | tf_op jit(solution)/shard_map/pallas_call | solution.py:408
  518.3 19.1 %collective-permute-done.32.refs_3_ = f32[8,256,128]{2,1,0:T(8,128)} collective-permute-done((f32[8,256,128]{2,1,0:T(8,128)}, f32[8,256,128]{2,1,0:T(8,128)}, u32[]{:S(2)}, u32[]{:S(2)}) %collective-permute-start.32) | collective-permute-done | bytes 1048608 | tf_op jit(solution)/shard_map/ppermute | solution.py:468
  539.3 2.4 shard_map.96
  543.9 2.6 collective-permute-start.37
  549.7 1.9 collective-permute-done.38
  551.6 2.5 collective-permute-start.39
  554.0 2.0 collective-permute-done.39
  557.5 3.7 shard_map.94.refs_4_
  561.2 24.5 %collective-permute-done.40 = f32[4,64]{1,0:T(4,128)S(1)} collective-permute-done((f32[4,64]{1,0:T(4,128)S(1)}, f32[4,64]{1,0:T(4,128)S(1)}, u32[]{:S(2)}, u32[]{:S(2)}) %collective-permute-start.40) | collective-permute-done | bytes 1056 | tf_op jit(solution)/shard_map/ppermute | solution.py:512
  588.7 3.7 shard_map.95
  (96 shorter events, 37.0 us)
Async XLA Ops:
  4.4 26.3 %collective-permute-start.6 = (f32[8,256,128]{2,1,0:T(8,128)}, f32[8,256,128]{2,1,0:T(8,128)S(1)}, u32[]{:S(2)}, u32[]{:S(2)}) collective-permute-start(f32[8,256,128]{2,1,0:T(8,128)} %get-tuple-element.116), channel_id=1, source_target_pairs={{0,16},{8,24},{16,0},{24,8},{1,17},{9,25},{17,1},{25,9},{2,18},{10... | collective-permute-start | bytes 3145736 | tf_op jit(solution)/shard_map/ppermute | solution.py:468
  31.7 22.1 %collective-permute-start.7 = (f32[8,256,128]{2,1,0:T(8,128)}, f32[8,256,128]{2,1,0:T(8,128)S(1)}, u32[]{:S(2)}, u32[]{:S(2)}) collective-permute-start(f32[8,256,128]{2,1,0:T(8,128)} %get-tuple-element.118), channel_id=1, source_target_pairs={{0,8},{8,0},{16,24},{24,16},{1,9},{9,1},{17,25},{25,17},{2,10},{10... | collective-permute-start | bytes 3145736 | tf_op jit(solution)/shard_map/ppermute | solution.py:468
  31.7 26.2 %collective-permute-start.8 = (f32[8,256,128]{2,1,0:T(8,128)}, f32[8,256,128]{2,1,0:T(8,128)S(1)}, u32[]{:S(2)}, u32[]{:S(2)}) collective-permute-start(f32[8,256,128]{2,1,0:T(8,128)} %get-tuple-element.119), channel_id=1, source_target_pairs={{0,16},{8,24},{16,0},{24,8},{1,17},{9,25},{17,1},{25,9},{2,18},{10... | collective-permute-start | bytes 3145736 | tf_op jit(solution)/shard_map/ppermute | solution.py:468
  33.5 46.1 %collective-permute-start.9 = (f32[8,256,128]{2,1,0:T(8,128)}, f32[8,256,128]{2,1,0:T(8,128)S(1)}, u32[]{:S(2)}, u32[]{:S(2)}) collective-permute-start(f32[8,256,128]{2,1,0:T(8,128)} %get-tuple-element.120), channel_id=1, source_target_pairs={{0,24},{8,16},{16,8},{24,0},{1,25},{9,17},{17,9},{25,1},{2,26},{10... | collective-permute-start | bytes 3145736 | tf_op jit(solution)/shard_map/ppermute | solution.py:468
  53.8 25.8 %copy-start.8 = (f32[8,256,128]{2,1,0:T(8,128)}, f32[8,256,128]{2,1,0:T(8,128)S(1)}, u32[]{:S(2)}) copy-start(f32[8,256,128]{2,1,0:T(8,128)S(1)} %collective-permute-done.7.refs_1_) | copy-start | bytes 3145732
  88.1 99.8 %all-to-all-start = ((f32[64,8,16,128]{3,2,1,0:T(8,128)}), f32[64,8,16,128]{3,2,1,0:T(8,128)}, u32[]{:S(2)}, u32[]{:S(2)}) async-start(f32[64,8,16,128]{3,2,1,0:T(8,128)} %shard_map.83.refs_5_), calls=%async_computation | async-start | bytes 8388608 | tf_op jit(solution)/shard_map/all_to_all | solution.py:577
  94.2 3.5 collective-permute-start.3
  94.2 26.2 %collective-permute-start.4 = (f32[8,256,128]{2,1,0:T(8,128)}, f32[8,256,128]{2,1,0:T(8,128)S(1)}, u32[]{:S(2)}, u32[]{:S(2)}) collective-permute-start(f32[8,256,128]{2,1,0:T(8,128)} %get-tuple-element.110), channel_id=1, source_target_pairs={{0,16},{8,24},{16,0},{24,8},{1,17},{9,25},{17,1},{25,9},{2,18},{10... | collective-permute-start | bytes 3145736 | tf_op jit(solution)/shard_map/ppermute | solution.py:468
  95.7 46.3 %collective-permute-start.5 = (f32[8,256,128]{2,1,0:T(8,128)}, f32[8,256,128]{2,1,0:T(8,128)S(1)}, u32[]{:S(2)}, u32[]{:S(2)}) collective-permute-start(f32[8,256,128]{2,1,0:T(8,128)} %get-tuple-element.111), channel_id=1, source_target_pairs={{0,24},{8,16},{16,8},{24,0},{1,25},{9,17},{17,9},{25,1},{2,26},{10... | collective-permute-start | bytes 3145736 | tf_op jit(solution)/shard_map/ppermute | solution.py:468
  96.0 55.7 %collective-permute-start.10 = (f32[8,256,128]{2,1,0:T(8,128)}, f32[8,256,128]{2,1,0:T(8,128)}, u32[]{:S(2)}, u32[]{:S(2)}) collective-permute-start(f32[8,256,128]{2,1,0:T(8,128)} %get-tuple-element.122), channel_id=1, source_target_pairs={{0,8},{8,0},{16,24},{24,16},{1,9},{9,1},{17,25},{25,17},{2,10},{10... | collective-permute-start | bytes 3145736 | tf_op jit(solution)/shard_map/ppermute | solution.py:468
  96.4 68.1 %collective-permute-start.11 = (f32[8,256,128]{2,1,0:T(8,128)}, f32[8,256,128]{2,1,0:T(8,128)}, u32[]{:S(2)}, u32[]{:S(2)}) collective-permute-start(f32[8,256,128]{2,1,0:T(8,128)} %get-tuple-element.124), channel_id=1, source_target_pairs={{0,24},{8,16},{16,8},{24,0},{1,25},{9,17},{17,9},{25,1},{2,26},{10... | collective-permute-start | bytes 3145736 | tf_op jit(solution)/shard_map/ppermute | solution.py:468
  97.6 68.4 %collective-permute-start = (f32[8,256,128]{2,1,0:T(8,128)}, f32[8,256,128]{2,1,0:T(8,128)}, u32[]{:S(2)}, u32[]{:S(2)}) collective-permute-start(f32[8,256,128]{2,1,0:T(8,128)} %get-tuple-element.104), channel_id=1, source_target_pairs={{0,8},{8,0},{16,24},{24,16},{1,9},{9,1},{17,25},{25,17},{2,10},{10... | collective-permute-start | bytes 3145736 | tf_op jit(solution)/shard_map/ppermute | solution.py:468
  120.4 90.0 %collective-permute-start.1 = (f32[8,256,128]{2,1,0:T(8,128)}, f32[8,256,128]{2,1,0:T(8,128)}, u32[]{:S(2)}, u32[]{:S(2)}) collective-permute-start(f32[8,256,128]{2,1,0:T(8,128)} %get-tuple-element.105), channel_id=1, source_target_pairs={{0,16},{8,24},{16,0},{24,8},{1,17},{9,25},{17,1},{25,9},{2,18},{10... | collective-permute-start | bytes 3145736 | tf_op jit(solution)/shard_map/ppermute | solution.py:468
  142.0 68.5 %collective-permute-start.2 = (f32[8,256,128]{2,1,0:T(8,128)}, f32[8,256,128]{2,1,0:T(8,128)}, u32[]{:S(2)}, u32[]{:S(2)}) collective-permute-start(f32[8,256,128]{2,1,0:T(8,128)} %get-tuple-element.106), channel_id=1, source_target_pairs={{0,24},{8,16},{16,8},{24,0},{1,25},{9,17},{17,9},{25,1},{2,26},{10... | collective-permute-start | bytes 3145736 | tf_op jit(solution)/shard_map/ppermute | solution.py:468
  151.8 67.9 %collective-permute-start.18 = (f32[8,256,128]{2,1,0:T(8,128)}, f32[8,256,128]{2,1,0:T(8,128)}, u32[]{:S(2)}, u32[]{:S(2)}) collective-permute-start(f32[8,256,128]{2,1,0:T(8,128)} %get-tuple-element.139), channel_id=1, source_target_pairs={{0,8},{8,0},{16,24},{24,16},{1,9},{9,1},{17,25},{25,17},{2,10},{10... | collective-permute-start | bytes 3145736 | tf_op jit(solution)/shard_map/ppermute | solution.py:468
  164.5 68.3 %collective-permute-start.19 = (f32[8,256,128]{2,1,0:T(8,128)}, f32[8,256,128]{2,1,0:T(8,128)}, u32[]{:S(2)}, u32[]{:S(2)}) collective-permute-start(f32[8,256,128]{2,1,0:T(8,128)} %get-tuple-element.140), channel_id=1, source_target_pairs={{0,16},{8,24},{16,0},{24,8},{1,17},{9,25},{17,1},{25,9},{2,18},{10... | collective-permute-start | bytes 3145736 | tf_op jit(solution)/shard_map/ppermute | solution.py:468
  166.0 88.4 %collective-permute-start.20 = (f32[8,256,128]{2,1,0:T(8,128)}, f32[8,256,128]{2,1,0:T(8,128)}, u32[]{:S(2)}, u32[]{:S(2)}) collective-permute-start(f32[8,256,128]{2,1,0:T(8,128)} %get-tuple-element.141), channel_id=1, source_target_pairs={{0,24},{8,16},{16,8},{24,0},{1,25},{9,17},{17,9},{25,1},{2,26},{10... | collective-permute-start | bytes 3145736 | tf_op jit(solution)/shard_map/ppermute | solution.py:468
  187.8 113.4 %all-to-all-start.1 = ((f32[64,8,16,128]{3,2,1,0:T(8,128)}), f32[64,8,16,128]{3,2,1,0:T(8,128)}, u32[]{:S(2)}, u32[]{:S(2)}) async-start(f32[64,8,16,128]{3,2,1,0:T(8,128)} %shard_map.84.refs_5_), calls=%async_computation.1 | async-start | bytes 8388608 | tf_op jit(solution)/shard_map/all_to_all | solution.py:577
  210.4 49.2 %collective-permute-start.15 = (f32[8,256,128]{2,1,0:T(8,128)}, f32[8,256,128]{2,1,0:T(8,128)}, u32[]{:S(2)}, u32[]{:S(2)}) collective-permute-start(f32[8,256,128]{2,1,0:T(8,128)} %get-tuple-element.132), channel_id=1, source_target_pairs={{0,8},{8,0},{16,24},{24,16},{1,9},{9,1},{17,25},{25,17},{2,10},{10... | collective-permute-start | bytes 3145736 | tf_op jit(solution)/shard_map/ppermute | solution.py:468
  210.5 67.3 %collective-permute-start.16 = (f32[8,256,128]{2,1,0:T(8,128)}, f32[8,256,128]{2,1,0:T(8,128)}, u32[]{:S(2)}, u32[]{:S(2)}) collective-permute-start(f32[8,256,128]{2,1,0:T(8,128)} %get-tuple-element.133), channel_id=1, source_target_pairs={{0,16},{8,24},{16,0},{24,8},{1,17},{9,25},{17,1},{25,9},{2,18},{10... | collective-permute-start | bytes 3145736 | tf_op jit(solution)/shard_map/ppermute | solution.py:468
  212.0 42.4 %copy-start.12 = (f32[8,256,128]{2,1,0:T(8,128)S(1)}, f32[8,256,128]{2,1,0:T(8,128)}, u32[]{:S(2)}) copy-start(f32[8,256,128]{2,1,0:T(8,128)} %get-tuple-element.128) | copy-start | bytes 3145732
  219.6 79.7 %collective-permute-start.17 = (f32[8,256,128]{2,1,0:T(8,128)}, f32[8,256,128]{2,1,0:T(8,128)}, u32[]{:S(2)}, u32[]{:S(2)}) collective-permute-start(f32[8,256,128]{2,1,0:T(8,128)} %get-tuple-element.134), channel_id=1, source_target_pairs={{0,24},{8,16},{16,8},{24,0},{1,25},{9,17},{17,9},{25,1},{2,26},{10... | collective-permute-start | bytes 3145736 | tf_op jit(solution)/shard_map/ppermute | solution.py:468
  232.9 74.3 %collective-permute-start.12 = (f32[8,256,128]{2,1,0:T(8,128)}, f32[8,256,128]{2,1,0:T(8,128)S(1)}, u32[]{:S(2)}, u32[]{:S(2)}) collective-permute-start(f32[8,256,128]{2,1,0:T(8,128)} %get-tuple-element.127), channel_id=1, source_target_pairs={{0,8},{8,0},{16,24},{24,16},{1,9},{9,1},{17,25},{25,17},{2,10},{10... | collective-permute-start | bytes 3145736 | tf_op jit(solution)/shard_map/ppermute | solution.py:468
  254.4 68.2 %collective-permute-start.13 = (f32[8,256,128]{2,1,0:T(8,128)S(1)}, f32[8,256,128]{2,1,0:T(8,128)S(1)}, u32[]{:S(2)}, u32[]{:S(2)}) collective-permute-start(f32[8,256,128]{2,1,0:T(8,128)S(1)} %copy-done.12), channel_id=1, source_target_pairs={{0,16},{8,24},{16,0},{24,8},{1,17},{9,25},{17,1},{25,9},{2,18},{10... | collective-permute-start | bytes 3145736 | tf_op jit(solution)/shard_map/ppermute | solution.py:468
  259.6 137.5 %collective-permute-start.21 = (f32[8,256,128]{2,1,0:T(8,128)}, f32[8,256,128]{2,1,0:T(8,128)}, u32[]{:S(2)}, u32[]{:S(2)}) collective-permute-start(f32[8,256,128]{2,1,0:T(8,128)} %get-tuple-element.150), channel_id=1, source_target_pairs={{0,8},{8,0},{16,24},{24,16},{1,9},{9,1},{17,25},{25,17},{2,10},{10... | collective-permute-start | bytes 3145736 | tf_op jit(solution)/shard_map/ppermute | solution.py:468
  277.8 121.1 %collective-permute-start.22 = (f32[8,256,128]{2,1,0:T(8,128)}, f32[8,256,128]{2,1,0:T(8,128)}, u32[]{:S(2)}, u32[]{:S(2)}) collective-permute-start(f32[8,256,128]{2,1,0:T(8,128)} %get-tuple-element.151), channel_id=1, source_target_pairs={{0,16},{8,24},{16,0},{24,8},{1,17},{9,25},{17,1},{25,9},{2,18},{10... | collective-permute-start | bytes 3145736 | tf_op jit(solution)/shard_map/ppermute | solution.py:468
  299.3 99.6 %collective-permute-start.23 = (f32[8,256,128]{2,1,0:T(8,128)}, f32[8,256,128]{2,1,0:T(8,128)}, u32[]{:S(2)}, u32[]{:S(2)}) collective-permute-start(f32[8,256,128]{2,1,0:T(8,128)} %get-tuple-element.152), channel_id=1, source_target_pairs={{0,24},{8,16},{16,8},{24,0},{1,25},{9,17},{17,9},{25,1},{2,26},{10... | collective-permute-start | bytes 3145736 | tf_op jit(solution)/shard_map/ppermute | solution.py:468
  301.2 99.5 %all-to-all-start.3 = ((f32[64,8,16,128]{3,2,1,0:T(8,128)}), f32[64,8,16,128]{3,2,1,0:T(8,128)}, u32[]{:S(2)}, u32[]{:S(2)}) async-start(f32[64,8,16,128]{3,2,1,0:T(8,128)} %shard_map.86.refs_5_), calls=%async_computation.3 | async-start | bytes 8388608 | tf_op jit(solution)/shard_map/all_to_all | solution.py:577
  307.1 33.6 %copy-start = (f32[8,256,128]{2,1,0:T(8,128)}, f32[8,256,128]{2,1,0:T(8,128)S(1)}, u32[]{:S(2)}) copy-start(f32[8,256,128]{2,1,0:T(8,128)S(1)} %collective-permute-done.12.refs_1_) | copy-start | bytes 3145732
  307.1 82.1 %collective-permute-start.14 = (f32[8,256,128]{2,1,0:T(8,128)}, f32[8,256,128]{2,1,0:T(8,128)}, u32[]{:S(2)}, u32[]{:S(2)}) collective-permute-start(f32[8,256,128]{2,1,0:T(8,128)} %get-tuple-element.129), channel_id=1, source_target_pairs={{0,24},{8,16},{16,8},{24,0},{1,25},{9,17},{17,9},{25,1},{2,26},{10... | collective-permute-start | bytes 3145736 | tf_op jit(solution)/shard_map/ppermute | solution.py:468
  322.6 77.6 %collective-permute-start.27 = (f32[8,256,128]{2,1,0:T(8,128)}, f32[8,256,128]{2,1,0:T(8,128)}, u32[]{:S(2)}, u32[]{:S(2)}) collective-permute-start(f32[8,256,128]{2,1,0:T(8,128)} %get-tuple-element.161), channel_id=1, source_target_pairs={{0,8},{8,0},{16,24},{24,16},{1,9},{9,1},{17,25},{25,17},{2,10},{10... | collective-permute-start | bytes 3145736 | tf_op jit(solution)/shard_map/ppermute | solution.py:468
  389.2 105.2 %collective-permute-start.24 = (f32[8,256,128]{2,1,0:T(8,128)}, f32[8,256,128]{2,1,0:T(8,128)}, u32[]{:S(2)}, u32[]{:S(2)}) collective-permute-start(f32[8,256,128]{2,1,0:T(8,128)} %get-tuple-element.157), channel_id=1, source_target_pairs={{0,8},{8,0},{16,24},{24,16},{1,9},{9,1},{17,25},{25,17},{2,10},{10... | collective-permute-start | bytes 3145736 | tf_op jit(solution)/shard_map/ppermute | solution.py:468
  397.1 97.9 %collective-permute-start.25 = (f32[8,256,128]{2,1,0:T(8,128)}, f32[8,256,128]{2,1,0:T(8,128)}, u32[]{:S(2)}, u32[]{:S(2)}) collective-permute-start(f32[8,256,128]{2,1,0:T(8,128)} %get-tuple-element.158), channel_id=1, source_target_pairs={{0,16},{8,24},{16,0},{24,8},{1,17},{9,25},{17,1},{25,9},{2,18},{10... | collective-permute-start | bytes 3145736 | tf_op jit(solution)/shard_map/ppermute | solution.py:468
  398.9 96.1 %collective-permute-start.26 = (f32[8,256,128]{2,1,0:T(8,128)}, f32[8,256,128]{2,1,0:T(8,128)}, u32[]{:S(2)}, u32[]{:S(2)}) collective-permute-start(f32[8,256,128]{2,1,0:T(8,128)} %get-tuple-element.159), channel_id=1, source_target_pairs={{0,24},{8,16},{16,8},{24,0},{1,25},{9,17},{17,9},{25,1},{2,26},{10... | collective-permute-start | bytes 3145736 | tf_op jit(solution)/shard_map/ppermute | solution.py:468
  398.9 69.4 %collective-permute-start.28 = (f32[8,256,128]{2,1,0:T(8,128)}, f32[8,256,128]{2,1,0:T(8,128)}, u32[]{:S(2)}, u32[]{:S(2)}) collective-permute-start(f32[8,256,128]{2,1,0:T(8,128)} %get-tuple-element.162), channel_id=1, source_target_pairs={{0,16},{8,24},{16,0},{24,8},{1,17},{9,25},{17,1},{25,9},{2,18},{10... | collective-permute-start | bytes 3145736 | tf_op jit(solution)/shard_map/ppermute | solution.py:468
  400.3 89.1 %collective-permute-start.29 = (f32[8,256,128]{2,1,0:T(8,128)}, f32[8,256,128]{2,1,0:T(8,128)}, u32[]{:S(2)}, u32[]{:S(2)}) collective-permute-start(f32[8,256,128]{2,1,0:T(8,128)} %get-tuple-element.163), channel_id=1, source_target_pairs={{0,24},{8,16},{16,8},{24,0},{1,25},{9,17},{17,9},{25,1},{2,26},{10... | collective-permute-start | bytes 3145736 | tf_op jit(solution)/shard_map/ppermute | solution.py:468
  400.7 99.8 %all-to-all-start.2 = ((f32[64,8,16,128]{3,2,1,0:T(8,128)}), f32[64,8,16,128]{3,2,1,0:T(8,128)}, u32[]{:S(2)}, u32[]{:S(2)}) async-start(f32[64,8,16,128]{3,2,1,0:T(8,128)} %shard_map.89), calls=%async_computation.2 | async-start | bytes 8388608 | tf_op jit(solution)/shard_map/all_to_all | solution.py:577
  468.3 50.0 %collective-permute-start.30 = (f32[8,256,128]{2,1,0:T(8,128)}, f32[8,256,128]{2,1,0:T(8,128)}, u32[]{:S(2)}, u32[]{:S(2)}) collective-permute-start(f32[8,256,128]{2,1,0:T(8,128)} %get-tuple-element.169), channel_id=1, source_target_pairs={{0,8},{8,0},{16,24},{24,16},{1,9},{9,1},{17,25},{25,17},{2,10},{10... | collective-permute-start | bytes 3145736 | tf_op jit(solution)/shard_map/ppermute | solution.py:468
  489.4 28.9 %collective-permute-start.31 = (f32[8,256,128]{2,1,0:T(8,128)}, f32[8,256,128]{2,1,0:T(8,128)}, u32[]{:S(2)}, u32[]{:S(2)}) collective-permute-start(f32[8,256,128]{2,1,0:T(8,128)} %get-tuple-element.170), channel_id=1, source_target_pairs={{0,16},{8,24},{16,0},{24,8},{1,17},{9,25},{17,1},{25,9},{2,18},{10... | collective-permute-start | bytes 3145736 | tf_op jit(solution)/shard_map/ppermute | solution.py:468
  494.4 43.0 %collective-permute-start.32 = (f32[8,256,128]{2,1,0:T(8,128)}, f32[8,256,128]{2,1,0:T(8,128)}, u32[]{:S(2)}, u32[]{:S(2)}) collective-permute-start(f32[8,256,128]{2,1,0:T(8,128)} %get-tuple-element.171), channel_id=1, source_target_pairs={{0,24},{8,16},{16,8},{24,0},{1,25},{9,17},{17,9},{25,1},{2,26},{10... | collective-permute-start | bytes 3145736 | tf_op jit(solution)/shard_map/ppermute | solution.py:468
  537.4 48.9 %collective-permute-start.33 = (f32[8,256,128]{2,1,0:T(8,128)}, f32[8,256,128]{2,1,0:T(8,128)S(1)}, u32[]{:S(2)}, u32[]{:S(2)}) collective-permute-start(f32[8,256,128]{2,1,0:T(8,128)} %get-tuple-element.173), channel_id=1, source_target_pairs={{0,8},{8,0},{16,24},{24,16},{1,9},{9,1},{17,25},{25,17},{2,10},{10... | collective-permute-start | bytes 3145736 | tf_op jit(solution)/shard_map/ppermute | solution.py:468
  537.6 48.7 %collective-permute-start.34 = (f32[8,256,128]{2,1,0:T(8,128)}, f32[8,256,128]{2,1,0:T(8,128)S(1)}, u32[]{:S(2)}, u32[]{:S(2)}) collective-permute-start(f32[8,256,128]{2,1,0:T(8,128)} %get-tuple-element.174), channel_id=1, source_target_pairs={{0,16},{8,24},{16,0},{24,8},{1,17},{9,25},{17,1},{25,9},{2,18},{10... | collective-permute-start | bytes 3145736 | tf_op jit(solution)/shard_map/ppermute | solution.py:468
  539.3 47.0 %collective-permute-start.35 = (f32[8,256,128]{2,1,0:T(8,128)}, f32[8,256,128]{2,1,0:T(8,128)S(1)}, u32[]{:S(2)}, u32[]{:S(2)}) collective-permute-start(f32[8,256,128]{2,1,0:T(8,128)} %get-tuple-element.175), channel_id=1, source_target_pairs={{0,24},{8,16},{16,8},{24,0},{1,25},{9,17},{17,9},{25,1},{2,26},{10... | collective-permute-start | bytes 3145736 | tf_op jit(solution)/shard_map/ppermute | solution.py:468
  541.7 1.4 collective-permute-start.36
  543.9 4.1 collective-permute-start.37
  548.0 3.6 collective-permute-start.38
  551.6 4.5 collective-permute-start.39
  556.1 29.7 %collective-permute-start.40 = (f32[4,64]{1,0:T(4,128)S(1)}, f32[4,64]{1,0:T(4,128)S(1)}, u32[]{:S(2)}, u32[]{:S(2)}) collective-permute-start(f32[4,64]{1,0:T(4,128)S(1)} %add.18), channel_id=1, source_target_pairs={{0,16},{8,24},{16,0},{24,8},{1,17},{9,25},{17,1},{25,9},{2,18},{10... | collective-permute-start | bytes 3080 | tf_op jit(solution)/shard_map/ppermute | solution.py:512
  (11 other events, 96.1 us)

commit v4 on v3

--- a/solution.py
+++ b/solution.py
@@ -502,12 +502,16 @@
     )(seat, *grads, *waited)
 
 
-def grand_total(value):
+def total_rounds():
     rounds = []
     for axis in ("grp", "dev"):
         count = lax.axis_size(axis)
         rounds.append([(axis, 1 << bit, count) for bit in range(count.bit_length() - 1)])
-    for axis, step, count in rounds[0][:1] + rounds[1] + rounds[0][1:]:
+    return rounds[0][:1] + rounds[1] + rounds[0][1:]
+
+
+def add_rounds(value, rounds):
+    for axis, step, count in rounds:
         pairs = [(member, member ^ step) for member in range(count)]
         value = value + lax.ppermute(value, axis, pairs)
     return value
@@ -534,7 +538,7 @@
         cut_pieces(density, seats, parts, chunk, size, list(state_cut[-1][:1]) if chunk else [])
         for chunk in range(chunks)
     ]
-    rho_there = [swap(pieces, parts) for pieces in rho]
+    rho_there = [swap(pieces, parts) for pieces in (rho[:2] if chunks > 3 else rho)]
     ahead = parts // 2
     state_cut[0], rho_there[0][ahead] = lax.optimization_barrier(
         (state_cut[0], rho_there[0][ahead])
@@ -542,7 +546,7 @@
     state = [swap(pieces, parts) for pieces in state_cut[:3]]
 
     shape = (2, rows // WIDE, parts, chunks, size, cols)
-    fields, closed, made, grads = [], [], [], []
+    fields, closed, made, grads, totals = [], [], [], [], []
 
     def close(chunk, waited):
         if chunk > 0:
@@ -553,11 +557,13 @@
         closed.append(out)
         if chunk == chunks - 2 and chunk > 0:
             out, rho_there[-1] = lax.optimization_barrier((out, rho_there[-1]))
-        if chunk == chunks - 1 and chunk > 1:
-            out, made[-1] = lax.optimization_barrier((out, made[-1]))
+        grads.append(grad)
+        if chunk == chunks - 1:
+            total = add_rounds(device_grad(grads, seats, parts, []), total_rounds()[:-1])
+            out, made[-1:], total = lax.optimization_barrier((out, made[-1:], total))
+            totals.append(total)
         if chunk > 0 or chunks < 4:
             made.append(swap(out, parts))
-        grads.append(grad)
 
     for chunk in range(chunks):
         waited = [rho[chunk][0]]
@@ -572,6 +578,8 @@
         if chunk + 1 == len(state) < chunks:
             pieces, field = lax.optimization_barrier((state_cut[chunk + 1], field))
             state.append(swap(pieces, parts))
+            pieces, state[-1] = lax.optimization_barrier((rho[2], state[-1]))
+            rho_there += [swap(pieces, parts), swap(rho[3], parts)]
             out, rho_there[2] = lax.optimization_barrier((closed[0], rho_there[2]))
             made.append(swap(out, parts))
         fields.append(lax.all_to_all(field, "dev", split_axis=0, concat_axis=0, tiled=True))
@@ -580,7 +588,7 @@
         while len(made) < min(max(chunk + 2, chunks - 1), chunks):
             close(len(made), [whole] if 0 < chunk == chunks - 2 else [])
         whole = place_pieces(made[chunk], seats, whole, chunk, shape, size, closed[-1][0])
-    grad = grand_total(device_grad(grads, seats, parts, []))
+    grad = add_rounds(totals[0], total_rounds()[-1:])
     return whole.reshape(costate.shape), grad.reshape(2, 2, LEVELS)
 
 

time: 594 us -> 603 us (1.015)
  waiting for transfers between devices: 355 us -> 372 us
  starting transfers between devices: 61.2 us -> 52.5 us
    ppermute x36, waiting for transfers between devices: 301 us -> 245 us  [swap(): moved.append(lax.ppermute(pieces[step], 'grp', pairs))]
    all_to_all x4, waiting for transfers between devices: 23.1 us -> 74.6 us  [per_device(): lax.all_to_all(field, 'dev', split_axis=0, concat_axis=0, tiled=True)]
    ppermute x5, waiting for transfers between devices: 31 us -> 52.8 us  [add_rounds(): value = value + lax.ppermute(value, axis, pairs)]
  transfers between devices with their start and end apart: 45 -> 45, of which waited for: 22 -> 22; matrix products, arithmetic and copies ran while one was open for 0% -> 0% of each run, Pallas kernels for 26% -> 25%
where the time goes in v4:
time: 603 us; the launch traced here: 602 us
  waiting for transfers between devices  372 us (62%)
  Pallas kernels  168 us (28%)
  starting transfers between devices  52.5 us (9%)
  local copies, waits for them, and re-layouts  6.13 us (1%)
    ppermute x36, waiting for transfers between devices, swap(): moved.append(lax.ppermute(pieces[step], 'grp', pairs))  245 us
    all_to_all x4, waiting for transfers between devices, per_device(): lax.all_to_all(field, 'dev', split_axis=0, concat_axis=0, tiled=True)  74.6 us
    pallas_call x4, Pallas kernels, close_columns(): pl.pallas_call(functools.partial(close_kernel, parts, size), grid=(firsts...  71 us
    ppermute x5, waiting for transfers between devices, add_rounds(): value = value + lax.ppermute(value, axis, pairs)  52.8 us
    pallas_call x4, Pallas kernels, turn_columns(): pl.pallas_call(functools.partial(turn_kernel, parts, size, group), grid=(...  30.6 us
    ppermute x36, starting transfers between devices, swap(): moved.append(lax.ppermute(pieces[step], 'grp', pairs))  27.8 us
    all_to_all x4, starting transfers between devices, per_device(): lax.all_to_all(field, 'dev', split_axis=0, concat_axis=0, tiled=True)  21.7 us
    pallas_call x1, Pallas kernels, open_state(): pl.pallas_call(functools.partial(open_kernel, count, len(waited)), grid=(...  19.5 us
  transfers between devices with their start and end apart: 45, of which 22 were waited for; matrix products, arithmetic and copies ran while one was open for 0% of the time, Pallas kernels for 25%

profile of v4, /device:TPU:0, one launch (start us, length us, event | category | flops | bytes accessed | tf_op | source)
XLA Modules:
  0.0 601.8 jit_solution(14714312424123810043)
XLA Ops:
  0.6 3.7 shard_map.82
  4.4 2.9 collective-permute-start.6
  7.9 4.6 shard_map.77
  12.5 10.4 %shard_map.78 = (f32[8,256,128]{2,1,0:T(8,128)}, f32[8,256,128]{2,1,0:T(8,128)}, f32[8,256,128]{2,1,0:T(8,128)}, f32[8,256,128]{2,1,0:T(8,128)}) custom-call(bf16[512,128]{1,0:T(8,128)(2,1)} %get-tuple-element.106.weight_ref, f32[2,1024,2048]{2,1,0:T(8,128)} %field_ref.3), custom_call_target="tpu_custom_call" | custom-call | flops 1024 | bytes 1024 | tf_op jit(solution)/shard_map/pallas_call | solution.py:210
  22.9 7.7 %collective-permute-done.6.refs_2_ = f32[8,256,128]{2,1,0:T(8,128)S(1)} collective-permute-done((f32[8,256,128]{2,1,0:T(8,128)}, f32[8,256,128]{2,1,0:T(8,128)S(1)}, u32[]{:S(2)}, u32[]{:S(2)}) %collective-permute-start.6) | collective-permute-done | bytes 1048608 | tf_op jit(solution)/shard_map/ppermute | solution.py:468
  31.7 1.7 collective-permute-start.8
  34.3 19.5 %shard_map.79 = (f32[8,256,128]{2,1,0:T(8,128)}, f32[8,256,128]{2,1,0:T(8,128)}, f32[8,256,128]{2,1,0:T(8,128)}, f32[8,256,128]{2,1,0:T(8,128)}, f32[8,256,128]{...) custom-call(bf16[2,192,256]{2,1,0:T(8,128)(2,1)} %slice.3.weight_ref, ...), custom_call_target="tpu_custom_call" | custom-call | flops 1024 | bytes 1024 | tf_op jit(solution)/shard_map/pallas_call | solution.py:235
  53.8 4.1 collective-permute-done.8.refs_2_
  57.9 21.7 %collective-permute-done.9.refs_3_ = f32[8,256,128]{2,1,0:T(8,128)S(1)} collective-permute-done((f32[8,256,128]{2,1,0:T(8,128)}, f32[8,256,128]{2,1,0:T(8,128)S(1)}, u32[]{:S(2)}, u32[]{:S(2)}) %collective-permute-start.9) | collective-permute-done | bytes 1048608 | tf_op jit(solution)/shard_map/ppermute | solution.py:468
  80.6 7.5 %shard_map.83.refs_5_ = f32[64,8,16,128]{3,2,1,0:T(8,128)} custom-call(bf16[256,256]{1,0:T(8,128)(2,1)} %get-tuple-element.104.weight_ref, f32[8,256,128]{2,1,0:T(8,128)} %get-tuple-element.129.refs_0_, f32[8,256,128]{2,1,0:T(8,128)} %copy-done.6, f32[8,256,128]{2,1,0:T(8,128)} %copy-done.7, f32[8,256,128]{2,1,0:T(8,128)} %copy-done.8, ...), custom_call_target="tpu_custom_call" | custom-call | flops 1024 | bytes 1024 | tf_op jit(solution)/shard_map/pallas_call | solution.py:336
  88.1 6.1 %all-to-all-start = ((f32[64,8,16,128]{3,2,1,0:T(8,128)}), f32[64,8,16,128]{3,2,1,0:T(8,128)}, u32[]{:S(2)}, u32[]{:S(2)}) async-start(f32[64,8,16,128]{3,2,1,0:T(8,128)} %shard_map.83.refs_5_), calls=%async_computation | async-start | bytes 8388608 | tf_op jit(solution)/shard_map/all_to_all | solution.py:585
  94.2 1.6 collective-permute-start.4
  97.7 3.7 shard_map.81
  101.3 3.7 shard_map.80
  105.5 15.0 %collective-permute-done.4.refs_2_ = f32[8,256,128]{2,1,0:T(8,128)S(1)} collective-permute-done((f32[8,256,128]{2,1,0:T(8,128)}, f32[8,256,128]{2,1,0:T(8,128)S(1)}, u32[]{:S(2)}, u32[]{:S(2)}) %collective-permute-start.4) | collective-permute-done | bytes 1048608 | tf_op jit(solution)/shard_map/ppermute | solution.py:468
  121.9 20.1 %collective-permute-done.5.refs_3_ = f32[8,256,128]{2,1,0:T(8,128)S(1)} collective-permute-done((f32[8,256,128]{2,1,0:T(8,128)}, f32[8,256,128]{2,1,0:T(8,128)S(1)}, u32[]{:S(2)}, u32[]{:S(2)}) %collective-permute-start.5) | collective-permute-done | bytes 1048608 | tf_op jit(solution)/shard_map/ppermute | solution.py:468
  142.0 2.2 collective-permute-start.2
  144.2 7.7 %shard_map.84.refs_5_ = f32[64,8,16,128]{3,2,1,0:T(8,128)} custom-call(bf16[256,256]{1,0:T(8,128)(2,1)} %get-tuple-element.104.weight_ref, f32[8,256,128]{2,1,0:T(8,128)} %get-tuple-element.120.refs_5_.refs_0_, f32[8,256,128]{2,1,0:T(8,128)} %copy-done.3, f32[8,256,128]{2,1,0:T(8,128)} %copy-done.4, f32[8,256,128]{2,1,0:T(8,128)} %copy-done.5, ...), custom_call_target="tpu_custom_call" | custom-call | flops 1024 | bytes 1024 | tf_op jit(solution)/shard_map/pallas_call | solution.py:336
  151.9 35.9 %all-to-all-done = f32[64,8,16,128]{3,2,1,0:T(8,128)} async-done(((f32[64,8,16,128]{3,2,1,0:T(8,128)}), f32[64,8,16,128]{3,2,1,0:T(8,128)}, u32[]{:S(2)}, u32[]{:S(2)}) %all-to-all-start) | async-done | bytes 4194336 | tf_op jit(solution)/shard_map/all_to_all | solution.py:585
  187.8 4.8 all-to-all-start.1
  192.6 17.8 %shard_map.85 = (f32[8,256,128]{2,1,0:T(8,128)}, f32[8,256,128]{2,1,0:T(8,128)}, f32[8,256,128]{2,1,0:T(8,128)}, f32[8,256,128]{2,1,0:T(8,128)}, f32[2,64,128]{2,1,0:T(8,128)}) custom-call(bf16[3,2,256,256]{3,2,1,0:T(8,128)(2,1)} %get-tuple-element.102.lane_ref, bf16[3,256,256]{2,1,0:T(8,128)(2,1)} %get-tuple-element.103.level_ref, ...), custom_call_target="tpu_custom_call" | custom-call | flops 199999995904 | bytes 1024 | tf_op jit(solution)/shard_map/pallas_call | solution.py:408
  210.5 7.7 %shard_map.86.refs_5_ = f32[64,8,16,128]{3,2,1,0:T(8,128)} custom-call(bf16[256,256]{1,0:T(8,128)(2,1)} %get-tuple-element.104.weight_ref, f32[8,256,128]{2,1,0:T(8,128)} %get-tuple-element.116.refs_0_, f32[8,256,128]{2,1,0:T(8,128)} %collective-permute-done.refs_1_, f32[8,256,128]{2,1,0:T(8,128)} %collective-permute-done.1.refs_2_, ...), custom_call_target="tpu_custom_call" | custom-call | flops 1024 | bytes 1024 | tf_op jit(solution)/shard_map/pallas_call | solution.py:336
  221.2 23.3 %collective-permute-done.13.refs_2_ = f32[8,256,128]{2,1,0:T(8,128)} collective-permute-done((f32[8,256,128]{2,1,0:T(8,128)}, f32[8,256,128]{2,1,0:T(8,128)}, u32[]{:S(2)}, u32[]{:S(2)}) %collective-permute-start.13) | collective-permute-done | bytes 1048608 | tf_op jit(solution)/shard_map/ppermute | solution.py:468
  244.4 21.7 %collective-permute-done.14.refs_3_ = f32[8,256,128]{2,1,0:T(8,128)} collective-permute-done((f32[8,256,128]{2,1,0:T(8,128)}, f32[8,256,128]{2,1,0:T(8,128)}, u32[]{:S(2)}, u32[]{:S(2)}) %collective-permute-start.14) | collective-permute-done | bytes 1048608 | tf_op jit(solution)/shard_map/ppermute | solution.py:468
  271.4 3.7 shard_map.87
  275.1 17.6 %collective-permute-done.19.refs_2_ = f32[8,256,128]{2,1,0:T(8,128)} collective-permute-done((f32[8,256,128]{2,1,0:T(8,128)}, f32[8,256,128]{2,1,0:T(8,128)}, u32[]{:S(2)}, u32[]{:S(2)}) %collective-permute-start.19) | collective-permute-done | bytes 1048608 | tf_op jit(solution)/shard_map/ppermute | solution.py:468
  292.6 21.5 %collective-permute-done.20.refs_3_ = f32[8,256,128]{2,1,0:T(8,128)} collective-permute-done((f32[8,256,128]{2,1,0:T(8,128)}, f32[8,256,128]{2,1,0:T(8,128)}, u32[]{:S(2)}, u32[]{:S(2)}) %collective-permute-start.20) | collective-permute-done | bytes 1048608 | tf_op jit(solution)/shard_map/ppermute | solution.py:468
  316.3 6.1 %all-to-all-start.3 = ((f32[64,8,16,128]{3,2,1,0:T(8,128)}), f32[64,8,16,128]{3,2,1,0:T(8,128)}, u32[]{:S(2)}, u32[]{:S(2)}) async-start(f32[64,8,16,128]{3,2,1,0:T(8,128)} %shard_map.86.refs_5_), calls=%async_computation.3 | async-start | bytes 8388608 | tf_op jit(solution)/shard_map/all_to_all | solution.py:585
  322.4 15.2 %collective-permute-done.16.refs_2_ = f32[8,256,128]{2,1,0:T(8,128)} collective-permute-done((f32[8,256,128]{2,1,0:T(8,128)S(1)}, f32[8,256,128]{2,1,0:T(8,128)}, u32[]{:S(2)}, u32[]{:S(2)}) %collective-permute-start.16) | collective-permute-done | bytes 1048608 | tf_op jit(solution)/shard_map/ppermute | solution.py:468
  337.6 21.4 %collective-permute-done.17.refs_3_ = f32[8,256,128]{2,1,0:T(8,128)} collective-permute-done((f32[8,256,128]{2,1,0:T(8,128)S(1)}, f32[8,256,128]{2,1,0:T(8,128)}, u32[]{:S(2)}, u32[]{:S(2)}) %collective-permute-start.17) | collective-permute-done | bytes 1048608 | tf_op jit(solution)/shard_map/ppermute | solution.py:468
  359.0 17.7 %shard_map.88 = (f32[8,256,128]{2,1,0:T(8,128)}, f32[8,256,128]{2,1,0:T(8,128)}, f32[8,256,128]{2,1,0:T(8,128)}, f32[8,256,128]{2,1,0:T(8,128)}, f32[2,64,128]{2,1,0:T(8,128)}) custom-call(bf16[3,2,256,256]{3,2,1,0:T(8,128)(2,1)} %get-tuple-element.102.lane_ref, bf16[3,256,256]{2,1,0:T(8,128)(2,1)} %get-tuple-element.103.level_ref, ...), custom_call_target="tpu_custom_call" | custom-call | flops 199999995904 | bytes 1024 | tf_op jit(solution)/shard_map/pallas_call | solution.py:408
  378.0 7.7 %shard_map.89 = f32[64,8,16,128]{3,2,1,0:T(8,128)} custom-call(bf16[256,256]{1,0:T(8,128)(2,1)} %get-tuple-element.104.weight_ref, f32[8,256,128]{2,1,0:T(8,128)} %get-tuple-element.142.refs_0_, f32[8,256,128]{2,1,0:T(8,128)} %collective-permute-done.12.refs_1_, f32[8,256,128]{2,1,0:T(8,128)} %collective-permute-done.13.refs_2_, ...), custom_call_target="tpu_custom_call" | custom-call | flops 1024 | bytes 1024 | tf_op jit(solution)/shard_map/pallas_call | solution.py:336
  387.2 28.6 %all-to-all-done.3 = f32[64,8,16,128]{3,2,1,0:T(8,128)} async-done(((f32[64,8,16,128]{3,2,1,0:T(8,128)}), f32[64,8,16,128]{3,2,1,0:T(8,128)}, u32[]{:S(2)}, u32[]{:S(2)}) %all-to-all-start.3) | async-done | bytes 4194336 | tf_op jit(solution)/shard_map/all_to_all | solution.py:585
  415.8 4.8 all-to-all-start.2
  421.3 17.8 %shard_map.90 = (f32[8,256,128]{2,1,0:T(8,128)}, f32[8,256,128]{2,1,0:T(8,128)}, f32[8,256,128]{2,1,0:T(8,128)}, f32[8,256,128]{2,1,0:T(8,128)}, f32[2,64,128]{2,1,0:T(8,128)}) custom-call(bf16[3,2,256,256]{3,2,1,0:T(8,128)(2,1)} %get-tuple-element.102.lane_ref, bf16[3,256,256]{2,1,0:T(8,128)(2,1)} %get-tuple-element.103.level_ref, ...), custom_call_target="tpu_custom_call" | custom-call | flops 199999995904 | bytes 1024 | tf_op jit(solution)/shard_map/pallas_call | solution.py:408
  439.0 33.4 %collective-permute-done.28.refs_2_ = f32[8,256,128]{2,1,0:T(8,128)} collective-permute-done((f32[8,256,128]{2,1,0:T(8,128)}, f32[8,256,128]{2,1,0:T(8,128)}, u32[]{:S(2)}, u32[]{:S(2)}) %collective-permute-start.28) | collective-permute-done | bytes 1048608 | tf_op jit(solution)/shard_map/ppermute | solution.py:468
  472.4 21.2 %collective-permute-done.29.refs_3_ = f32[8,256,128]{2,1,0:T(8,128)} collective-permute-done((f32[8,256,128]{2,1,0:T(8,128)}, f32[8,256,128]{2,1,0:T(8,128)}, u32[]{:S(2)}, u32[]{:S(2)}) %collective-permute-start.29) | collective-permute-done | bytes 1048608 | tf_op jit(solution)/shard_map/ppermute | solution.py:468
  495.1 3.7 shard_map.91.refs_4_
  499.1 3.7 shard_map.92.refs_4_
  502.8 10.1 %all-to-all-done.2 = f32[64,8,16,128]{3,2,1,0:T(8,128)} async-done(((f32[64,8,16,128]{3,2,1,0:T(8,128)}), f32[64,8,16,128]{3,2,1,0:T(8,128)}, u32[]{:S(2)}, u32[]{:S(2)}) %all-to-all-start.2) | async-done | bytes 4194336 | tf_op jit(solution)/shard_map/all_to_all | solution.py:585
  512.9 17.8 %shard_map.93 = (f32[8,256,128]{2,1,0:T(8,128)}, f32[8,256,128]{2,1,0:T(8,128)}, f32[8,256,128]{2,1,0:T(8,128)}, f32[8,256,128]{2,1,0:T(8,128)}, f32[2,64,128]{2,1,0:T(8,128)}) custom-call(bf16[3,2,256,256]{3,2,1,0:T(8,128)(2,1)} %get-tuple-element.102.lane_ref, bf16[3,256,256]{2,1,0:T(8,128)(2,1)} %get-tuple-element.103.level_ref, ...), custom_call_target="tpu_custom_call" | custom-call | flops 199999995904 | bytes 1024 | tf_op jit(solution)/shard_map/pallas_call | solution.py:408
  530.7 2.4 shard_map.94
  536.6 2.1 collective-permute-done.34
  538.7 3.6 collective-permute-done.35
  543.2 3.6 collective-permute-done.36
  549.4 3.7 shard_map.95.refs_4_
  553.1 42.1 %collective-permute-done.40 = f32[4,64]{1,0:T(4,128)S(1)} collective-permute-done((f32[4,64]{1,0:T(4,128)S(1)}, f32[4,64]{1,0:T(4,128)S(1)}, u32[]{:S(2)}, u32[]{:S(2)}) %collective-permute-start.40) | collective-permute-done | bytes 1056 | tf_op jit(solution)/shard_map/ppermute | solution.py:516
  598.1 3.7 shard_map.96
  (98 shorter events, 32.3 us)
Async XLA Ops:
  4.4 26.3 %collective-permute-start.6 = (f32[8,256,128]{2,1,0:T(8,128)}, f32[8,256,128]{2,1,0:T(8,128)S(1)}, u32[]{:S(2)}, u32[]{:S(2)}) collective-permute-start(f32[8,256,128]{2,1,0:T(8,128)} %get-tuple-element.128), channel_id=1, source_target_pairs={{0,16},{8,24},{16,0},{24,8},{1,17},{9,25},{17,1},{25,9},{2,18},{10... | collective-permute-start | bytes 3145736 | tf_op jit(solution)/shard_map/ppermute | solution.py:468
  31.7 22.1 %collective-permute-start.7 = (f32[8,256,128]{2,1,0:T(8,128)}, f32[8,256,128]{2,1,0:T(8,128)S(1)}, u32[]{:S(2)}, u32[]{:S(2)}) collective-permute-start(f32[8,256,128]{2,1,0:T(8,128)} %get-tuple-element.130), channel_id=1, source_target_pairs={{0,8},{8,0},{16,24},{24,16},{1,9},{9,1},{17,25},{25,17},{2,10},{10... | collective-permute-start | bytes 3145736 | tf_op jit(solution)/shard_map/ppermute | solution.py:468
  31.7 26.2 %collective-permute-start.8 = (f32[8,256,128]{2,1,0:T(8,128)}, f32[8,256,128]{2,1,0:T(8,128)S(1)}, u32[]{:S(2)}, u32[]{:S(2)}) collective-permute-start(f32[8,256,128]{2,1,0:T(8,128)} %get-tuple-element.131), channel_id=1, source_target_pairs={{0,16},{8,24},{16,0},{24,8},{1,17},{9,25},{17,1},{25,9},{2,18},{10... | collective-permute-start | bytes 3145736 | tf_op jit(solution)/shard_map/ppermute | solution.py:468
  33.5 46.1 %collective-permute-start.9 = (f32[8,256,128]{2,1,0:T(8,128)}, f32[8,256,128]{2,1,0:T(8,128)S(1)}, u32[]{:S(2)}, u32[]{:S(2)}) collective-permute-start(f32[8,256,128]{2,1,0:T(8,128)} %get-tuple-element.132), channel_id=1, source_target_pairs={{0,24},{8,16},{16,8},{24,0},{1,25},{9,17},{17,9},{25,1},{2,26},{10... | collective-permute-start | bytes 3145736 | tf_op jit(solution)/shard_map/ppermute | solution.py:468
  88.1 99.7 %all-to-all-start = ((f32[64,8,16,128]{3,2,1,0:T(8,128)}), f32[64,8,16,128]{3,2,1,0:T(8,128)}, u32[]{:S(2)}, u32[]{:S(2)}) async-start(f32[64,8,16,128]{3,2,1,0:T(8,128)} %shard_map.83.refs_5_), calls=%async_computation | async-start | bytes 8388608 | tf_op jit(solution)/shard_map/all_to_all | solution.py:585
  94.2 10.8 %collective-permute-start.3 = (f32[8,256,128]{2,1,0:T(8,128)}, f32[8,256,128]{2,1,0:T(8,128)S(1)}, u32[]{:S(2)}, u32[]{:S(2)}) collective-permute-start(f32[8,256,128]{2,1,0:T(8,128)} %get-tuple-element.121), channel_id=1, source_target_pairs={{0,8},{8,0},{16,24},{24,16},{1,9},{9,1},{17,25},{25,17},{2,10},{10... | collective-permute-start | bytes 3145736 | tf_op jit(solution)/shard_map/ppermute | solution.py:468
  94.2 26.2 %collective-permute-start.4 = (f32[8,256,128]{2,1,0:T(8,128)}, f32[8,256,128]{2,1,0:T(8,128)S(1)}, u32[]{:S(2)}, u32[]{:S(2)}) collective-permute-start(f32[8,256,128]{2,1,0:T(8,128)} %get-tuple-element.122), channel_id=1, source_target_pairs={{0,16},{8,24},{16,0},{24,8},{1,17},{9,25},{17,1},{25,9},{2,18},{10... | collective-permute-start | bytes 3145736 | tf_op jit(solution)/shard_map/ppermute | solution.py:468
  95.8 46.3 %collective-permute-start.5 = (f32[8,256,128]{2,1,0:T(8,128)}, f32[8,256,128]{2,1,0:T(8,128)S(1)}, u32[]{:S(2)}, u32[]{:S(2)}) collective-permute-start(f32[8,256,128]{2,1,0:T(8,128)} %get-tuple-element.123), channel_id=1, source_target_pairs={{0,24},{8,16},{16,8},{24,0},{1,25},{9,17},{17,9},{25,1},{2,26},{10... | collective-permute-start | bytes 3145736 | tf_op jit(solution)/shard_map/ppermute | solution.py:468
  96.1 96.6 %collective-permute-start.10 = (f32[8,256,128]{2,1,0:T(8,128)}, f32[8,256,128]{2,1,0:T(8,128)}, u32[]{:S(2)}, u32[]{:S(2)}) collective-permute-start(f32[8,256,128]{2,1,0:T(8,128)} %get-tuple-element.134), channel_id=1, source_target_pairs={{0,8},{8,0},{16,24},{24,16},{1,9},{9,1},{17,25},{25,17},{2,10},{10... | collective-permute-start | bytes 3145736 | tf_op jit(solution)/shard_map/ppermute | solution.py:468
  96.4 96.2 %collective-permute-start.11 = (f32[8,256,128]{2,1,0:T(8,128)}, f32[8,256,128]{2,1,0:T(8,128)}, u32[]{:S(2)}, u32[]{:S(2)}) collective-permute-start(f32[8,256,128]{2,1,0:T(8,128)} %get-tuple-element.136), channel_id=1, source_target_pairs={{0,24},{8,16},{16,8},{24,0},{1,25},{9,17},{17,9},{25,1},{2,26},{10... | collective-permute-start | bytes 3145736 | tf_op jit(solution)/shard_map/ppermute | solution.py:468
  105.0 105.4 %collective-permute-start = (f32[8,256,128]{2,1,0:T(8,128)}, f32[8,256,128]{2,1,0:T(8,128)}, u32[]{:S(2)}, u32[]{:S(2)}) collective-permute-start(f32[8,256,128]{2,1,0:T(8,128)} %get-tuple-element.117), channel_id=1, source_target_pairs={{0,8},{8,0},{16,24},{24,16},{1,9},{9,1},{17,25},{25,17},{2,10},{10... | collective-permute-start | bytes 3145736 | tf_op jit(solution)/shard_map/ppermute | solution.py:468
  120.4 90.0 %collective-permute-start.1 = (f32[8,256,128]{2,1,0:T(8,128)}, f32[8,256,128]{2,1,0:T(8,128)}, u32[]{:S(2)}, u32[]{:S(2)}) collective-permute-start(f32[8,256,128]{2,1,0:T(8,128)} %get-tuple-element.118), channel_id=1, source_target_pairs={{0,16},{8,24},{16,0},{24,8},{1,17},{9,25},{17,1},{25,9},{2,18},{10... | collective-permute-start | bytes 3145736 | tf_op jit(solution)/shard_map/ppermute | solution.py:468
  142.0 68.4 %collective-permute-start.2 = (f32[8,256,128]{2,1,0:T(8,128)}, f32[8,256,128]{2,1,0:T(8,128)}, u32[]{:S(2)}, u32[]{:S(2)}) collective-permute-start(f32[8,256,128]{2,1,0:T(8,128)} %get-tuple-element.119), channel_id=1, source_target_pairs={{0,24},{8,16},{16,8},{24,0},{1,25},{9,17},{17,9},{25,1},{2,26},{10... | collective-permute-start | bytes 3145736 | tf_op jit(solution)/shard_map/ppermute | solution.py:468
  187.8 128.4 %all-to-all-start.1 = ((f32[64,8,16,128]{3,2,1,0:T(8,128)}), f32[64,8,16,128]{3,2,1,0:T(8,128)}, u32[]{:S(2)}, u32[]{:S(2)}) async-start(f32[64,8,16,128]{3,2,1,0:T(8,128)} %shard_map.84.refs_5_), calls=%async_computation.1 | async-start | bytes 8388608 | tf_op jit(solution)/shard_map/all_to_all | solution.py:585
  210.5 57.5 %copy-start.12 = (f32[8,256,128]{2,1,0:T(8,128)S(1)}, f32[8,256,128]{2,1,0:T(8,128)}, u32[]{:S(2)}) copy-start(f32[8,256,128]{2,1,0:T(8,128)} %get-tuple-element.148) | copy-start | bytes 3145732
  210.5 58.0 %copy-start.11 = (f32[8,256,128]{2,1,0:T(8,128)S(1)}, f32[8,256,128]{2,1,0:T(8,128)}, u32[]{:S(2)}) copy-start(f32[8,256,128]{2,1,0:T(8,128)} %get-tuple-element.149) | copy-start | bytes 3145732
  210.5 60.6 %copy-start.10 = (f32[8,256,128]{2,1,0:T(8,128)S(1)}, f32[8,256,128]{2,1,0:T(8,128)}, u32[]{:S(2)}) copy-start(f32[8,256,128]{2,1,0:T(8,128)} %get-tuple-element.150) | copy-start | bytes 3145732
  218.2 3.0 collective-permute-start.12
  218.2 26.3 %collective-permute-start.13 = (f32[8,256,128]{2,1,0:T(8,128)}, f32[8,256,128]{2,1,0:T(8,128)}, u32[]{:S(2)}, u32[]{:S(2)}) collective-permute-start(f32[8,256,128]{2,1,0:T(8,128)} %get-tuple-element.140), channel_id=1, source_target_pairs={{0,16},{8,24},{16,0},{24,8},{1,17},{9,25},{17,1},{25,9},{2,18},{10... | collective-permute-start | bytes 3145736 | tf_op jit(solution)/shard_map/ppermute | solution.py:468
  219.7 46.5 %collective-permute-start.14 = (f32[8,256,128]{2,1,0:T(8,128)}, f32[8,256,128]{2,1,0:T(8,128)}, u32[]{:S(2)}, u32[]{:S(2)}) collective-permute-start(f32[8,256,128]{2,1,0:T(8,128)} %get-tuple-element.141), channel_id=1, source_target_pairs={{0,24},{8,16},{16,8},{24,0},{1,25},{9,17},{17,9},{25,1},{2,26},{10... | collective-permute-start | bytes 3145736 | tf_op jit(solution)/shard_map/ppermute | solution.py:468
  266.1 3.9 collective-permute-start.18
  266.3 26.3 %collective-permute-start.19 = (f32[8,256,128]{2,1,0:T(8,128)}, f32[8,256,128]{2,1,0:T(8,128)}, u32[]{:S(2)}, u32[]{:S(2)}) collective-permute-start(f32[8,256,128]{2,1,0:T(8,128)} %get-tuple-element.157), channel_id=1, source_target_pairs={{0,16},{8,24},{16,0},{24,8},{1,17},{9,25},{17,1},{25,9},{2,18},{10... | collective-permute-start | bytes 3145736 | tf_op jit(solution)/shard_map/ppermute | solution.py:468
  267.8 46.3 %collective-permute-start.20 = (f32[8,256,128]{2,1,0:T(8,128)}, f32[8,256,128]{2,1,0:T(8,128)}, u32[]{:S(2)}, u32[]{:S(2)}) collective-permute-start(f32[8,256,128]{2,1,0:T(8,128)} %get-tuple-element.158), channel_id=1, source_target_pairs={{0,24},{8,16},{16,8},{24,0},{1,25},{9,17},{17,9},{25,1},{2,26},{10... | collective-permute-start | bytes 3145736 | tf_op jit(solution)/shard_map/ppermute | solution.py:468
  268.0 47.4 %collective-permute-start.15 = (f32[8,256,128]{2,1,0:T(8,128)S(1)}, f32[8,256,128]{2,1,0:T(8,128)}, u32[]{:S(2)}, u32[]{:S(2)}) collective-permute-start(f32[8,256,128]{2,1,0:T(8,128)S(1)} %copy-done.12), channel_id=1, source_target_pairs={{0,8},{8,0},{16,24},{24,16},{1,9},{9,1},{17,25},{25,17},{2,10},{10... | collective-permute-start | bytes 3145736 | tf_op jit(solution)/shard_map/ppermute | solution.py:468
  268.5 69.1 %collective-permute-start.16 = (f32[8,256,128]{2,1,0:T(8,128)S(1)}, f32[8,256,128]{2,1,0:T(8,128)}, u32[]{:S(2)}, u32[]{:S(2)}) collective-permute-start(f32[8,256,128]{2,1,0:T(8,128)S(1)} %copy-done.11), channel_id=1, source_target_pairs={{0,16},{8,24},{16,0},{24,8},{1,17},{9,25},{17,1},{25,9},{2,18},{10... | collective-permute-start | bytes 3145736 | tf_op jit(solution)/shard_map/ppermute | solution.py:468
  271.1 87.9 %collective-permute-start.17 = (f32[8,256,128]{2,1,0:T(8,128)S(1)}, f32[8,256,128]{2,1,0:T(8,128)}, u32[]{:S(2)}, u32[]{:S(2)}) collective-permute-start(f32[8,256,128]{2,1,0:T(8,128)S(1)} %copy-done.10), channel_id=1, source_target_pairs={{0,24},{8,16},{16,8},{24,0},{1,25},{9,17},{17,9},{25,1},{2,26},{10... | collective-permute-start | bytes 3145736 | tf_op jit(solution)/shard_map/ppermute | solution.py:468
  292.6 93.0 %collective-permute-start.21 = (f32[8,256,128]{2,1,0:T(8,128)}, f32[8,256,128]{2,1,0:T(8,128)}, u32[]{:S(2)}, u32[]{:S(2)}) collective-permute-start(f32[8,256,128]{2,1,0:T(8,128)} %get-tuple-element.167), channel_id=1, source_target_pairs={{0,8},{8,0},{16,24},{24,16},{1,9},{9,1},{17,25},{25,17},{2,10},{10... | collective-permute-start | bytes 3145736 | tf_op jit(solution)/shard_map/ppermute | solution.py:468
  314.1 73.1 %collective-permute-start.22 = (f32[8,256,128]{2,1,0:T(8,128)}, f32[8,256,128]{2,1,0:T(8,128)}, u32[]{:S(2)}, u32[]{:S(2)}) collective-permute-start(f32[8,256,128]{2,1,0:T(8,128)} %get-tuple-element.168), channel_id=1, source_target_pairs={{0,16},{8,24},{16,0},{24,8},{1,17},{9,25},{17,1},{25,9},{2,18},{10... | collective-permute-start | bytes 3145736 | tf_op jit(solution)/shard_map/ppermute | solution.py:468
  315.4 105.2 %collective-permute-start.23 = (f32[8,256,128]{2,1,0:T(8,128)}, f32[8,256,128]{2,1,0:T(8,128)}, u32[]{:S(2)}, u32[]{:S(2)}) collective-permute-start(f32[8,256,128]{2,1,0:T(8,128)} %get-tuple-element.169), channel_id=1, source_target_pairs={{0,24},{8,16},{16,8},{24,0},{1,25},{9,17},{17,9},{25,1},{2,26},{10... | collective-permute-start | bytes 3145736 | tf_op jit(solution)/shard_map/ppermute | solution.py:468
  316.3 99.5 %all-to-all-start.3 = ((f32[64,8,16,128]{3,2,1,0:T(8,128)}), f32[64,8,16,128]{3,2,1,0:T(8,128)}, u32[]{:S(2)}, u32[]{:S(2)}) async-start(f32[64,8,16,128]{3,2,1,0:T(8,128)} %shard_map.86.refs_5_), calls=%async_computation.3 | async-start | bytes 8388608 | tf_op jit(solution)/shard_map/all_to_all | solution.py:585
  337.6 83.7 %collective-permute-start.27 = (f32[8,256,128]{2,1,0:T(8,128)}, f32[8,256,128]{2,1,0:T(8,128)}, u32[]{:S(2)}, u32[]{:S(2)}) collective-permute-start(f32[8,256,128]{2,1,0:T(8,128)} %get-tuple-element.178), channel_id=1, source_target_pairs={{0,8},{8,0},{16,24},{24,16},{1,9},{9,1},{17,25},{25,17},{2,10},{10... | collective-permute-start | bytes 3145736 | tf_op jit(solution)/shard_map/ppermute | solution.py:468
  376.7 122.1 %collective-permute-start.24 = (f32[8,256,128]{2,1,0:T(8,128)}, f32[8,256,128]{2,1,0:T(8,128)}, u32[]{:S(2)}, u32[]{:S(2)}) collective-permute-start(f32[8,256,128]{2,1,0:T(8,128)} %get-tuple-element.174), channel_id=1, source_target_pairs={{0,8},{8,0},{16,24},{24,16},{1,9},{9,1},{17,25},{25,17},{2,10},{10... | collective-permute-start | bytes 3145736 | tf_op jit(solution)/shard_map/ppermute | solution.py:468
  385.7 113.4 %collective-permute-start.25 = (f32[8,256,128]{2,1,0:T(8,128)}, f32[8,256,128]{2,1,0:T(8,128)}, u32[]{:S(2)}, u32[]{:S(2)}) collective-permute-start(f32[8,256,128]{2,1,0:T(8,128)} %get-tuple-element.175), channel_id=1, source_target_pairs={{0,16},{8,24},{16,0},{24,8},{1,17},{9,25},{17,1},{25,9},{2,18},{10... | collective-permute-start | bytes 3145736 | tf_op jit(solution)/shard_map/ppermute | solution.py:468
  387.2 111.9 %collective-permute-start.26 = (f32[8,256,128]{2,1,0:T(8,128)}, f32[8,256,128]{2,1,0:T(8,128)}, u32[]{:S(2)}, u32[]{:S(2)}) collective-permute-start(f32[8,256,128]{2,1,0:T(8,128)} %get-tuple-element.176), channel_id=1, source_target_pairs={{0,24},{8,16},{16,8},{24,0},{1,25},{9,17},{17,9},{25,1},{2,26},{10... | collective-permute-start | bytes 3145736 | tf_op jit(solution)/shard_map/ppermute | solution.py:468
  415.8 97.1 %all-to-all-start.2 = ((f32[64,8,16,128]{3,2,1,0:T(8,128)}), f32[64,8,16,128]{3,2,1,0:T(8,128)}, u32[]{:S(2)}, u32[]{:S(2)}) async-start(f32[64,8,16,128]{3,2,1,0:T(8,128)} %shard_map.89), calls=%async_computation.2 | async-start | bytes 8388608 | tf_op jit(solution)/shard_map/all_to_all | solution.py:585
  420.6 51.8 %collective-permute-start.28 = (f32[8,256,128]{2,1,0:T(8,128)}, f32[8,256,128]{2,1,0:T(8,128)}, u32[]{:S(2)}, u32[]{:S(2)}) collective-permute-start(f32[8,256,128]{2,1,0:T(8,128)} %get-tuple-element.179), channel_id=1, source_target_pairs={{0,16},{8,24},{16,0},{24,8},{1,17},{9,25},{17,1},{25,9},{2,18},{10... | collective-permute-start | bytes 3145736 | tf_op jit(solution)/shard_map/ppermute | solution.py:468
  421.3 72.4 %collective-permute-start.29 = (f32[8,256,128]{2,1,0:T(8,128)}, f32[8,256,128]{2,1,0:T(8,128)}, u32[]{:S(2)}, u32[]{:S(2)}) collective-permute-start(f32[8,256,128]{2,1,0:T(8,128)} %get-tuple-element.180), channel_id=1, source_target_pairs={{0,24},{8,16},{16,8},{24,0},{1,25},{9,17},{17,9},{25,1},{2,26},{10... | collective-permute-start | bytes 3145736 | tf_op jit(solution)/shard_map/ppermute | solution.py:468
  472.4 74.4 %collective-permute-start.30 = (f32[8,256,128]{2,1,0:T(8,128)}, f32[8,256,128]{2,1,0:T(8,128)}, u32[]{:S(2)}, u32[]{:S(2)}) collective-permute-start(f32[8,256,128]{2,1,0:T(8,128)} %get-tuple-element.186), channel_id=1, source_target_pairs={{0,8},{8,0},{16,24},{24,16},{1,9},{9,1},{17,25},{25,17},{2,10},{10... | collective-permute-start | bytes 3145736 | tf_op jit(solution)/shard_map/ppermute | solution.py:468
  493.6 53.2 %collective-permute-start.31 = (f32[8,256,128]{2,1,0:T(8,128)}, f32[8,256,128]{2,1,0:T(8,128)}, u32[]{:S(2)}, u32[]{:S(2)}) collective-permute-start(f32[8,256,128]{2,1,0:T(8,128)} %get-tuple-element.187), channel_id=1, source_target_pairs={{0,16},{8,24},{16,0},{24,8},{1,17},{9,25},{17,1},{25,9},{2,18},{10... | collective-permute-start | bytes 3145736 | tf_op jit(solution)/shard_map/ppermute | solution.py:468
  498.8 48.0 %collective-permute-start.32 = (f32[8,256,128]{2,1,0:T(8,128)}, f32[8,256,128]{2,1,0:T(8,128)}, u32[]{:S(2)}, u32[]{:S(2)}) collective-permute-start(f32[8,256,128]{2,1,0:T(8,128)} %get-tuple-element.188), channel_id=1, source_target_pairs={{0,24},{8,16},{16,8},{24,0},{1,25},{9,17},{17,9},{25,1},{2,26},{10... | collective-permute-start | bytes 3145736 | tf_op jit(solution)/shard_map/ppermute | solution.py:468
  533.1 1.4 collective-permute-start.33
  535.1 3.6 collective-permute-start.34
  538.7 3.6 collective-permute-start.35
  542.3 4.5 collective-permute-start.36
  546.8 49.0 %collective-permute-start.37 = (f32[8,256,128]{2,1,0:T(8,128)}, f32[8,256,128]{2,1,0:T(8,128)S(1)}, u32[]{:S(2)}, u32[]{:S(2)}) collective-permute-start(f32[8,256,128]{2,1,0:T(8,128)} %get-tuple-element.194), channel_id=1, source_target_pairs={{0,8},{8,0},{16,24},{24,16},{1,9},{9,1},{17,25},{25,17},{2,10},{10... | collective-permute-start | bytes 3145736 | tf_op jit(solution)/shard_map/ppermute | solution.py:468
  546.9 48.9 %collective-permute-start.38 = (f32[8,256,128]{2,1,0:T(8,128)}, f32[8,256,128]{2,1,0:T(8,128)S(1)}, u32[]{:S(2)}, u32[]{:S(2)}) collective-permute-start(f32[8,256,128]{2,1,0:T(8,128)} %get-tuple-element.195), channel_id=1, source_target_pairs={{0,16},{8,24},{16,0},{24,8},{1,17},{9,25},{17,1},{25,9},{2,18},{10... | collective-permute-start | bytes 3145736 | tf_op jit(solution)/shard_map/ppermute | solution.py:468
  547.6 48.2 %collective-permute-start.39 = (f32[8,256,128]{2,1,0:T(8,128)}, f32[8,256,128]{2,1,0:T(8,128)S(1)}, u32[]{:S(2)}, u32[]{:S(2)}) collective-permute-start(f32[8,256,128]{2,1,0:T(8,128)} %get-tuple-element.196), channel_id=1, source_target_pairs={{0,24},{8,16},{16,8},{24,0},{1,25},{9,17},{17,9},{25,1},{2,26},{10... | collective-permute-start | bytes 3145736 | tf_op jit(solution)/shard_map/ppermute | solution.py:468
  548.8 46.4 %collective-permute-start.40 = (f32[4,64]{1,0:T(4,128)S(1)}, f32[4,64]{1,0:T(4,128)S(1)}, u32[]{:S(2)}, u32[]{:S(2)}) collective-permute-start(f32[4,64]{1,0:T(4,128)S(1)} %add.18), channel_id=1, source_target_pairs={{0,16},{8,24},{16,0},{24,8},{1,17},{9,25},{17,1},{25,9},{2,18},{10... | collective-permute-start | bytes 3080 | tf_op jit(solution)/shard_map/ppermute | solution.py:516
  (12 other events, 140.2 us)

commit v5 on v4

--- a/solution.py
+++ b/solution.py
@@ -538,7 +538,7 @@
         cut_pieces(density, seats, parts, chunk, size, list(state_cut[-1][:1]) if chunk else [])
         for chunk in range(chunks)
     ]
-    rho_there = [swap(pieces, parts) for pieces in (rho[:2] if chunks > 3 else rho)]
+    rho_there = [swap(pieces, parts) for pieces in rho]
     ahead = parts // 2
     state_cut[0], rho_there[0][ahead] = lax.optimization_barrier(
         (state_cut[0], rho_there[0][ahead])
@@ -559,7 +559,7 @@
             out, rho_there[-1] = lax.optimization_barrier((out, rho_there[-1]))
         grads.append(grad)
         if chunk == chunks - 1:
-            total = add_rounds(device_grad(grads, seats, parts, []), total_rounds()[:-1])
+            total = add_rounds(device_grad(grads, seats, parts, []), total_rounds())
             out, made[-1:], total = lax.optimization_barrier((out, made[-1:], total))
             totals.append(total)
         if chunk > 0 or chunks < 4:
@@ -578,8 +578,6 @@
         if chunk + 1 == len(state) < chunks:
             pieces, field = lax.optimization_barrier((state_cut[chunk + 1], field))
             state.append(swap(pieces, parts))
-            pieces, state[-1] = lax.optimization_barrier((rho[2], state[-1]))
-            rho_there += [swap(pieces, parts), swap(rho[3], parts)]
             out, rho_there[2] = lax.optimization_barrier((closed[0], rho_there[2]))
             made.append(swap(out, parts))
         fields.append(lax.all_to_all(field, "dev", split_axis=0, concat_axis=0, tiled=True))
@@ -588,8 +586,7 @@
         while len(made) < min(max(chunk + 2, chunks - 1), chunks):
             close(len(made), [whole] if 0 < chunk == chunks - 2 else [])
         whole = place_pieces(made[chunk], seats, whole, chunk, shape, size, closed[-1][0])
-    grad = add_rounds(totals[0], total_rounds()[-1:])
-    return whole.reshape(costate.shape), grad.reshape(2, 2, LEVELS)
+    return whole.reshape(costate.shape), totals[0].reshape(2, 2, LEVELS)
 
 
 def solution(mesh):

time: 603 us -> 592 us (0.982)
  waiting for transfers between devices: 372 us -> 360 us
    ppermute x36, waiting for transfers between devices: 245 us -> 324 us  [swap(): moved.append(lax.ppermute(pieces[step], 'grp', pairs))]
    all_to_all x4, waiting for transfers between devices: 74.6 us -> 23.1 us  [per_device(): lax.all_to_all(field, 'dev', split_axis=0, concat_axis=0, tiled=True)]
    ppermute x5, waiting for transfers between devices: 52.8 us -> 12.5 us  [add_rounds(): value = value + lax.ppermute(value, axis, pairs)]
  transfers between devices with their start and end apart: 45 -> 45, of which waited for: 22 -> 23; matrix products, arithmetic and copies ran while one was open for 0% -> 0% of each run, Pallas kernels for 25% -> 26%
where the time goes in v5:
time: 592 us; the launch traced here: 591 us
  waiting for transfers between devices  360 us (61%)
  Pallas kernels  168 us (28%)
  starting transfers between devices  56.7 us (10%)
    ppermute x36, waiting for transfers between devices, swap(): moved.append(lax.ppermute(pieces[step], 'grp', pairs))  324 us
    pallas_call x4, Pallas kernels, close_columns(): pl.pallas_call(functools.partial(close_kernel, parts, size), grid=(firsts...  71.3 us
    pallas_call x4, Pallas kernels, turn_columns(): pl.pallas_call(functools.partial(turn_kernel, parts, size, group), grid=(...  30.2 us
    ppermute x36, starting transfers between devices, swap(): moved.append(lax.ppermute(pieces[step], 'grp', pairs))  29.6 us
    all_to_all x4, waiting for transfers between devices, per_device(): lax.all_to_all(field, 'dev', split_axis=0, concat_axis=0, tiled=True)  23.1 us
    all_to_all x4, starting transfers between devices, per_device(): lax.all_to_all(field, 'dev', split_axis=0, concat_axis=0, tiled=True)  22.9 us
    pallas_call x1, Pallas kernels, open_state(): pl.pallas_call(functools.partial(open_kernel, count, len(waited)), grid=(...  19.5 us
    pallas_call x4, Pallas kernels, cut_pieces(): pl.pallas_call(functools.partial(cut_kernel, size, len(waited)), grid=(fi...  14.9 us
  transfers between devices with their start and end apart: 45, of which 23 were waited for; matrix products, arithmetic and copies ran while one was open for 0% of the time, Pallas kernels for 26%

profile of v5, /device:TPU:0, one launch (start us, length us, event | category | flops | bytes accessed | tf_op | source)
XLA Modules:
  0.0 591.2 jit_solution(3823006984287159267)
XLA Ops:
  0.6 3.8 shard_map.82
  4.4 2.9 collective-permute-start.6
  8.0 4.6 shard_map.77
  12.6 10.4 %shard_map.78 = (f32[8,256,128]{2,1,0:T(8,128)}, f32[8,256,128]{2,1,0:T(8,128)}, f32[8,256,128]{2,1,0:T(8,128)}, f32[8,256,128]{2,1,0:T(8,128)}) custom-call(bf16[512,128]{1,0:T(8,128)(2,1)} %get-tuple-element.98.weight_ref, f32[2,1024,2048]{2,1,0:T(8,128)} %field_ref.3), custom_call_target="tpu_custom_call" | custom-call | flops 1024 | bytes 1024 | tf_op jit(solution)/shard_map/pallas_call | solution.py:210
  23.0 7.7 %collective-permute-done.6.refs_2_ = f32[8,256,128]{2,1,0:T(8,128)S(1)} collective-permute-done((f32[8,256,128]{2,1,0:T(8,128)}, f32[8,256,128]{2,1,0:T(8,128)S(1)}, u32[]{:S(2)}, u32[]{:S(2)}) %collective-permute-start.6) | collective-permute-done | bytes 1048608 | tf_op jit(solution)/shard_map/ppermute | solution.py:468
  34.3 19.5 %shard_map.79 = (f32[8,256,128]{2,1,0:T(8,128)}, f32[8,256,128]{2,1,0:T(8,128)}, f32[8,256,128]{2,1,0:T(8,128)}, f32[8,256,128]{2,1,0:T(8,128)}, f32[8,256,128]{...) custom-call(bf16[2,192,256]{2,1,0:T(8,128)(2,1)} %slice.3.weight_ref, ...), custom_call_target="tpu_custom_call" | custom-call | flops 1024 | bytes 1024 | tf_op jit(solution)/shard_map/pallas_call | solution.py:235
  53.8 4.1 collective-permute-done.8.refs_2_
  57.9 21.7 %collective-permute-done.9.refs_3_ = f32[8,256,128]{2,1,0:T(8,128)S(1)} collective-permute-done((f32[8,256,128]{2,1,0:T(8,128)}, f32[8,256,128]{2,1,0:T(8,128)S(1)}, u32[]{:S(2)}, u32[]{:S(2)}) %collective-permute-start.9) | collective-permute-done | bytes 1048608 | tf_op jit(solution)/shard_map/ppermute | solution.py:468
  80.6 7.5 %shard_map.83.refs_5_ = f32[64,8,16,128]{3,2,1,0:T(8,128)} custom-call(bf16[256,256]{1,0:T(8,128)(2,1)} %get-tuple-element.96.weight_ref, f32[8,256,128]{2,1,0:T(8,128)} %get-tuple-element.118.refs_0_, f32[8,256,128]{2,1,0:T(8,128)} %copy-done.8, f32[8,256,128]{2,1,0:T(8,128)} %copy-done.9, f32[8,256,128]{2,1,0:T(8,128)} %copy-done.10, ...), custom_call_target="tpu_custom_call" | custom-call | flops 1024 | bytes 1024 | tf_op jit(solution)/shard_map/pallas_call | solution.py:336
  88.1 6.1 %all-to-all-start = ((f32[64,8,16,128]{3,2,1,0:T(8,128)}), f32[64,8,16,128]{3,2,1,0:T(8,128)}, u32[]{:S(2)}, u32[]{:S(2)}) async-start(f32[64,8,16,128]{3,2,1,0:T(8,128)} %shard_map.83.refs_5_), calls=%async_computation | async-start | bytes 8388608 | tf_op jit(solution)/shard_map/all_to_all | solution.py:583
  98.0 3.7 shard_map.81
  101.7 3.7 shard_map.80
  105.4 15.0 %collective-permute-done.4.refs_2_ = f32[8,256,128]{2,1,0:T(8,128)S(1)} collective-permute-done((f32[8,256,128]{2,1,0:T(8,128)}, f32[8,256,128]{2,1,0:T(8,128)S(1)}, u32[]{:S(2)}, u32[]{:S(2)}) %collective-permute-start.4) | collective-permute-done | bytes 1048608 | tf_op jit(solution)/shard_map/ppermute | solution.py:468
  121.9 20.1 %collective-permute-done.5.refs_3_ = f32[8,256,128]{2,1,0:T(8,128)S(1)} collective-permute-done((f32[8,256,128]{2,1,0:T(8,128)}, f32[8,256,128]{2,1,0:T(8,128)S(1)}, u32[]{:S(2)}, u32[]{:S(2)}) %collective-permute-start.5) | collective-permute-done | bytes 1048608 | tf_op jit(solution)/shard_map/ppermute | solution.py:468
  142.0 2.2 collective-permute-start.2
  144.2 7.5 %shard_map.84.refs_5_ = f32[64,8,16,128]{3,2,1,0:T(8,128)} custom-call(bf16[256,256]{1,0:T(8,128)(2,1)} %get-tuple-element.96.weight_ref, f32[8,256,128]{2,1,0:T(8,128)} %get-tuple-element.109.refs_5_.refs_0_, f32[8,256,128]{2,1,0:T(8,128)} %copy-done.5, f32[8,256,128]{2,1,0:T(8,128)} %copy-done.6, f32[8,256,128]{2,1,0:T(8,128)} %copy-done.7, ...), custom_call_target="tpu_custom_call" | custom-call | flops 1024 | bytes 1024 | tf_op jit(solution)/shard_map/pallas_call | solution.py:336
  151.8 12.8 %collective-permute-done.11.refs_3_ = f32[8,256,128]{2,1,0:T(8,128)} collective-permute-done((f32[8,256,128]{2,1,0:T(8,128)}, f32[8,256,128]{2,1,0:T(8,128)}, u32[]{:S(2)}, u32[]{:S(2)}) %collective-permute-start.11) | collective-permute-done | bytes 1048608 | tf_op jit(solution)/shard_map/ppermute | solution.py:468
  166.6 21.2 %all-to-all-done = f32[64,8,16,128]{3,2,1,0:T(8,128)} async-done(((f32[64,8,16,128]{3,2,1,0:T(8,128)}), f32[64,8,16,128]{3,2,1,0:T(8,128)}, u32[]{:S(2)}, u32[]{:S(2)}) %all-to-all-start) | async-done | bytes 4194336 | tf_op jit(solution)/shard_map/all_to_all | solution.py:583
  187.8 4.8 all-to-all-start.1
  192.6 17.8 %shard_map.85 = (f32[8,256,128]{2,1,0:T(8,128)}, f32[8,256,128]{2,1,0:T(8,128)}, f32[8,256,128]{2,1,0:T(8,128)}, f32[8,256,128]{2,1,0:T(8,128)}, f32[2,64,128]{2,1,0:T(8,128)}) custom-call(bf16[3,2,256,256]{3,2,1,0:T(8,128)(2,1)} %get-tuple-element.94.lane_ref, bf16[3,256,256]{2,1,0:T(8,128)(2,1)} %get-tuple-element.95.level_ref, ...), custom_call_target="tpu_custom_call" | custom-call | flops 199999995904 | bytes 1024 | tf_op jit(solution)/shard_map/pallas_call | solution.py:408
  212.0 7.6 %shard_map.86.refs_5_ = f32[64,8,16,128]{3,2,1,0:T(8,128)} custom-call(bf16[256,256]{1,0:T(8,128)(2,1)} %get-tuple-element.96.weight_ref, f32[8,256,128]{2,1,0:T(8,128)} %get-tuple-element.104.refs_0_, f32[8,256,128]{2,1,0:T(8,128)} %collective-permute-done.refs_1_, f32[8,256,128]{2,1,0:T(8,128)} %collective-permute-done.1.refs_2_, ...), custom_call_target="tpu_custom_call" | custom-call | flops 1024 | bytes 1024 | tf_op jit(solution)/shard_map/pallas_call | solution.py:336
  219.9 12.9 %collective-permute-done.19.refs_2_ = f32[8,256,128]{2,1,0:T(8,128)} collective-permute-done((f32[8,256,128]{2,1,0:T(8,128)}, f32[8,256,128]{2,1,0:T(8,128)}, u32[]{:S(2)}, u32[]{:S(2)}) %collective-permute-start.19) | collective-permute-done | bytes 1048608 | tf_op jit(solution)/shard_map/ppermute | solution.py:468
  232.9 21.5 %collective-permute-done.20.refs_3_ = f32[8,256,128]{2,1,0:T(8,128)} collective-permute-done((f32[8,256,128]{2,1,0:T(8,128)}, f32[8,256,128]{2,1,0:T(8,128)}, u32[]{:S(2)}, u32[]{:S(2)}) %collective-permute-start.20) | collective-permute-done | bytes 1048608 | tf_op jit(solution)/shard_map/ppermute | solution.py:468
  255.9 3.7 shard_map.87
  260.3 17.5 %collective-permute-done.16.refs_2_ = f32[8,256,128]{2,1,0:T(8,128)} collective-permute-done((f32[8,256,128]{2,1,0:T(8,128)}, f32[8,256,128]{2,1,0:T(8,128)}, u32[]{:S(2)}, u32[]{:S(2)}) %collective-permute-start.16) | collective-permute-done | bytes 1048608 | tf_op jit(solution)/shard_map/ppermute | solution.py:468
  279.3 20.0 %collective-permute-done.17.refs_3_ = f32[8,256,128]{2,1,0:T(8,128)} collective-permute-done((f32[8,256,128]{2,1,0:T(8,128)}, f32[8,256,128]{2,1,0:T(8,128)}, u32[]{:S(2)}, u32[]{:S(2)}) %collective-permute-start.17) | collective-permute-done | bytes 1048608 | tf_op jit(solution)/shard_map/ppermute | solution.py:468
  301.2 5.9 %all-to-all-start.3 = ((f32[64,8,16,128]{3,2,1,0:T(8,128)}), f32[64,8,16,128]{3,2,1,0:T(8,128)}, u32[]{:S(2)}, u32[]{:S(2)}) async-start(f32[64,8,16,128]{3,2,1,0:T(8,128)} %shard_map.86.refs_5_), calls=%async_computation.3 | async-start | bytes 8388608 | tf_op jit(solution)/shard_map/all_to_all | solution.py:583
  307.2 15.4 %collective-permute-done.13.refs_2_ = f32[8,256,128]{2,1,0:T(8,128)S(1)} collective-permute-done((f32[8,256,128]{2,1,0:T(8,128)S(1)}, f32[8,256,128]{2,1,0:T(8,128)S(1)}, u32[]{:S(2)}, u32[]{:S(2)}) %collective-permute-start.13) | collective-permute-done | bytes 1048608 | tf_op jit(solution)/shard_map/ppermute | solution.py:468
  322.6 18.1 %shard_map.88 = (f32[8,256,128]{2,1,0:T(8,128)}, f32[8,256,128]{2,1,0:T(8,128)}, f32[8,256,128]{2,1,0:T(8,128)}, f32[8,256,128]{2,1,0:T(8,128)}, f32[2,64,128]{2,1,0:T(8,128)}) custom-call(bf16[3,2,256,256]{3,2,1,0:T(8,128)(2,1)} %get-tuple-element.94.lane_ref, bf16[3,256,256]{2,1,0:T(8,128)(2,1)} %get-tuple-element.95.level_ref, ...), custom_call_target="tpu_custom_call" | custom-call | flops 199999995904 | bytes 1024 | tf_op jit(solution)/shard_map/pallas_call | solution.py:408
  340.7 48.5 %collective-permute-done.14.refs_3_ = f32[8,256,128]{2,1,0:T(8,128)} collective-permute-done((f32[8,256,128]{2,1,0:T(8,128)}, f32[8,256,128]{2,1,0:T(8,128)}, u32[]{:S(2)}, u32[]{:S(2)}) %collective-permute-start.14) | collective-permute-done | bytes 1048608 | tf_op jit(solution)/shard_map/ppermute | solution.py:468
  389.5 7.6 %shard_map.89 = f32[64,8,16,128]{3,2,1,0:T(8,128)} custom-call(bf16[256,256]{1,0:T(8,128)(2,1)} %get-tuple-element.96.weight_ref, f32[8,256,128]{2,1,0:T(8,128)} %get-tuple-element.127.refs_0_, f32[8,256,128]{2,1,0:T(8,128)} %copy-done, f32[8,256,128]{2,1,0:T(8,128)} %copy-done.1, f32[8,256,128]{2,1,0:T(8,128)} %collective-permute-done.14.refs_3_, ...), custom_call_target="tpu_custom_call" | custom-call | flops 1024 | bytes 1024 | tf_op jit(solution)/shard_map/pallas_call | solution.py:336
  400.7 6.2 %all-to-all-start.2 = ((f32[64,8,16,128]{3,2,1,0:T(8,128)}), f32[64,8,16,128]{3,2,1,0:T(8,128)}, u32[]{:S(2)}, u32[]{:S(2)}) async-start(f32[64,8,16,128]{3,2,1,0:T(8,128)} %shard_map.89), calls=%async_computation.2 | async-start | bytes 8388608 | tf_op jit(solution)/shard_map/all_to_all | solution.py:583
  406.9 17.8 %shard_map.90 = (f32[8,256,128]{2,1,0:T(8,128)}, f32[8,256,128]{2,1,0:T(8,128)}, f32[8,256,128]{2,1,0:T(8,128)}, f32[8,256,128]{2,1,0:T(8,128)}, f32[2,64,128]{2,1,0:T(8,128)}) custom-call(bf16[3,2,256,256]{3,2,1,0:T(8,128)(2,1)} %get-tuple-element.94.lane_ref, bf16[3,256,256]{2,1,0:T(8,128)(2,1)} %get-tuple-element.95.level_ref, ...), custom_call_target="tpu_custom_call" | custom-call | flops 199999995904 | bytes 1024 | tf_op jit(solution)/shard_map/pallas_call | solution.py:408
  424.7 43.7 %collective-permute-done.28.refs_2_ = f32[8,256,128]{2,1,0:T(8,128)} collective-permute-done((f32[8,256,128]{2,1,0:T(8,128)}, f32[8,256,128]{2,1,0:T(8,128)}, u32[]{:S(2)}, u32[]{:S(2)}) %collective-permute-start.28) | collective-permute-done | bytes 1048608 | tf_op jit(solution)/shard_map/ppermute | solution.py:468
  468.4 21.0 %collective-permute-done.29.refs_3_ = f32[8,256,128]{2,1,0:T(8,128)} collective-permute-done((f32[8,256,128]{2,1,0:T(8,128)}, f32[8,256,128]{2,1,0:T(8,128)}, u32[]{:S(2)}, u32[]{:S(2)}) %collective-permute-start.29) | collective-permute-done | bytes 1048608 | tf_op jit(solution)/shard_map/ppermute | solution.py:468
  490.7 3.7 shard_map.91.refs_4_
  495.0 3.7 shard_map.92.refs_4_
  498.6 1.9 all-to-all-done.2
  500.6 17.7 %shard_map.93 = (f32[8,256,128]{2,1,0:T(8,128)}, f32[8,256,128]{2,1,0:T(8,128)}, f32[8,256,128]{2,1,0:T(8,128)}, f32[8,256,128]{2,1,0:T(8,128)}, f32[2,64,128]{2,1,0:T(8,128)}) custom-call(bf16[3,2,256,256]{3,2,1,0:T(8,128)(2,1)} %get-tuple-element.94.lane_ref, bf16[3,256,256]{2,1,0:T(8,128)(2,1)} %get-tuple-element.95.level_ref, ...), custom_call_target="tpu_custom_call" | custom-call | flops 199999995904 | bytes 1024 | tf_op jit(solution)/shard_map/pallas_call | solution.py:408
  518.3 2.4 shard_map.94
  524.3 2.1 collective-permute-done.34
  526.5 3.4 collective-permute-done.35
  531.1 3.4 collective-permute-done.36
  535.8 2.3 collective-permute-done.37
  540.5 3.7 shard_map.95.refs_4_
  544.2 20.7 %collective-permute-done.39.refs_2_ = f32[8,256,128]{2,1,0:T(8,128)S(1)} collective-permute-done((f32[8,256,128]{2,1,0:T(8,128)}, f32[8,256,128]{2,1,0:T(8,128)S(1)}, u32[]{:S(2)}, u32[]{:S(2)}) %collective-permute-start.39) | collective-permute-done | bytes 1048608 | tf_op jit(solution)/shard_map/ppermute | solution.py:468
  564.9 21.6 %collective-permute-done.40.refs_3_ = f32[8,256,128]{2,1,0:T(8,128)S(1)} collective-permute-done((f32[8,256,128]{2,1,0:T(8,128)}, f32[8,256,128]{2,1,0:T(8,128)S(1)}, u32[]{:S(2)}, u32[]{:S(2)}) %collective-permute-start.40) | collective-permute-done | bytes 1048608 | tf_op jit(solution)/shard_map/ppermute | solution.py:468
  587.5 3.7 shard_map.96
  (96 shorter events, 35.0 us)
Async XLA Ops:
  4.4 26.3 %collective-permute-start.6 = (f32[8,256,128]{2,1,0:T(8,128)}, f32[8,256,128]{2,1,0:T(8,128)S(1)}, u32[]{:S(2)}, u32[]{:S(2)}) collective-permute-start(f32[8,256,128]{2,1,0:T(8,128)} %get-tuple-element.117), channel_id=1, source_target_pairs={{0,16},{8,24},{16,0},{24,8},{1,17},{9,25},{17,1},{25,9},{2,18},{10... | collective-permute-start | bytes 3145736 | tf_op jit(solution)/shard_map/ppermute | solution.py:468
  31.7 22.1 %collective-permute-start.7 = (f32[8,256,128]{2,1,0:T(8,128)}, f32[8,256,128]{2,1,0:T(8,128)S(1)}, u32[]{:S(2)}, u32[]{:S(2)}) collective-permute-start(f32[8,256,128]{2,1,0:T(8,128)} %get-tuple-element.119), channel_id=1, source_target_pairs={{0,8},{8,0},{16,24},{24,16},{1,9},{9,1},{17,25},{25,17},{2,10},{10... | collective-permute-start | bytes 3145736 | tf_op jit(solution)/shard_map/ppermute | solution.py:468
  31.7 26.2 %collective-permute-start.8 = (f32[8,256,128]{2,1,0:T(8,128)}, f32[8,256,128]{2,1,0:T(8,128)S(1)}, u32[]{:S(2)}, u32[]{:S(2)}) collective-permute-start(f32[8,256,128]{2,1,0:T(8,128)} %get-tuple-element.120), channel_id=1, source_target_pairs={{0,16},{8,24},{16,0},{24,8},{1,17},{9,25},{17,1},{25,9},{2,18},{10... | collective-permute-start | bytes 3145736 | tf_op jit(solution)/shard_map/ppermute | solution.py:468
  33.5 46.1 %collective-permute-start.9 = (f32[8,256,128]{2,1,0:T(8,128)}, f32[8,256,128]{2,1,0:T(8,128)S(1)}, u32[]{:S(2)}, u32[]{:S(2)}) collective-permute-start(f32[8,256,128]{2,1,0:T(8,128)} %get-tuple-element.121), channel_id=1, source_target_pairs={{0,24},{8,16},{16,8},{24,0},{1,25},{9,17},{17,9},{25,1},{2,26},{10... | collective-permute-start | bytes 3145736 | tf_op jit(solution)/shard_map/ppermute | solution.py:468
  88.1 99.8 %all-to-all-start = ((f32[64,8,16,128]{3,2,1,0:T(8,128)}), f32[64,8,16,128]{3,2,1,0:T(8,128)}, u32[]{:S(2)}, u32[]{:S(2)}) async-start(f32[64,8,16,128]{3,2,1,0:T(8,128)} %shard_map.83.refs_5_), calls=%async_computation | async-start | bytes 8388608 | tf_op jit(solution)/shard_map/all_to_all | solution.py:583
  94.2 3.5 collective-permute-start.3
  94.2 26.2 %collective-permute-start.4 = (f32[8,256,128]{2,1,0:T(8,128)}, f32[8,256,128]{2,1,0:T(8,128)S(1)}, u32[]{:S(2)}, u32[]{:S(2)}) collective-permute-start(f32[8,256,128]{2,1,0:T(8,128)} %get-tuple-element.111), channel_id=1, source_target_pairs={{0,16},{8,24},{16,0},{24,8},{1,17},{9,25},{17,1},{25,9},{2,18},{10... | collective-permute-start | bytes 3145736 | tf_op jit(solution)/shard_map/ppermute | solution.py:468
  95.7 46.3 %collective-permute-start.5 = (f32[8,256,128]{2,1,0:T(8,128)}, f32[8,256,128]{2,1,0:T(8,128)S(1)}, u32[]{:S(2)}, u32[]{:S(2)}) collective-permute-start(f32[8,256,128]{2,1,0:T(8,128)} %get-tuple-element.112), channel_id=1, source_target_pairs={{0,24},{8,16},{16,8},{24,0},{1,25},{9,17},{17,9},{25,1},{2,26},{10... | collective-permute-start | bytes 3145736 | tf_op jit(solution)/shard_map/ppermute | solution.py:468
  96.0 55.7 %collective-permute-start.10 = (f32[8,256,128]{2,1,0:T(8,128)}, f32[8,256,128]{2,1,0:T(8,128)}, u32[]{:S(2)}, u32[]{:S(2)}) collective-permute-start(f32[8,256,128]{2,1,0:T(8,128)} %get-tuple-element.123), channel_id=1, source_target_pairs={{0,8},{8,0},{16,24},{24,16},{1,9},{9,1},{17,25},{25,17},{2,10},{10... | collective-permute-start | bytes 3145736 | tf_op jit(solution)/shard_map/ppermute | solution.py:468
  96.4 68.1 %collective-permute-start.11 = (f32[8,256,128]{2,1,0:T(8,128)}, f32[8,256,128]{2,1,0:T(8,128)}, u32[]{:S(2)}, u32[]{:S(2)}) collective-permute-start(f32[8,256,128]{2,1,0:T(8,128)} %get-tuple-element.125), channel_id=1, source_target_pairs={{0,24},{8,16},{16,8},{24,0},{1,25},{9,17},{17,9},{25,1},{2,26},{10... | collective-permute-start | bytes 3145736 | tf_op jit(solution)/shard_map/ppermute | solution.py:468
  97.6 68.4 %collective-permute-start = (f32[8,256,128]{2,1,0:T(8,128)}, f32[8,256,128]{2,1,0:T(8,128)}, u32[]{:S(2)}, u32[]{:S(2)}) collective-permute-start(f32[8,256,128]{2,1,0:T(8,128)} %get-tuple-element.105), channel_id=1, source_target_pairs={{0,8},{8,0},{16,24},{24,16},{1,9},{9,1},{17,25},{25,17},{2,10},{10... | collective-permute-start | bytes 3145736 | tf_op jit(solution)/shard_map/ppermute | solution.py:468
  120.4 90.0 %collective-permute-start.1 = (f32[8,256,128]{2,1,0:T(8,128)}, f32[8,256,128]{2,1,0:T(8,128)}, u32[]{:S(2)}, u32[]{:S(2)}) collective-permute-start(f32[8,256,128]{2,1,0:T(8,128)} %get-tuple-element.106), channel_id=1, source_target_pairs={{0,16},{8,24},{16,0},{24,8},{1,17},{9,25},{17,1},{25,9},{2,18},{10... | collective-permute-start | bytes 3145736 | tf_op jit(solution)/shard_map/ppermute | solution.py:468
  142.0 68.5 %collective-permute-start.2 = (f32[8,256,128]{2,1,0:T(8,128)}, f32[8,256,128]{2,1,0:T(8,128)}, u32[]{:S(2)}, u32[]{:S(2)}) collective-permute-start(f32[8,256,128]{2,1,0:T(8,128)} %get-tuple-element.107), channel_id=1, source_target_pairs={{0,24},{8,16},{16,8},{24,0},{1,25},{9,17},{17,9},{25,1},{2,26},{10... | collective-permute-start | bytes 3145736 | tf_op jit(solution)/shard_map/ppermute | solution.py:468
  151.8 67.9 %collective-permute-start.18 = (f32[8,256,128]{2,1,0:T(8,128)}, f32[8,256,128]{2,1,0:T(8,128)}, u32[]{:S(2)}, u32[]{:S(2)}) collective-permute-start(f32[8,256,128]{2,1,0:T(8,128)} %get-tuple-element.140), channel_id=1, source_target_pairs={{0,8},{8,0},{16,24},{24,16},{1,9},{9,1},{17,25},{25,17},{2,10},{10... | collective-permute-start | bytes 3145736 | tf_op jit(solution)/shard_map/ppermute | solution.py:468
  164.5 68.3 %collective-permute-start.19 = (f32[8,256,128]{2,1,0:T(8,128)}, f32[8,256,128]{2,1,0:T(8,128)}, u32[]{:S(2)}, u32[]{:S(2)}) collective-permute-start(f32[8,256,128]{2,1,0:T(8,128)} %get-tuple-element.141), channel_id=1, source_target_pairs={{0,16},{8,24},{16,0},{24,8},{1,17},{9,25},{17,1},{25,9},{2,18},{10... | collective-permute-start | bytes 3145736 | tf_op jit(solution)/shard_map/ppermute | solution.py:468
  166.0 88.4 %collective-permute-start.20 = (f32[8,256,128]{2,1,0:T(8,128)}, f32[8,256,128]{2,1,0:T(8,128)}, u32[]{:S(2)}, u32[]{:S(2)}) collective-permute-start(f32[8,256,128]{2,1,0:T(8,128)} %get-tuple-element.142), channel_id=1, source_target_pairs={{0,24},{8,16},{16,8},{24,0},{1,25},{9,17},{17,9},{25,1},{2,26},{10... | collective-permute-start | bytes 3145736 | tf_op jit(solution)/shard_map/ppermute | solution.py:468
  187.8 113.4 %all-to-all-start.1 = ((f32[64,8,16,128]{3,2,1,0:T(8,128)}), f32[64,8,16,128]{3,2,1,0:T(8,128)}, u32[]{:S(2)}, u32[]{:S(2)}) async-start(f32[64,8,16,128]{3,2,1,0:T(8,128)} %shard_map.84.refs_5_), calls=%async_computation.1 | async-start | bytes 8388608 | tf_op jit(solution)/shard_map/all_to_all | solution.py:583
  210.4 49.2 %collective-permute-start.15 = (f32[8,256,128]{2,1,0:T(8,128)}, f32[8,256,128]{2,1,0:T(8,128)}, u32[]{:S(2)}, u32[]{:S(2)}) collective-permute-start(f32[8,256,128]{2,1,0:T(8,128)} %get-tuple-element.133), channel_id=1, source_target_pairs={{0,8},{8,0},{16,24},{24,16},{1,9},{9,1},{17,25},{25,17},{2,10},{10... | collective-permute-start | bytes 3145736 | tf_op jit(solution)/shard_map/ppermute | solution.py:468
  210.5 67.3 %collective-permute-start.16 = (f32[8,256,128]{2,1,0:T(8,128)}, f32[8,256,128]{2,1,0:T(8,128)}, u32[]{:S(2)}, u32[]{:S(2)}) collective-permute-start(f32[8,256,128]{2,1,0:T(8,128)} %get-tuple-element.134), channel_id=1, source_target_pairs={{0,16},{8,24},{16,0},{24,8},{1,17},{9,25},{17,1},{25,9},{2,18},{10... | collective-permute-start | bytes 3145736 | tf_op jit(solution)/shard_map/ppermute | solution.py:468
  212.0 42.4 %copy-start.12 = (f32[8,256,128]{2,1,0:T(8,128)S(1)}, f32[8,256,128]{2,1,0:T(8,128)}, u32[]{:S(2)}) copy-start(f32[8,256,128]{2,1,0:T(8,128)} %get-tuple-element.129) | copy-start | bytes 3145732
  219.6 79.7 %collective-permute-start.17 = (f32[8,256,128]{2,1,0:T(8,128)}, f32[8,256,128]{2,1,0:T(8,128)}, u32[]{:S(2)}, u32[]{:S(2)}) collective-permute-start(f32[8,256,128]{2,1,0:T(8,128)} %get-tuple-element.135), channel_id=1, source_target_pairs={{0,24},{8,16},{16,8},{24,0},{1,25},{9,17},{17,9},{25,1},{2,26},{10... | collective-permute-start | bytes 3145736 | tf_op jit(solution)/shard_map/ppermute | solution.py:468
  232.9 74.3 %collective-permute-start.12 = (f32[8,256,128]{2,1,0:T(8,128)}, f32[8,256,128]{2,1,0:T(8,128)S(1)}, u32[]{:S(2)}, u32[]{:S(2)}) collective-permute-start(f32[8,256,128]{2,1,0:T(8,128)} %get-tuple-element.128), channel_id=1, source_target_pairs={{0,8},{8,0},{16,24},{24,16},{1,9},{9,1},{17,25},{25,17},{2,10},{10... | collective-permute-start | bytes 3145736 | tf_op jit(solution)/shard_map/ppermute | solution.py:468
  254.4 68.2 %collective-permute-start.13 = (f32[8,256,128]{2,1,0:T(8,128)S(1)}, f32[8,256,128]{2,1,0:T(8,128)S(1)}, u32[]{:S(2)}, u32[]{:S(2)}) collective-permute-start(f32[8,256,128]{2,1,0:T(8,128)S(1)} %copy-done.12), channel_id=1, source_target_pairs={{0,16},{8,24},{16,0},{24,8},{1,17},{9,25},{17,1},{25,9},{2,18},{10... | collective-permute-start | bytes 3145736 | tf_op jit(solution)/shard_map/ppermute | solution.py:468
  259.6 137.5 %collective-permute-start.21 = (f32[8,256,128]{2,1,0:T(8,128)}, f32[8,256,128]{2,1,0:T(8,128)}, u32[]{:S(2)}, u32[]{:S(2)}) collective-permute-start(f32[8,256,128]{2,1,0:T(8,128)} %get-tuple-element.151), channel_id=1, source_target_pairs={{0,8},{8,0},{16,24},{24,16},{1,9},{9,1},{17,25},{25,17},{2,10},{10... | collective-permute-start | bytes 3145736 | tf_op jit(solution)/shard_map/ppermute | solution.py:468
  277.8 121.1 %collective-permute-start.22 = (f32[8,256,128]{2,1,0:T(8,128)}, f32[8,256,128]{2,1,0:T(8,128)}, u32[]{:S(2)}, u32[]{:S(2)}) collective-permute-start(f32[8,256,128]{2,1,0:T(8,128)} %get-tuple-element.152), channel_id=1, source_target_pairs={{0,16},{8,24},{16,0},{24,8},{1,17},{9,25},{17,1},{25,9},{2,18},{10... | collective-permute-start | bytes 3145736 | tf_op jit(solution)/shard_map/ppermute | solution.py:468
  299.3 99.6 %collective-permute-start.23 = (f32[8,256,128]{2,1,0:T(8,128)}, f32[8,256,128]{2,1,0:T(8,128)}, u32[]{:S(2)}, u32[]{:S(2)}) collective-permute-start(f32[8,256,128]{2,1,0:T(8,128)} %get-tuple-element.153), channel_id=1, source_target_pairs={{0,24},{8,16},{16,8},{24,0},{1,25},{9,17},{17,9},{25,1},{2,26},{10... | collective-permute-start | bytes 3145736 | tf_op jit(solution)/shard_map/ppermute | solution.py:468
  301.2 99.5 %all-to-all-start.3 = ((f32[64,8,16,128]{3,2,1,0:T(8,128)}), f32[64,8,16,128]{3,2,1,0:T(8,128)}, u32[]{:S(2)}, u32[]{:S(2)}) async-start(f32[64,8,16,128]{3,2,1,0:T(8,128)} %shard_map.86.refs_5_), calls=%async_computation.3 | async-start | bytes 8388608 | tf_op jit(solution)/shard_map/all_to_all | solution.py:583
  307.1 33.6 %copy-start = (f32[8,256,128]{2,1,0:T(8,128)}, f32[8,256,128]{2,1,0:T(8,128)S(1)}, u32[]{:S(2)}) copy-start(f32[8,256,128]{2,1,0:T(8,128)S(1)} %collective-permute-done.12.refs_1_) | copy-start | bytes 3145732
  307.1 82.1 %collective-permute-start.14 = (f32[8,256,128]{2,1,0:T(8,128)}, f32[8,256,128]{2,1,0:T(8,128)}, u32[]{:S(2)}, u32[]{:S(2)}) collective-permute-start(f32[8,256,128]{2,1,0:T(8,128)} %get-tuple-element.130), channel_id=1, source_target_pairs={{0,24},{8,16},{16,8},{24,0},{1,25},{9,17},{17,9},{25,1},{2,26},{10... | collective-permute-start | bytes 3145736 | tf_op jit(solution)/shard_map/ppermute | solution.py:468
  322.6 77.6 %collective-permute-start.27 = (f32[8,256,128]{2,1,0:T(8,128)}, f32[8,256,128]{2,1,0:T(8,128)}, u32[]{:S(2)}, u32[]{:S(2)}) collective-permute-start(f32[8,256,128]{2,1,0:T(8,128)} %get-tuple-element.162), channel_id=1, source_target_pairs={{0,8},{8,0},{16,24},{24,16},{1,9},{9,1},{17,25},{25,17},{2,10},{10... | collective-permute-start | bytes 3145736 | tf_op jit(solution)/shard_map/ppermute | solution.py:468
  389.2 105.2 %collective-permute-start.24 = (f32[8,256,128]{2,1,0:T(8,128)}, f32[8,256,128]{2,1,0:T(8,128)}, u32[]{:S(2)}, u32[]{:S(2)}) collective-permute-start(f32[8,256,128]{2,1,0:T(8,128)} %get-tuple-element.158), channel_id=1, source_target_pairs={{0,8},{8,0},{16,24},{24,16},{1,9},{9,1},{17,25},{25,17},{2,10},{10... | collective-permute-start | bytes 3145736 | tf_op jit(solution)/shard_map/ppermute | solution.py:468
  397.1 97.9 %collective-permute-start.25 = (f32[8,256,128]{2,1,0:T(8,128)}, f32[8,256,128]{2,1,0:T(8,128)}, u32[]{:S(2)}, u32[]{:S(2)}) collective-permute-start(f32[8,256,128]{2,1,0:T(8,128)} %get-tuple-element.159), channel_id=1, source_target_pairs={{0,16},{8,24},{16,0},{24,8},{1,17},{9,25},{17,1},{25,9},{2,18},{10... | collective-permute-start | bytes 3145736 | tf_op jit(solution)/shard_map/ppermute | solution.py:468
  398.9 96.1 %collective-permute-start.26 = (f32[8,256,128]{2,1,0:T(8,128)}, f32[8,256,128]{2,1,0:T(8,128)}, u32[]{:S(2)}, u32[]{:S(2)}) collective-permute-start(f32[8,256,128]{2,1,0:T(8,128)} %get-tuple-element.160), channel_id=1, source_target_pairs={{0,24},{8,16},{16,8},{24,0},{1,25},{9,17},{17,9},{25,1},{2,26},{10... | collective-permute-start | bytes 3145736 | tf_op jit(solution)/shard_map/ppermute | solution.py:468
  398.9 69.4 %collective-permute-start.28 = (f32[8,256,128]{2,1,0:T(8,128)}, f32[8,256,128]{2,1,0:T(8,128)}, u32[]{:S(2)}, u32[]{:S(2)}) collective-permute-start(f32[8,256,128]{2,1,0:T(8,128)} %get-tuple-element.163), channel_id=1, source_target_pairs={{0,16},{8,24},{16,0},{24,8},{1,17},{9,25},{17,1},{25,9},{2,18},{10... | collective-permute-start | bytes 3145736 | tf_op jit(solution)/shard_map/ppermute | solution.py:468
  400.3 89.1 %collective-permute-start.29 = (f32[8,256,128]{2,1,0:T(8,128)}, f32[8,256,128]{2,1,0:T(8,128)}, u32[]{:S(2)}, u32[]{:S(2)}) collective-permute-start(f32[8,256,128]{2,1,0:T(8,128)} %get-tuple-element.164), channel_id=1, source_target_pairs={{0,24},{8,16},{16,8},{24,0},{1,25},{9,17},{17,9},{25,1},{2,26},{10... | collective-permute-start | bytes 3145736 | tf_op jit(solution)/shard_map/ppermute | solution.py:468
  400.7 99.8 %all-to-all-start.2 = ((f32[64,8,16,128]{3,2,1,0:T(8,128)}), f32[64,8,16,128]{3,2,1,0:T(8,128)}, u32[]{:S(2)}, u32[]{:S(2)}) async-start(f32[64,8,16,128]{3,2,1,0:T(8,128)} %shard_map.89), calls=%async_computation.2 | async-start | bytes 8388608 | tf_op jit(solution)/shard_map/all_to_all | solution.py:583
  468.3 70.2 %collective-permute-start.30 = (f32[8,256,128]{2,1,0:T(8,128)}, f32[8,256,128]{2,1,0:T(8,128)}, u32[]{:S(2)}, u32[]{:S(2)}) collective-permute-start(f32[8,256,128]{2,1,0:T(8,128)} %get-tuple-element.170), channel_id=1, source_target_pairs={{0,8},{8,0},{16,24},{24,16},{1,9},{9,1},{17,25},{25,17},{2,10},{10... | collective-permute-start | bytes 3145736 | tf_op jit(solution)/shard_map/ppermute | solution.py:468
  489.4 49.2 %collective-permute-start.31 = (f32[8,256,128]{2,1,0:T(8,128)}, f32[8,256,128]{2,1,0:T(8,128)}, u32[]{:S(2)}, u32[]{:S(2)}) collective-permute-start(f32[8,256,128]{2,1,0:T(8,128)} %get-tuple-element.171), channel_id=1, source_target_pairs={{0,16},{8,24},{16,0},{24,8},{1,17},{9,25},{17,1},{25,9},{2,18},{10... | collective-permute-start | bytes 3145736 | tf_op jit(solution)/shard_map/ppermute | solution.py:468
  494.4 44.2 %collective-permute-start.32 = (f32[8,256,128]{2,1,0:T(8,128)}, f32[8,256,128]{2,1,0:T(8,128)}, u32[]{:S(2)}, u32[]{:S(2)}) collective-permute-start(f32[8,256,128]{2,1,0:T(8,128)} %get-tuple-element.172), channel_id=1, source_target_pairs={{0,24},{8,16},{16,8},{24,0},{1,25},{9,17},{17,9},{25,1},{2,26},{10... | collective-permute-start | bytes 3145736 | tf_op jit(solution)/shard_map/ppermute | solution.py:468
  520.7 1.4 collective-permute-start.33
  522.8 3.6 collective-permute-start.34
  526.3 3.6 collective-permute-start.35
  529.9 4.5 collective-permute-start.36
  534.4 3.6 collective-permute-start.37
  538.6 5.6 collective-permute-start.38
  538.7 26.2 %collective-permute-start.39 = (f32[8,256,128]{2,1,0:T(8,128)}, f32[8,256,128]{2,1,0:T(8,128)S(1)}, u32[]{:S(2)}, u32[]{:S(2)}) collective-permute-start(f32[8,256,128]{2,1,0:T(8,128)} %get-tuple-element.179), channel_id=1, source_target_pairs={{0,16},{8,24},{16,0},{24,8},{1,17},{9,25},{17,1},{25,9},{2,18},{10... | collective-permute-start | bytes 3145736 | tf_op jit(solution)/shard_map/ppermute | solution.py:468
  540.1 46.4 %collective-permute-start.40 = (f32[8,256,128]{2,1,0:T(8,128)}, f32[8,256,128]{2,1,0:T(8,128)S(1)}, u32[]{:S(2)}, u32[]{:S(2)}) collective-permute-start(f32[8,256,128]{2,1,0:T(8,128)} %get-tuple-element.180), channel_id=1, source_target_pairs={{0,24},{8,16},{16,8},{24,0},{1,25},{9,17},{17,9},{25,1},{2,26},{10... | collective-permute-start | bytes 3145736 | tf_op jit(solution)/shard_map/ppermute | solution.py:468
  544.2 42.3 %copy-start.2 = (f32[8,256,128]{2,1,0:T(8,128)}, f32[8,256,128]{2,1,0:T(8,128)S(1)}, u32[]{:S(2)}) copy-start(f32[8,256,128]{2,1,0:T(8,128)S(1)} %collective-permute-done.38.refs_1_) | copy-start | bytes 3145732
  (11 other events, 141.2 us)
